TPU v7x, 128 devices: a whole 4x4x4 slice. The times are simulated.
128 devices in a mesh: replica: 8 (over x, core), tensor: 16 (over z, y).
Axes of the slice: x: 4, y: 4, z: 4, core: 2. Of those that a mesh axis runs over, the one named last changes fastest.
Arguments:
- gated_hidden: bfloat16 [2, 1024, 14336], P(None, 'replica', 'tensor'), may hold values from -6 to 6
- coded_weight: bfloat16 [14336, 8192], P('tensor'), may hold values from -6 to 6, as said below
- block_exponent: int32 [448, 8192], P('tensor'), may hold values from 117 to 120
- stream_input: bfloat16 [2, 1024, 8192], P(None, 'replica', 'tensor'), may hold values from -6 to 6
- lower_layer: bfloat16 [1024, 8192], P('replica', 'tensor'), may hold values from -6 to 6
- middle_layer: bfloat16 [1024, 8192], P('replica', 'tensor'), may hold values from -6 to 6
- prior_lower: bfloat16 [1024, 8192], P('replica', 'tensor'), may hold values from -6 to 6
- prior_middle: bfloat16 [1024, 8192], P('replica', 'tensor'), may hold values from -6 to 6
- prior_upper: bfloat16 [1024, 8192], P('replica', 'tensor'), may hold values from -6 to 6
- accepted: int32 [1024], P('replica'), may hold values from 0 to 2, as said below
- draft_input_weight: float32 [3, 8192, 8192], P(None, 'tensor', 'replica'), may hold values from -0.44194174 to 0.44194174
- draft_gain: float32 [8192], P('replica'), may hold values from 0.5 to 2
Outputs:
- upper_layer: bfloat16 [2, 1024, 8192], P(None, 'replica', 'tensor')
- new_weight: bfloat16 [3, 8192, 8192], P(None, 'tensor', 'replica')
Inputs may be any that keep to these rules, and one draw needn't show every extreme that they name: `coded_weight`: the values of the FP4 E2M1 grid: 0, 0.5, 1, 1.5, 2, 3, 4, 6 and their negatives. The accepted lengths of the 128 rows of one replica (aligned blocks of 128 rows) sum to at most 192, and to exactly that in at least one block.
All inputs are finite; a program needn't handle non-finite values.
Results may differ from a plain program's by a relative error of at most 0.005.
Values may be sent and summed in bfloat16 or wider, within the bound.
No kernel may reach another device: no remote copies, remote signals or barrier semaphores. Data moves between devices by JAX's collectives and lax.ppermute only.
A program may use at most 128 MiB of HBM per device.

v0:
```python
import functools

import jax
import jax.numpy as jnp
from jax import lax
from jax.experimental import pallas as pl
from jax.experimental.pallas import tpu as pltpu
from jax.sharding import PartitionSpec as P

step_rate = 8.0
epsilon = 1e-06
side = 4
cores = 2
block_units = 32
f32 = jnp.float32
bf16 = jnp.bfloat16
mesh_axes = ("replica", "tensor")
vmem = 56 * 1024 * 1024


def coordinates(device):
    replica, tensor = divmod(device, side * side)
    x, c = divmod(replica, cores)
    z, y = divmod(tensor, side)
    return x, c, z, y


def device_at(x, c, z, y):
    return ((x % side) * cores + c % cores) * side * side + (z % side) * side + y % side


def moved(target):
    return [(d, target(*coordinates(d))) for d in range(side * cores * side * side)]


def along_first(shift):
    return moved(
        lambda x, c, z, y: device_at(x, c, z + shift * (c == 0), y + shift * (c == 1))
    )


def along_second(shift):
    return moved(
        lambda x, c, z, y: device_at(x, c, z + shift * (c == 1), y + shift * (c == 0))
    )


def along_x(shift):
    return moved(lambda x, c, z, y: device_at(x + shift, c, z, y))


def other_core():
    return moved(lambda x, c, z, y: device_at(x, 1 - c, z, y))


def send(array, pairs):
    return lax.ppermute(array, mesh_axes, pairs)


def plus(*terms):
    return functools.reduce(jnp.add, [term.astype(f32) for term in terms])


def other_core_rows():
    return moved(lambda x, c, z, y: device_at(x, 1 - c, y, z))


def row_block(c, tensor):
    z, y = tensor // side, tensor % side
    return z * side + y if c == 0 else y * side + z


def turned(pieces, places):
    for bit in (1, 2):
        moves = places // bit % 2 == 1
        pieces = [
            jnp.where(moves, pieces[(j - bit) % side], pieces[j]) for j in range(side)
        ]
    return pieces


def place():
    replica, tensor = lax.axis_index("replica"), lax.axis_index("tensor")
    x, c = replica // cores, replica % cores
    z, y = tensor // side, tensor % side
    return x, c, jnp.where(c == 0, z, y), jnp.where(c == 0, y, z)


def down_kernel(blocks_ref, tokens_ref, *refs):
    coded_refs, exponent_refs, pieces = refs[:2], refs[2:4], refs[4:]
    i = pl.program_id(0)
    totals = []
    for coded_ref, exponent_ref in zip(coded_refs, exponent_refs):
        units, columns = coded_ref.shape
        factor = jnp.exp2(exponent_ref[...].astype(f32) - 127.0).astype(bf16)
        weight = coded_ref[...].reshape(units // block_units, block_units, columns)
        weight = (weight * factor[:, None, :]).reshape(units, columns)
        totals.append(jnp.dot(tokens_ref[...], weight, preferred_element_type=f32))
    for k, piece in enumerate(pieces):

        @pl.when(i == k)
        def _():
            for half, total in enumerate(totals):
                piece[half] = total.astype(piece.dtype)


def down_pieces(blocks, tokens, coded_weight, block_exponent, kind):
    rows, units = tokens.shape
    width = coded_weight.shape[1] // (side * side)
    count = blocks.shape[0]

    def column_block(height, half):
        return pl.BlockSpec((height, width), lambda i, blocks: (0, blocks[2 * i + half]))

    return pl.pallas_call(
        down_kernel,
        grid_spec=pltpu.PrefetchScalarGridSpec(
            num_scalar_prefetch=1,
            grid=(count // 2,),
            in_specs=[
                pl.BlockSpec((rows, units), lambda i, blocks: (0, 0)),
                column_block(units, 0),
                column_block(units, 1),
                column_block(units // block_units, 0),
                column_block(units // block_units, 1),
            ],
            out_specs=[
                pl.BlockSpec((2, rows, width), lambda i, blocks: (0, 0, 0))
                for _ in range(count // 2)
            ],
        ),
        out_shape=[jax.ShapeDtypeStruct((2, rows, width), kind)] * (count // 2),
        compiler_params=pltpu.CompilerParams(vmem_limit_bytes=vmem),
        cost_estimate=pl.CostEstimate(
            flops=2 * rows * units * width * count,
            bytes_accessed=3 * units * width * count,
            transcendentals=0,
        ),
        name="down_projection",
    )(blocks, tokens, coded_weight, coded_weight, block_exponent, block_exponent)


def round_kernel(after_ref, wide_ref, out_ref):
    out_ref[...] = wide_ref[...].astype(bf16)


def rounded_rows(wide, start, count, after):
    step, columns = min(256, count), wide.shape[1]
    return pl.pallas_call(
        round_kernel,
        grid=(count // step,),
        in_specs=[
            pl.BlockSpec(memory_space=pl.ANY),
            pl.BlockSpec((step, columns), lambda i: (start // step + i, 0)),
        ],
        out_specs=pl.BlockSpec((step, columns), lambda i: (i, 0)),
        out_shape=jax.ShapeDtypeStruct((count, columns), bf16),
        compiler_params=pltpu.CompilerParams(vmem_limit_bytes=vmem),
        cost_estimate=pl.CostEstimate(
            flops=count * columns, bytes_accessed=6 * count * columns, transcendentals=0
        ),
        name="round_weight",
    )(after, wide)


def reduce_blocks(near, direct, own, q):
    low_right = send(near[0], along_first(1))
    high_left = send(near[1], along_first(-1))
    high_right = send(direct[1], along_first(1))
    low_left = send(direct[2], along_first(-1))
    low_right = send(direct[0] + low_right, along_first(1))
    high_left = send(direct[3] + high_left, along_first(-1))
    summed = jnp.concatenate(
        [plus(own[0], low_right, low_left), plus(own[1], high_left, high_right)]
    )
    halved = summed.astype(bf16)

    def at(array, shift):
        return lax.dynamic_index_in_dim(array, (q + shift) % side, 0, keepdims=False)

    parts = [send(at(halved, shift), along_second(shift)) for shift in (1, 3, 2)]
    return plus(at(summed, 0), *parts), summed[0, :8, :128]


def body(
    gated_hidden,
    coded_weight,
    block_exponent,
    stream_input,
    lower_layer,
    middle_layer,
    prior_lower,
    prior_middle,
    prior_upper,
    accepted,
    draft_input_weight,
    draft_gain,
):
    steps, rows, unit_count = gated_hidden.shape
    feature_slice = stream_input.shape[2]
    out_slice = draft_input_weight.shape[2]
    replicas = lax.axis_size("replica")
    tensors = lax.axis_size("tensor")
    width = feature_slice * tensors
    slots_all = steps * rows * replicas
    slots = rows * 3 // 4
    x, c, p, q = place()

    with jax.named_scope("down"):
        tokens = gated_hidden.reshape(steps * rows, unit_count)
        second = jnp.arange(side, dtype=jnp.int32)

        def columns(shift):
            first = (p + shift) % side
            return jnp.where(c == 0, first * side + second, second * side + first)

        near = down_pieces(columns(2), tokens, coded_weight, block_exponent, bf16)
        near, accepted = lax.optimization_barrier((near, accepted))

    with jax.named_scope("select"):
        row = jnp.arange(rows, dtype=jnp.int32)
        before = row[:, None] <= row[None, :]
        first_live = (accepted >= 1).astype(jnp.int32)
        second_live = (accepted >= 2).astype(jnp.int32)
        first_slot = jnp.sum(jnp.where(before, first_live[:, None], 0), axis=0) - 1
        second_slot = 2 * slots - jnp.sum(jnp.where(before, second_live[:, None], 0), axis=0)
        first_slot = jnp.where(first_live == 1, first_slot, -1)
        second_slot = jnp.where(second_live == 1, second_slot, -1)
        slot = jnp.arange(2 * slots, dtype=jnp.int32)[:, None]
        select = (slot == jnp.concatenate([first_slot, second_slot])[None, :]).astype(bf16)

        def pick(chosen, first, second):
            return jnp.dot(
                chosen, jnp.concatenate([first, second]), preferred_element_type=f32
            ).astype(bf16)

        pair = pick(
            select,
            jnp.concatenate([prior_lower, prior_middle], axis=1),
            jnp.concatenate([lower_layer, middle_layer], axis=1),
        )
        front = jnp.dot(
            select[:slots, :rows], prior_upper, preferred_element_type=f32
        ).astype(bf16)
        folded = jnp.concatenate([front[: slots // 2], front[slots // 2 :]], axis=1)
        payload = jnp.concatenate([pair, folded])
    gathered = lax.all_gather(payload, "replica", axis=0, tiled=True)

    with jax.named_scope("down"):
        others, payload = lax.optimization_barrier(
            (jnp.concatenate([columns(1), columns(3)]), payload)
        )
        direct = down_pieces(others, tokens, coded_weight, block_exponent, bf16)
        direct, mine = lax.optimization_barrier((direct, columns(0)))
        own = down_pieces(mine, tokens, coded_weight, block_exponent, f32)

    with jax.named_scope("reduce_down"):
        mixed, first_sum = reduce_blocks(near, direct, own, q)
    flat_weight = draft_input_weight.reshape(3 * feature_slice, out_slice)
    pair_weight = rounded_rows(flat_weight, 0, 2 * feature_slice, first_sum)
    third_weight = rounded_rows(flat_weight, 2 * feature_slice, feature_slice, first_sum)
    upper_layer = (
        stream_input.astype(f32) + mixed.reshape(steps, rows, feature_slice)
    ).astype(bf16)

    with jax.named_scope("back"):
        back = pick(select[slots:], prior_upper, upper_layer[0])
        chips = [back] + [send(back, along_x(-shift)) for shift in (1, 2, 3)]
        chips = jnp.stack(turned(chips, x))
        others = send(chips, other_core())

    with jax.named_scope("targets"):
        chosen = pick(select, upper_layer[0], upper_layer[1])
        parity = lax.axis_index("tensor") % 2
        even, odd = chosen[:slots], chosen[slots:]
        posted = [jnp.where((parity + turn) % 2 == 0, even, odd) for turn in range(2)]
        got = []
        for turn in range(2):
            routes = []
            for d in range(replicas * tensors):
                r, t = divmod(d, tensors)
                owner = t // 2
                taken = row_block(owner % cores, 2 * r + (t + turn) % 2)
                routes.append((d, owner * tensors + taken))
            got.append(send(posted[turn], routes))

    with jax.named_scope("forward"):
        by_replica = gathered.reshape(replicas, -1, 2 * feature_slice)
        stride = by_replica.shape[1]
        pairs, fronts = by_replica[:, : 2 * slots], by_replica[:, 2 * slots :]
        fronts = jnp.concatenate(
            [fronts[:, :, :feature_slice], fronts[:, :, feature_slice:]], axis=1
        )

        def replica_of(shift, half):
            return 2 * ((p + shift) % side) + half

        def pair_product(weight, shift, half):
            rows_of = lax.dynamic_slice_in_dim(
                gathered, replica_of(shift, half) * stride, 2 * slots, axis=0
            )
            return jnp.dot(rows_of, weight, preferred_element_type=f32)

        def third_product(weight, shift, half):
            rows_of = lax.dynamic_slice_in_dim(
                thirds, replica_of(shift, half) * 2 * slots, 2 * slots, axis=0
            )
            return jnp.dot(rows_of, weight, preferred_element_type=f32)

        def piece(total, kind):
            return total.astype(kind).reshape(2, slots, out_slice)

        far_pairs = [pair_product(pair_weight, 2, half) for half in range(2)]
        others, fronts, far_pairs, _ = lax.optimization_barrier(
            (others, fronts, far_pairs, posted)
        )
        backs = jnp.stack(
            [jnp.where(c == 0, chips, others), jnp.where(c == 0, others, chips)], axis=1
        ).reshape(replicas, slots, feature_slice)
        thirds = jnp.concatenate([fronts, backs], axis=1).reshape(-1, feature_slice)
        near = [
            piece(far_pairs[half] + third_product(third_weight, 2, half), bf16)
            for half in range(2)
        ]
        _, got, pair_weight, third_weight = lax.optimization_barrier(
            (near, got, pair_weight, third_weight)
        )
        direct = [
            piece(
                pair_product(pair_weight, shift, half) + third_product(third_weight, shift, half),
                bf16,
            )
            for shift in (1, 3)
            for half in range(2)
        ]
        _, pair_weight, third_weight = lax.optimization_barrier(
            (direct, pair_weight, third_weight)
        )
        own = [
            piece(
                pair_product(pair_weight, 0, half) + third_product(third_weight, 0, half), f32
            )
            for half in range(2)
        ]

    with jax.named_scope("reduce_draft"):
        drafted, _ = reduce_blocks(near, direct, own, q)

    with jax.named_scope("norm"):
        front_rows = q % 2 == 0
        targets = jnp.concatenate(
            [jnp.where(front_rows, got[0], got[1]), jnp.where(front_rows, got[1], got[0])],
            axis=1,
        ).astype(f32)
        gain = draft_gain[None, :]
        scaled = gain * drafted
        sums = jnp.stack(
            [
                jnp.sum(drafted * drafted, axis=1),
                jnp.sum(scaled * scaled, axis=1),
                jnp.sum(scaled * targets, axis=1),
            ]
        )
        sums = sums + send(sums, other_core_rows())
        sums = sums + send(sums, along_x(1)) + send(sums, along_x(2)) + send(sums, along_x(3))
        scale = lax.rsqrt(sums[0] / width + epsilon)
        inner = (scale * sums[1] - sums[2]) / slots_all
        error = gain * (scaled * scale[:, None] - targets) / slots_all
        slope = (scale[:, None] * error - drafted * (scale**3 * inner / width)[:, None]).astype(
            bf16
        )

    with jax.named_scope("gather_slope"):
        ring = [slope] + [send(slope, along_second(-shift)) for shift in (1, 2, 3)]
        ring = turned(ring, q)
        upper_half, lower_half = jnp.concatenate(ring[:2]), jnp.concatenate(ring[2:])
        previous_upper = send(upper_half, along_first(1))
        following_lower = send(lower_half, along_first(-1))
        previous_lower = send(lower_half, along_first(1))
        following_upper = send(upper_half, along_first(-1))
        low = send(previous_upper, along_first(1))
        high = send(following_lower, along_first(-1))

    with jax.named_scope("step"):
        features = jnp.concatenate([pairs.reshape(-1, 2 * feature_slice), thirds], axis=1)

        def product(places, slopes):
            inputs = [
                lax.dynamic_slice_in_dim(
                    features, (2 * ((p + shift) % side) + half) * 2 * slots, 2 * slots, axis=0
                )
                for shift, half in places
            ]
            return lax.dot_general(
                jnp.concatenate(inputs),
                jnp.concatenate(slopes),
                (((0,), (0,)), ((), ())),
                preferred_element_type=f32,
            )

        upper_half, lower_half, previous_upper, following_lower = lax.optimization_barrier(
            (upper_half, lower_half, previous_upper, following_lower)
        )
        total = product([(0, 0), (0, 1)], [upper_half, lower_half])
        total = lax.optimization_barrier(
            total + product([(3, 0), (1, 1)], [previous_upper, following_lower])
        )
        total = lax.optimization_barrier(
            total + product([(3, 1), (1, 0)], [previous_lower, following_upper])
        )
        total = total + product([(2, 0), (2, 1)], [low, high])
        new_weight = (flat_weight - step_rate * total).astype(bf16)
        new_weight = new_weight.reshape(draft_input_weight.shape)
    return (upper_layer, new_weight)


def solution(mesh):
    return jax.shard_map(
        body,
        mesh=mesh,
        in_specs=(
            P(None, "replica", "tensor"),
            P("tensor", None),
            P("tensor", None),
            P(None, "replica", "tensor"),
            P("replica", "tensor"),
            P("replica", "tensor"),
            P("replica", "tensor"),
            P("replica", "tensor"),
            P("replica", "tensor"),
            P("replica"),
            P(None, "tensor", "replica"),
            P("replica"),
        ),
        out_specs=(P(None, "replica", "tensor"), P(None, "tensor", "replica")),
        check_vma=False,
    )
```

profile of v0, /device:TPU:0, one launch (start us, length us, event | category | flops | bytes accessed | tf_op | source)
XLA Modules:
  0.0 179.8 jit_solution(15729248657529995257)
XLA Ops:
  7.8 5.4 %down_projection.3 = (bf16[2,256,512]{2,1,0:T(8,128)(2,1)}, bf16[2,256,512]{2,1,0:T(8,128)(2,1)}) custom-call(s32[4]{0:T(128)} %broadcast_select_fusion.17.blocks_ref, bf16[256,896]{1,0:T(8,128)(2,1)} %bitcast.119, bf16[896,8192]{1,0:T(8,128)(2,1)} %refs_1_.5, bf16[896,8192]{1,0:T(8,128)(2,1)} %refs_1_.5, s32[28,8192]{1,0:T(8,128)} %refs_3_.5, ...), custom_call_target="tpu_custom_call" | custom-call | flops 939524096 | bytes 5505024 | tf_op jit(solution)/shard_map/down/down_projection/pallas_call | solution.py:115
  15.2 2.1 %collective-permute-start = (bf16[2,256,512]{2,1,0:T(8,128)(2,1)S(1)}, bf16[2,256,512]{2,1,0:T(8,128)(2,1)S(1)}, u32[]{:S(2)}, u32[]{:S(2)}) collective-permute-start(bf16[2,256,512]{2,1,0:T(8,128)(2,1)S(1)} %copy-done.13), channel_id=1, source_target_pairs={{0,4},{1,5},{2,6},{3,7},{4,8},{5,9},{6,10},{7,11},{8,12},{9,13},{1... | collective-permute-start | bytes 1572872 | tf_op jit(solution)/shard_map/reduce_down/ppermute | solution.py:57
  17.2 2.2 %collective-permute-start.3 = (bf16[2,256,512]{2,1,0:T(8,128)(2,1)}, bf16[2,256,512]{2,1,0:T(8,128)(2,1)S(1)}, u32[]{:S(2)}, u32[]{:S(2)}) collective-permute-start(bf16[2,256,512]{2,1,0:T(8,128)(2,1)} %get-tuple-element.48), channel_id=1, source_target_pairs={{0,12},{1,13},{2,14},{3,15},{4,0},{5,1},{6,2},{7,3},{8,4},{9,5},{1... | collective-permute-start | bytes 1572872 | tf_op jit(solution)/shard_map/reduce_down/ppermute | solution.py:57
  20.6 8.0 %down_projection.4 = (bf16[2,256,512]{2,1,0:T(8,128)(2,1)}, bf16[2,256,512]{2,1,0:T(8,128)(2,1)}, bf16[2,256,512]{2,1,0:T(8,128)(2,1)}, bf16[2,256,512]{2,1,0:T(8,128)(2,1)}) custom-call(s32[8]{0:T(128)} %pad_add_fusion.1.blocks_ref, bf16[256,896]{1,0:T(8,128)(2,1)} %bitcast.120, bf16[896,8192]{1,0:T(8,128)(2,1)} %refs_1_.5, bf16[896,8192]{1,0:T(8,128)(2,1)} %refs_1_.5, ...), custom_call_target="tpu_custom_call" | custom-call | flops 1879048192 | bytes 11010048 | tf_op jit(solution)/shard_map/down/down_projection/pallas_call | solution.py:115
  33.2 3.2 %collective-permute-start.4 = (bf16[2,256,512]{2,1,0:T(8,128)(2,1)S(1)}, bf16[2,256,512]{2,1,0:T(8,128)(2,1)}, u32[]{:S(2)}, u32[]{:S(2)}) collective-permute-start(bf16[2,256,512]{2,1,0:T(8,128)(2,1)S(1)} %add.418), channel_id=1, source_target_pairs={{0,12},{1,13},{2,14},{3,15},{4,0},{5,1},{6,2},{7,3},{8,4},{9,5},{1... | collective-permute-start | bytes 1572872 | tf_op jit(solution)/shard_map/reduce_down/ppermute | solution.py:57
  36.5 5.7 %down_projection.5 = (f32[2,256,512]{2,1,0:T(8,128)}, f32[2,256,512]{2,1,0:T(8,128)}) custom-call(s32[4]{0:T(128)} %get-tuple-element.41.blocks_ref, bf16[256,896]{1,0:T(8,128)(2,1)} %bitcast.121, bf16[896,8192]{1,0:T(8,128)(2,1)} %refs_1_.5, bf16[896,8192]{1,0:T(8,128)(2,1)} %refs_1_.5, s32[28,8192]{1,0:T(8,128)} %refs_3_.5, s32[28,8192]{1,0:T(8,128)} %refs_3_.5), custom_call_target="tpu_custom_call" | custom-call | flops 939524096 | bytes 5505024 | tf_op jit(solution)/shard_map/down/down_projection/pallas_call | solution.py:115
  43.8 4.0 %collective-permute-done.5 = bf16[2,256,512]{2,1,0:T(8,128)(2,1)S(1)} collective-permute-done((bf16[2,256,512]{2,1,0:T(8,128)(2,1)}, bf16[2,256,512]{2,1,0:T(8,128)(2,1)S(1)}, u32[]{:S(2)}, u32[]{:S(2)}) %collective-permute-start.5) | collective-permute-done | bytes 524320 | tf_op jit(solution)/shard_map/reduce_down/ppermute | solution.py:57
  51.6 2.9 %collective-permute-start.8 = (bf16[256,512]{1,0:T(8,128)(2,1)S(1)}, bf16[256,512]{1,0:T(8,128)(2,1)S(1)}, u32[]{:S(2)}, u32[]{:S(2)}) collective-permute-start(bf16[256,512]{1,0:T(8,128)(2,1)S(1)} %get-tuple-element.81), channel_id=1, source_target_pairs={{0,2},{1,3},{2,0},{3,1},{4,6},{5,7},{6,4},{7,5},{8,10},{9,11},{10,... | collective-permute-start | bytes 786440 | tf_op jit(solution)/shard_map/reduce_down/ppermute | solution.py:57
  56.4 2.4 %round_weight.3 = bf16[512,1024]{1,0:T(8,128)(2,1)} custom-call(f32[8,128]{1,0:T(8,128)} %slice_bitcast_fusion.2.after_ref, f32[1536,1024]{1,0:T(8,128)} %bitcast.100), custom_call_target="tpu_custom_call" | custom-call | flops 524288 | bytes 3145728 | tf_op jit(solution)/shard_map/round_weight/pallas_call | solution.py:149
  58.9 4.2 %round_weight.2 = bf16[1024,1024]{1,0:T(8,128)(2,1)} custom-call(f32[8,128]{1,0:T(8,128)} %slice_bitcast_fusion.2.after_ref, f32[1536,1024]{1,0:T(8,128)} %bitcast.101), custom_call_target="tpu_custom_call" | custom-call | flops 1048576 | bytes 6291456 | tf_op jit(solution)/shard_map/round_weight/pallas_call | solution.py:149
  65.9 2.7 %collective-permute-start.10 = (bf16[96,512]{1,0:T(8,128)(2,1)S(1)}, bf16[96,512]{1,0:T(8,128)(2,1)S(1)}, u32[]{:S(2)}, u32[]{:S(2)}) collective-permute-start(bf16[96,512]{1,0:T(8,128)(2,1)S(1)} %convolution_convert_fusion.2), channel_id=1, source_target_pairs={{0,64},{1,65},{2,66},{3,67},{4,68},{5,69},{6,70},{7,71},{8,72},{9,... | collective-permute-start | bytes 294920 | tf_op jit(solution)/shard_map/back/ppermute | solution.py:57
  71.7 2.1 %collective-permute-start.13 = (bf16[96,512]{1,0:T(8,128)(2,1)}, bf16[96,512]{1,0:T(8,128)(2,1)}, u32[]{:S(2)}, u32[]{:S(2)}) collective-permute-start(bf16[96,512]{1,0:T(8,128)(2,1)} %get-tuple-element.101), channel_id=1, source_target_pairs={{0,0},{1,1},{2,16},{3,20},{4,32},{5,33},{6,48},{7,52},{8,64},{9,65... | collective-permute-start | bytes 294920 | tf_op jit(solution)/shard_map/targets/ppermute | solution.py:57
  80.8 3.9 %collective-permute-start.18 = (bf16[2,96,1024]{2,1,0:T(8,128)(2,1)S(1)}, bf16[2,96,1024]{2,1,0:T(8,128)(2,1)S(1)}, u32[]{:S(2)}, u32[]{:S(2)}) collective-permute-start(bf16[2,96,1024]{2,1,0:T(8,128)(2,1)S(1)} %bitcast.131), channel_id=1, source_target_pairs={{0,12},{1,13},{2,14},{3,15},{4,0},{5,1},{6,2},{7,3},{8,4},{9,5},{1... | collective-permute-start | bytes 1179656 | tf_op jit(solution)/shard_map/reduce_draft/ppermute | solution.py:57
  86.7 3.3 %collective-permute-start.17 = (bf16[2,96,1024]{2,1,0:T(8,128)(2,1)S(1)}, bf16[2,96,1024]{2,1,0:T(8,128)(2,1)S(1)}, u32[]{:S(2)}, u32[]{:S(2)}) collective-permute-start(bf16[2,96,1024]{2,1,0:T(8,128)(2,1)S(1)} %bitcast.129), channel_id=1, source_target_pairs={{0,12},{1,13},{2,14},{3,15},{4,0},{5,1},{6,2},{7,3},{8,4},{9,5},{1... | collective-permute-start | bytes 1179656 | tf_op jit(solution)/shard_map/reduce_draft/ppermute | solution.py:57
  93.9 3.3 %collective-permute-start.19 = (bf16[2,96,1024]{2,1,0:T(8,128)(2,1)S(1)}, bf16[2,96,1024]{2,1,0:T(8,128)(2,1)S(1)}, u32[]{:S(2)}, u32[]{:S(2)}) collective-permute-start(bf16[2,96,1024]{2,1,0:T(8,128)(2,1)S(1)} %add.475), channel_id=1, source_target_pairs={{0,12},{1,13},{2,14},{3,15},{4,0},{5,1},{6,2},{7,3},{8,4},{9,5},{1... | collective-permute-start | bytes 1179656 | tf_op jit(solution)/shard_map/reduce_draft/ppermute | solution.py:57
  100.0 2.5 %collective-permute-done.19 = bf16[2,96,1024]{2,1,0:T(8,128)(2,1)S(1)} collective-permute-done((bf16[2,96,1024]{2,1,0:T(8,128)(2,1)S(1)}, bf16[2,96,1024]{2,1,0:T(8,128)(2,1)S(1)}, u32[]{:S(2)}, u32[]{:S(2)}) %collective-permute-start.19) | collective-permute-done | bytes 393248 | tf_op jit(solution)/shard_map/reduce_draft/ppermute | solution.py:57
  102.7 4.1 %collective-permute-done.16 = bf16[2,96,1024]{2,1,0:T(8,128)(2,1)S(1)} collective-permute-done((bf16[2,96,1024]{2,1,0:T(8,128)(2,1)S(1)}, bf16[2,96,1024]{2,1,0:T(8,128)(2,1)S(1)}, u32[]{:S(2)}, u32[]{:S(2)}) %collective-permute-start.16) | collective-permute-done | bytes 393248 | tf_op jit(solution)/shard_map/reduce_draft/ppermute | solution.py:57
  109.1 4.5 %collective-permute-start.23 = (bf16[96,1024]{1,0:T(8,128)(2,1)S(1)}, bf16[96,1024]{1,0:T(8,128)(2,1)S(1)}, u32[]{:S(2)}, u32[]{:S(2)}) collective-permute-start(bf16[96,1024]{1,0:T(8,128)(2,1)S(1)} %get-tuple-element.88), channel_id=1, source_target_pairs={{0,2},{1,3},{2,0},{3,1},{4,6},{5,7},{6,4},{7,5},{8,10},{9,11},{10,... | collective-permute-start | bytes 589832 | tf_op jit(solution)/shard_map/reduce_draft/ppermute | solution.py:57
  113.6 2.5 %collective-permute-start.22 = (bf16[96,1024]{1,0:T(8,128)(2,1)S(1)}, bf16[96,1024]{1,0:T(8,128)(2,1)S(1)}, u32[]{:S(2)}, u32[]{:S(2)}) collective-permute-start(bf16[96,1024]{1,0:T(8,128)(2,1)S(1)} %get-tuple-element.89), channel_id=1, source_target_pairs={{0,3},{1,0},{2,1},{3,2},{4,7},{5,4},{6,5},{7,6},{8,11},{9,8},{10,9... | collective-permute-start | bytes 589832 | tf_op jit(solution)/shard_map/reduce_draft/ppermute | solution.py:57
  117.1 2.2 %collective-permute-done.23 = bf16[96,1024]{1,0:T(8,128)(2,1)S(1)} collective-permute-done((bf16[96,1024]{1,0:T(8,128)(2,1)S(1)}, bf16[96,1024]{1,0:T(8,128)(2,1)S(1)}, u32[]{:S(2)}, u32[]{:S(2)}) %collective-permute-start.23) | collective-permute-done | bytes 196640 | tf_op jit(solution)/shard_map/reduce_draft/ppermute | solution.py:57
  123.1 3.0 %collective-permute-done.26 = f32[3,96]{1,0:T(4,128)S(1)} collective-permute-done((f32[3,96]{1,0:T(4,128)S(1)}, f32[3,96]{1,0:T(4,128)S(1)}, u32[]{:S(2)}, u32[]{:S(2)}) %collective-permute-start.26) | collective-permute-done | bytes 1184 | tf_op jit(solution)/shard_map/norm/ppermute | solution.py:57
  127.6 4.3 %collective-permute-start.30 = (bf16[96,1024]{1,0:T(8,128)(2,1)S(1)}, bf16[96,1024]{1,0:T(8,128)(2,1)S(1)}, u32[]{:S(2)}, u32[]{:S(2)}) collective-permute-start(bf16[96,1024]{1,0:T(8,128)(2,1)S(1)} %fusion.55), channel_id=1, source_target_pairs={{0,1},{1,2},{2,3},{3,0},{4,5},{5,6},{6,7},{7,4},{8,9},{9,10},{10,1... | collective-permute-start | bytes 589832 | tf_op jit(solution)/shard_map/gather_slope/ppermute | solution.py:57
  131.9 5.3 %collective-permute-start.29 = (bf16[96,1024]{1,0:T(8,128)(2,1)S(1)}, bf16[96,1024]{1,0:T(8,128)(2,1)S(1)}, u32[]{:S(2)}, u32[]{:S(2)}) collective-permute-start(bf16[96,1024]{1,0:T(8,128)(2,1)S(1)} %fusion.55), channel_id=1, source_target_pairs={{0,2},{1,3},{2,0},{3,1},{4,6},{5,7},{6,4},{7,5},{8,10},{9,11},{10,... | collective-permute-start | bytes 589832 | tf_op jit(solution)/shard_map/gather_slope/ppermute | solution.py:57
  137.3 2.2 %collective-permute-start.28 = (bf16[96,1024]{1,0:T(8,128)(2,1)S(1)}, bf16[96,1024]{1,0:T(8,128)(2,1)S(1)}, u32[]{:S(2)}, u32[]{:S(2)}) collective-permute-start(bf16[96,1024]{1,0:T(8,128)(2,1)S(1)} %fusion.55), channel_id=1, source_target_pairs={{0,3},{1,0},{2,1},{3,2},{4,7},{5,4},{6,5},{7,6},{8,11},{9,8},{10,9... | collective-permute-start | bytes 589832 | tf_op jit(solution)/shard_map/gather_slope/ppermute | solution.py:57
  139.5 2.3 %slice.67 = bf16[8,192,1024]{2,1,0:T(8,128)(2,1)S(1)} slice(bf16[8,240,1024]{2,1,0:T(8,128)(2,1)} %bitcast.118), slice={[0:8], [0:192], [0:1024]} | slice | bytes 6291456 | tf_op jit(solution)/shard_map/forward/slice | solution.py:290
  141.8 5.2 %collective-permute-done.29 = bf16[96,1024]{1,0:T(8,128)(2,1)S(1)} collective-permute-done((bf16[96,1024]{1,0:T(8,128)(2,1)S(1)}, bf16[96,1024]{1,0:T(8,128)(2,1)S(1)}, u32[]{:S(2)}, u32[]{:S(2)}) %collective-permute-start.29) | collective-permute-done | bytes 196640 | tf_op jit(solution)/shard_map/gather_slope/ppermute | solution.py:57
  147.2 3.3 %collective-permute-start.32 = (bf16[192,1024]{1,0:T(8,128)(2,1)S(1)}, bf16[192,1024]{1,0:T(8,128)(2,1)S(1)}, u32[]{:S(2)}, u32[]{:S(2)}) collective-permute-start(bf16[192,1024]{1,0:T(8,128)(2,1)S(1)} %pad_maximum_fusion.7), channel_id=1, source_target_pairs={{0,12},{1,13},{2,14},{3,15},{4,0},{5,1},{6,2},{7,3},{8,4},{9,5},{1... | collective-permute-start | bytes 1179656 | tf_op jit(solution)/shard_map/gather_slope/ppermute | solution.py:57
  151.0 2.0 %collective-permute-start.33 = (bf16[192,1024]{1,0:T(8,128)(2,1)S(1)}, bf16[192,1024]{1,0:T(8,128)(2,1)S(1)}, u32[]{:S(2)}, u32[]{:S(2)}) collective-permute-start(bf16[192,1024]{1,0:T(8,128)(2,1)S(1)} %pad_maximum_fusion.7), channel_id=1, source_target_pairs={{0,4},{1,5},{2,6},{3,7},{4,8},{5,9},{6,10},{7,11},{8,12},{9,13},{1... | collective-permute-start | bytes 1179656 | tf_op jit(solution)/shard_map/gather_slope/ppermute | solution.py:57
  153.0 3.2 %collective-permute-done.31 = bf16[192,1024]{1,0:T(8,128)(2,1)S(1)} collective-permute-done((bf16[192,1024]{1,0:T(8,128)(2,1)S(1)}, bf16[192,1024]{1,0:T(8,128)(2,1)S(1)}, u32[]{:S(2)}, u32[]{:S(2)}) %collective-permute-start.31) | collective-permute-done | bytes 393248 | tf_op jit(solution)/shard_map/gather_slope/ppermute | solution.py:57
  159.9 3.4 %collective-permute-start.36 = (bf16[192,1024]{1,0:T(8,128)(2,1)S(1)}, bf16[192,1024]{1,0:T(8,128)(2,1)S(1)}, u32[]{:S(2)}, u32[]{:S(2)}) collective-permute-start(bf16[192,1024]{1,0:T(8,128)(2,1)S(1)} %collective-permute-done.32), channel_id=1, source_target_pairs={{0,12},{1,13},{2,14},{3,15},{4,0},{5,1},{6,2},{7,3},{8,4},{9,5},{1... | collective-permute-start | bytes 1179656 | tf_op jit(solution)/shard_map/gather_slope/ppermute | solution.py:57
  165.3 3.7 %collective-permute-done.35 = bf16[192,1024]{1,0:T(8,128)(2,1)S(1)} collective-permute-done((bf16[192,1024]{1,0:T(8,128)(2,1)S(1)}, bf16[192,1024]{1,0:T(8,128)(2,1)S(1)}, u32[]{:S(2)}, u32[]{:S(2)}) %collective-permute-start.35) | collective-permute-done | bytes 393248 | tf_op jit(solution)/shard_map/gather_slope/ppermute | solution.py:57
  169.0 4.0 %subtract_convert_fusion = bf16[1536,1024]{1,0:T(8,128)(2,1)} fusion(f32[1536,1024]{1,0:T(8,128)S(1)} %bitcast.104, f32[1536,1024]{1,0:T(8,128)S(1)} %convolution_add_fusion, bf16[192,1536]{1,0:T(8,128)(2,1)S(1)} %get-tuple-element.76, bf16[192,1536]{1,0:T(8,128)(2,1)S(1)} %get-tuple-element.70, bf16[192,1024]{1,0:T(8,128)(2,1)S(1)} %collective-permute-done.36, ...), kind=kOutput, calls=%fused_computation.16 | convolution fusion | flops 1218183168 | bytes 17694720 | tf_op jit(solution)/shard_map/step/dot_general | solution.py:394
  (167 shorter events, 51.9 us)
Async XLA Ops:
  7.2 67.4 %all-gather.2.cloned.1.call-start = ((), (), s32[]{:S(2)}) async-start(), calls=%async_computation | async-start | bytes 4423680 | tf_op jit(solution)/shard_map/all_gather | solution.py:247
  15.2 15.4 %collective-permute-start = (bf16[2,256,512]{2,1,0:T(8,128)(2,1)S(1)}, bf16[2,256,512]{2,1,0:T(8,128)(2,1)S(1)}, u32[]{:S(2)}, u32[]{:S(2)}) collective-permute-start(bf16[2,256,512]{2,1,0:T(8,128)(2,1)S(1)} %copy-done.13), channel_id=1, source_target_pairs={{0,4},{1,5},{2,6},{3,7},{4,8},{5,9},{6,10},{7,11},{8,12},{9,13},{1... | collective-permute-start | bytes 1572872 | tf_op jit(solution)/shard_map/reduce_down/ppermute | solution.py:57
  17.2 14.8 %collective-permute-start.3 = (bf16[2,256,512]{2,1,0:T(8,128)(2,1)}, bf16[2,256,512]{2,1,0:T(8,128)(2,1)S(1)}, u32[]{:S(2)}, u32[]{:S(2)}) collective-permute-start(bf16[2,256,512]{2,1,0:T(8,128)(2,1)} %get-tuple-element.48), channel_id=1, source_target_pairs={{0,12},{1,13},{2,14},{3,15},{4,0},{5,1},{6,2},{7,3},{8,4},{9,5},{1... | collective-permute-start | bytes 1572872 | tf_op jit(solution)/shard_map/reduce_down/ppermute | solution.py:57
  28.7 13.4 %collective-permute-start.2 = (bf16[2,256,512]{2,1,0:T(8,128)(2,1)}, bf16[2,256,512]{2,1,0:T(8,128)(2,1)S(1)}, u32[]{:S(2)}, u32[]{:S(2)}) collective-permute-start(bf16[2,256,512]{2,1,0:T(8,128)(2,1)} %get-tuple-element.45), channel_id=1, source_target_pairs={{0,12},{1,13},{2,14},{3,15},{4,0},{5,1},{6,2},{7,3},{8,4},{9,5},{1... | collective-permute-start | bytes 1572872 | tf_op jit(solution)/shard_map/reduce_down/ppermute | solution.py:57
  31.8 10.5 %collective-permute-start.1 = (bf16[2,256,512]{2,1,0:T(8,128)(2,1)S(1)}, bf16[2,256,512]{2,1,0:T(8,128)(2,1)S(1)}, u32[]{:S(2)}, u32[]{:S(2)}) collective-permute-start(bf16[2,256,512]{2,1,0:T(8,128)(2,1)S(1)} %add.415), channel_id=1, source_target_pairs={{0,4},{1,5},{2,6},{3,7},{4,8},{5,9},{6,10},{7,11},{8,12},{9,13},{1... | collective-permute-start | bytes 1572872 | tf_op jit(solution)/shard_map/reduce_down/ppermute | solution.py:57
  32.0 15.9 %collective-permute-start.5 = (bf16[2,256,512]{2,1,0:T(8,128)(2,1)}, bf16[2,256,512]{2,1,0:T(8,128)(2,1)S(1)}, u32[]{:S(2)}, u32[]{:S(2)}) collective-permute-start(bf16[2,256,512]{2,1,0:T(8,128)(2,1)} %get-tuple-element.49), channel_id=1, source_target_pairs={{0,4},{1,5},{2,6},{3,7},{4,8},{5,9},{6,10},{7,11},{8,12},{9,13},{1... | collective-permute-start | bytes 1572872 | tf_op jit(solution)/shard_map/reduce_down/ppermute | solution.py:57
  33.2 14.7 %collective-permute-start.4 = (bf16[2,256,512]{2,1,0:T(8,128)(2,1)S(1)}, bf16[2,256,512]{2,1,0:T(8,128)(2,1)}, u32[]{:S(2)}, u32[]{:S(2)}) collective-permute-start(bf16[2,256,512]{2,1,0:T(8,128)(2,1)S(1)} %add.418), channel_id=1, source_target_pairs={{0,12},{1,13},{2,14},{3,15},{4,0},{5,1},{6,2},{7,3},{8,4},{9,5},{1... | collective-permute-start | bytes 1572872 | tf_op jit(solution)/shard_map/reduce_down/ppermute | solution.py:57
  50.0 13.0 %collective-permute-start.6 = (bf16[256,512]{1,0:T(8,128)(2,1)}, bf16[256,512]{1,0:T(8,128)(2,1)S(1)}, u32[]{:S(2)}, u32[]{:S(2)}) collective-permute-start(bf16[256,512]{1,0:T(8,128)(2,1)} %get-tuple-element.80), channel_id=1, source_target_pairs={{0,1},{1,2},{2,3},{3,0},{4,5},{5,6},{6,7},{7,4},{8,9},{9,10},{10,1... | collective-permute-start | bytes 786440 | tf_op jit(solution)/shard_map/reduce_down/ppermute | solution.py:57
  51.6 11.5 %collective-permute-start.8 = (bf16[256,512]{1,0:T(8,128)(2,1)S(1)}, bf16[256,512]{1,0:T(8,128)(2,1)S(1)}, u32[]{:S(2)}, u32[]{:S(2)}) collective-permute-start(bf16[256,512]{1,0:T(8,128)(2,1)S(1)} %get-tuple-element.81), channel_id=1, source_target_pairs={{0,2},{1,3},{2,0},{3,1},{4,6},{5,7},{6,4},{7,5},{8,10},{9,11},{10,... | collective-permute-start | bytes 786440 | tf_op jit(solution)/shard_map/reduce_down/ppermute | solution.py:57
  54.5 8.6 %collective-permute-start.7 = (bf16[256,512]{1,0:T(8,128)(2,1)S(1)}, bf16[256,512]{1,0:T(8,128)(2,1)S(1)}, u32[]{:S(2)}, u32[]{:S(2)}) collective-permute-start(bf16[256,512]{1,0:T(8,128)(2,1)S(1)} %get-tuple-element.82), channel_id=1, source_target_pairs={{0,3},{1,0},{2,1},{3,2},{4,7},{5,4},{6,5},{7,6},{8,11},{9,8},{10,9... | collective-permute-start | bytes 786440 | tf_op jit(solution)/shard_map/reduce_down/ppermute | solution.py:57
  64.3 9.5 %collective-permute-start.11 = (bf16[96,512]{1,0:T(8,128)(2,1)S(1)}, bf16[96,512]{1,0:T(8,128)(2,1)S(1)}, u32[]{:S(2)}, u32[]{:S(2)}) collective-permute-start(bf16[96,512]{1,0:T(8,128)(2,1)S(1)} %convolution_convert_fusion.2), channel_id=1, source_target_pairs={{0,32},{1,33},{2,34},{3,35},{4,36},{5,37},{6,38},{7,39},{8,40},{9,... | collective-permute-start | bytes 294920 | tf_op jit(solution)/shard_map/back/ppermute | solution.py:57
  65.9 7.9 %collective-permute-start.10 = (bf16[96,512]{1,0:T(8,128)(2,1)S(1)}, bf16[96,512]{1,0:T(8,128)(2,1)S(1)}, u32[]{:S(2)}, u32[]{:S(2)}) collective-permute-start(bf16[96,512]{1,0:T(8,128)(2,1)S(1)} %convolution_convert_fusion.2), channel_id=1, source_target_pairs={{0,64},{1,65},{2,66},{3,67},{4,68},{5,69},{6,70},{7,71},{8,72},{9,... | collective-permute-start | bytes 294920 | tf_op jit(solution)/shard_map/back/ppermute | solution.py:57
  71.0 14.3 %collective-permute-start.14 = (bf16[96,512]{1,0:T(8,128)(2,1)}, bf16[96,512]{1,0:T(8,128)(2,1)}, u32[]{:S(2)}, u32[]{:S(2)}) collective-permute-start(bf16[96,512]{1,0:T(8,128)(2,1)} %get-tuple-element.100), channel_id=1, source_target_pairs={{0,1},{1,0},{2,20},{3,16},{4,33},{5,32},{6,52},{7,48},{8,65},{9,64... | collective-permute-start | bytes 294920 | tf_op jit(solution)/shard_map/targets/ppermute | solution.py:57
  71.7 13.7 %collective-permute-start.13 = (bf16[96,512]{1,0:T(8,128)(2,1)}, bf16[96,512]{1,0:T(8,128)(2,1)}, u32[]{:S(2)}, u32[]{:S(2)}) collective-permute-start(bf16[96,512]{1,0:T(8,128)(2,1)} %get-tuple-element.101), channel_id=1, source_target_pairs={{0,0},{1,1},{2,16},{3,20},{4,32},{5,33},{6,48},{7,52},{8,64},{9,65... | collective-permute-start | bytes 294920 | tf_op jit(solution)/shard_map/targets/ppermute | solution.py:57
  80.8 13.0 %collective-permute-start.18 = (bf16[2,96,1024]{2,1,0:T(8,128)(2,1)S(1)}, bf16[2,96,1024]{2,1,0:T(8,128)(2,1)S(1)}, u32[]{:S(2)}, u32[]{:S(2)}) collective-permute-start(bf16[2,96,1024]{2,1,0:T(8,128)(2,1)S(1)} %bitcast.131), channel_id=1, source_target_pairs={{0,12},{1,13},{2,14},{3,15},{4,0},{5,1},{6,2},{7,3},{8,4},{9,5},{1... | collective-permute-start | bytes 1179656 | tf_op jit(solution)/shard_map/reduce_draft/ppermute | solution.py:57
  85.2 12.4 %collective-permute-start.15 = (bf16[2,96,1024]{2,1,0:T(8,128)(2,1)S(1)}, bf16[2,96,1024]{2,1,0:T(8,128)(2,1)S(1)}, u32[]{:S(2)}, u32[]{:S(2)}) collective-permute-start(bf16[2,96,1024]{2,1,0:T(8,128)(2,1)S(1)} %bitcast.130), channel_id=1, source_target_pairs={{0,4},{1,5},{2,6},{3,7},{4,8},{5,9},{6,10},{7,11},{8,12},{9,13},{1... | collective-permute-start | bytes 1179656 | tf_op jit(solution)/shard_map/reduce_draft/ppermute | solution.py:57
  86.7 16.0 %collective-permute-start.17 = (bf16[2,96,1024]{2,1,0:T(8,128)(2,1)S(1)}, bf16[2,96,1024]{2,1,0:T(8,128)(2,1)S(1)}, u32[]{:S(2)}, u32[]{:S(2)}) collective-permute-start(bf16[2,96,1024]{2,1,0:T(8,128)(2,1)S(1)} %bitcast.129), channel_id=1, source_target_pairs={{0,12},{1,13},{2,14},{3,15},{4,0},{5,1},{6,2},{7,3},{8,4},{9,5},{1... | collective-permute-start | bytes 1179656 | tf_op jit(solution)/shard_map/reduce_draft/ppermute | solution.py:57
  90.9 9.1 %collective-permute-start.20 = (bf16[2,96,1024]{2,1,0:T(8,128)(2,1)S(1)}, bf16[2,96,1024]{2,1,0:T(8,128)(2,1)S(1)}, u32[]{:S(2)}, u32[]{:S(2)}) collective-permute-start(bf16[2,96,1024]{2,1,0:T(8,128)(2,1)S(1)} %bitcast.132), channel_id=1, source_target_pairs={{0,4},{1,5},{2,6},{3,7},{4,8},{5,9},{6,10},{7,11},{8,12},{9,13},{1... | collective-permute-start | bytes 1179656 | tf_op jit(solution)/shard_map/reduce_draft/ppermute | solution.py:57
  93.9 8.6 %collective-permute-start.19 = (bf16[2,96,1024]{2,1,0:T(8,128)(2,1)S(1)}, bf16[2,96,1024]{2,1,0:T(8,128)(2,1)S(1)}, u32[]{:S(2)}, u32[]{:S(2)}) collective-permute-start(bf16[2,96,1024]{2,1,0:T(8,128)(2,1)S(1)} %add.475), channel_id=1, source_target_pairs={{0,12},{1,13},{2,14},{3,15},{4,0},{5,1},{6,2},{7,3},{8,4},{9,5},{1... | collective-permute-start | bytes 1179656 | tf_op jit(solution)/shard_map/reduce_draft/ppermute | solution.py:57
  97.7 9.1 %collective-permute-start.16 = (bf16[2,96,1024]{2,1,0:T(8,128)(2,1)S(1)}, bf16[2,96,1024]{2,1,0:T(8,128)(2,1)S(1)}, u32[]{:S(2)}, u32[]{:S(2)}) collective-permute-start(bf16[2,96,1024]{2,1,0:T(8,128)(2,1)S(1)} %add.470), channel_id=1, source_target_pairs={{0,4},{1,5},{2,6},{3,7},{4,8},{5,9},{6,10},{7,11},{8,12},{9,13},{1... | collective-permute-start | bytes 1179656 | tf_op jit(solution)/shard_map/reduce_draft/ppermute | solution.py:57
  107.1 10.0 %collective-permute-start.21 = (bf16[96,1024]{1,0:T(8,128)(2,1)S(1)}, bf16[96,1024]{1,0:T(8,128)(2,1)S(1)}, u32[]{:S(2)}, u32[]{:S(2)}) collective-permute-start(bf16[96,1024]{1,0:T(8,128)(2,1)S(1)} %get-tuple-element.87), channel_id=1, source_target_pairs={{0,1},{1,2},{2,3},{3,0},{4,5},{5,6},{6,7},{7,4},{8,9},{9,10},{10,1... | collective-permute-start | bytes 589832 | tf_op jit(solution)/shard_map/reduce_draft/ppermute | solution.py:57
  109.1 10.2 %collective-permute-start.23 = (bf16[96,1024]{1,0:T(8,128)(2,1)S(1)}, bf16[96,1024]{1,0:T(8,128)(2,1)S(1)}, u32[]{:S(2)}, u32[]{:S(2)}) collective-permute-start(bf16[96,1024]{1,0:T(8,128)(2,1)S(1)} %get-tuple-element.88), channel_id=1, source_target_pairs={{0,2},{1,3},{2,0},{3,1},{4,6},{5,7},{6,4},{7,5},{8,10},{9,11},{10,... | collective-permute-start | bytes 589832 | tf_op jit(solution)/shard_map/reduce_draft/ppermute | solution.py:57
  113.6 5.7 %collective-permute-start.22 = (bf16[96,1024]{1,0:T(8,128)(2,1)S(1)}, bf16[96,1024]{1,0:T(8,128)(2,1)S(1)}, u32[]{:S(2)}, u32[]{:S(2)}) collective-permute-start(bf16[96,1024]{1,0:T(8,128)(2,1)S(1)} %get-tuple-element.89), channel_id=1, source_target_pairs={{0,3},{1,0},{2,1},{3,2},{4,7},{5,4},{6,5},{7,6},{8,11},{9,8},{10,9... | collective-permute-start | bytes 589832 | tf_op jit(solution)/shard_map/reduce_draft/ppermute | solution.py:57
  127.6 14.2 %collective-permute-start.30 = (bf16[96,1024]{1,0:T(8,128)(2,1)S(1)}, bf16[96,1024]{1,0:T(8,128)(2,1)S(1)}, u32[]{:S(2)}, u32[]{:S(2)}) collective-permute-start(bf16[96,1024]{1,0:T(8,128)(2,1)S(1)} %fusion.55), channel_id=1, source_target_pairs={{0,1},{1,2},{2,3},{3,0},{4,5},{5,6},{6,7},{7,4},{8,9},{9,10},{10,1... | collective-permute-start | bytes 589832 | tf_op jit(solution)/shard_map/gather_slope/ppermute | solution.py:57
  131.9 15.0 %collective-permute-start.29 = (bf16[96,1024]{1,0:T(8,128)(2,1)S(1)}, bf16[96,1024]{1,0:T(8,128)(2,1)S(1)}, u32[]{:S(2)}, u32[]{:S(2)}) collective-permute-start(bf16[96,1024]{1,0:T(8,128)(2,1)S(1)} %fusion.55), channel_id=1, source_target_pairs={{0,2},{1,3},{2,0},{3,1},{4,6},{5,7},{6,4},{7,5},{8,10},{9,11},{10,... | collective-permute-start | bytes 589832 | tf_op jit(solution)/shard_map/gather_slope/ppermute | solution.py:57
  137.3 9.7 %collective-permute-start.28 = (bf16[96,1024]{1,0:T(8,128)(2,1)S(1)}, bf16[96,1024]{1,0:T(8,128)(2,1)S(1)}, u32[]{:S(2)}, u32[]{:S(2)}) collective-permute-start(bf16[96,1024]{1,0:T(8,128)(2,1)S(1)} %fusion.55), channel_id=1, source_target_pairs={{0,3},{1,0},{2,1},{3,2},{4,7},{5,4},{6,5},{7,6},{8,11},{9,8},{10,9... | collective-permute-start | bytes 589832 | tf_op jit(solution)/shard_map/gather_slope/ppermute | solution.py:57
  147.1 9.1 %collective-permute-start.31 = (bf16[192,1024]{1,0:T(8,128)(2,1)S(1)}, bf16[192,1024]{1,0:T(8,128)(2,1)S(1)}, u32[]{:S(2)}, u32[]{:S(2)}) collective-permute-start(bf16[192,1024]{1,0:T(8,128)(2,1)S(1)} %pad_maximum_fusion.6), channel_id=1, source_target_pairs={{0,4},{1,5},{2,6},{3,7},{4,8},{5,9},{6,10},{7,11},{8,12},{9,13},{1... | collective-permute-start | bytes 1179656 | tf_op jit(solution)/shard_map/gather_slope/ppermute | solution.py:57
  147.2 8.9 %collective-permute-start.32 = (bf16[192,1024]{1,0:T(8,128)(2,1)S(1)}, bf16[192,1024]{1,0:T(8,128)(2,1)S(1)}, u32[]{:S(2)}, u32[]{:S(2)}) collective-permute-start(bf16[192,1024]{1,0:T(8,128)(2,1)S(1)} %pad_maximum_fusion.7), channel_id=1, source_target_pairs={{0,12},{1,13},{2,14},{3,15},{4,0},{5,1},{6,2},{7,3},{8,4},{9,5},{1... | collective-permute-start | bytes 1179656 | tf_op jit(solution)/shard_map/gather_slope/ppermute | solution.py:57
  150.9 12.4 %collective-permute-start.34 = (bf16[192,1024]{1,0:T(8,128)(2,1)S(1)}, bf16[192,1024]{1,0:T(8,128)(2,1)S(1)}, u32[]{:S(2)}, u32[]{:S(2)}) collective-permute-start(bf16[192,1024]{1,0:T(8,128)(2,1)S(1)} %pad_maximum_fusion.6), channel_id=1, source_target_pairs={{0,12},{1,13},{2,14},{3,15},{4,0},{5,1},{6,2},{7,3},{8,4},{9,5},{1... | collective-permute-start | bytes 1179656 | tf_op jit(solution)/shard_map/gather_slope/ppermute | solution.py:57
  151.0 12.3 %collective-permute-start.33 = (bf16[192,1024]{1,0:T(8,128)(2,1)S(1)}, bf16[192,1024]{1,0:T(8,128)(2,1)S(1)}, u32[]{:S(2)}, u32[]{:S(2)}) collective-permute-start(bf16[192,1024]{1,0:T(8,128)(2,1)S(1)} %pad_maximum_fusion.7), channel_id=1, source_target_pairs={{0,4},{1,5},{2,6},{3,7},{4,8},{5,9},{6,10},{7,11},{8,12},{9,13},{1... | collective-permute-start | bytes 1179656 | tf_op jit(solution)/shard_map/gather_slope/ppermute | solution.py:57
  159.8 9.2 %collective-permute-start.35 = (bf16[192,1024]{1,0:T(8,128)(2,1)S(1)}, bf16[192,1024]{1,0:T(8,128)(2,1)S(1)}, u32[]{:S(2)}, u32[]{:S(2)}) collective-permute-start(bf16[192,1024]{1,0:T(8,128)(2,1)S(1)} %collective-permute-done.31), channel_id=1, source_target_pairs={{0,4},{1,5},{2,6},{3,7},{4,8},{5,9},{6,10},{7,11},{8,12},{9,13},{1... | collective-permute-start | bytes 1179656 | tf_op jit(solution)/shard_map/gather_slope/ppermute | solution.py:57
  159.9 9.1 %collective-permute-start.36 = (bf16[192,1024]{1,0:T(8,128)(2,1)S(1)}, bf16[192,1024]{1,0:T(8,128)(2,1)S(1)}, u32[]{:S(2)}, u32[]{:S(2)}) collective-permute-start(bf16[192,1024]{1,0:T(8,128)(2,1)S(1)} %collective-permute-done.32), channel_id=1, source_target_pairs={{0,12},{1,13},{2,14},{3,15},{4,0},{5,1},{6,2},{7,3},{8,4},{9,5},{1... | collective-permute-start | bytes 1179656 | tf_op jit(solution)/shard_map/gather_slope/ppermute | solution.py:57
  (26 other events, 150.6 us)
Sparse Core Ops, SparseCore 0:
  15.3 33.4 all-gather.1
where the time goes:
time: 181 us; the launch traced here: 180 us
  starting transfers between devices  67.1 us (37%)
  waiting for transfers between devices  32.7 us (18%)
  Pallas kernels  25.7 us (14%)
  matrix products  19.3 us (11%)
  between operations  14.8 us (8%)
  other arithmetic  12.3 us (7%)
  local copies, waits for them, and re-layouts  7.9 us (4%)
    ppermute x37, starting transfers between devices, send(): return lax.ppermute(array, mesh_axes, pairs)  67.1 us
    ppermute x37, waiting for transfers between devices, send(): return lax.ppermute(array, mesh_axes, pairs)  32.7 us
    pallas_call x3, Pallas kernels, down_pieces(): pl.pallas_call(down_kernel, grid_spec=pltpu.PrefetchScalarGridSpec(num_sc...  19.1 us
    dot_general x4, matrix products, product(): lax.dot_general(jnp.concatenate(inputs), jnp.concatenate(slopes), (((0,),...  9.62 us
    pallas_call x2, Pallas kernels, rounded_rows(): pl.pallas_call(round_kernel, grid=(count // step,), in_specs=[pl.BlockSpe...  6.62 us
    dot_general x8, matrix products, pair_product(): return jnp.dot(rows_of, weight, preferred_element_type=f32)  5.82 us
  transfers between devices with their start and end apart: 38, of which 14 were waited for; matrix products, arithmetic and copies ran while one was open for 16% of the time, Pallas kernels for 11%

commit v1 on v0

--- a/solution.py
+++ b/solution.py
@@ -140,27 +140,57 @@
     )(blocks, tokens, coded_weight, coded_weight, block_exponent, block_exponent)
 
 
-def round_kernel(after_ref, wide_ref, out_ref):
-    out_ref[...] = wide_ref[...].astype(bf16)
-
-
-def rounded_rows(wide, start, count, after):
-    step, columns = min(256, count), wide.shape[1]
+def round_kernel(pair_steps, after_ref, wide_ref, pair_ref, third_ref):
+    narrow = wide_ref[...].astype(bf16)
+
+    @pl.when(pl.program_id(0) < pair_steps)
+    def _():
+        pair_ref[...] = narrow
+
+    @pl.when(pl.program_id(0) >= pair_steps)
+    def _():
+        third_ref[...] = narrow
+
+
+def rounded_weight(wide, after):
+    rows, columns = wide.shape
+    step = rows // 6
+    pair_steps = 4
     return pl.pallas_call(
-        round_kernel,
-        grid=(count // step,),
+        functools.partial(round_kernel, pair_steps),
+        grid=(6,),
         in_specs=[
             pl.BlockSpec(memory_space=pl.ANY),
-            pl.BlockSpec((step, columns), lambda i: (start // step + i, 0)),
+            pl.BlockSpec((step, columns), lambda i: (i, 0)),
         ],
-        out_specs=pl.BlockSpec((step, columns), lambda i: (i, 0)),
-        out_shape=jax.ShapeDtypeStruct((count, columns), bf16),
+        out_specs=[
+            pl.BlockSpec((step, columns), lambda i: (jnp.minimum(i, pair_steps - 1), 0)),
+            pl.BlockSpec((step, columns), lambda i: (jnp.maximum(i - pair_steps, 0), 0)),
+        ],
+        out_shape=[
+            jax.ShapeDtypeStruct((step * pair_steps, columns), bf16),
+            jax.ShapeDtypeStruct((rows - step * pair_steps, columns), bf16),
+        ],
         compiler_params=pltpu.CompilerParams(vmem_limit_bytes=vmem),
         cost_estimate=pl.CostEstimate(
-            flops=count * columns, bytes_accessed=6 * count * columns, transcendentals=0
+            flops=rows * columns, bytes_accessed=6 * rows * columns, transcendentals=0
         ),
         name="round_weight",
     )(after, wide)
+
+
+def held_kernel(after_ref, value_ref, out_ref):
+    out_ref[...] = value_ref[...]
+
+
+def held(value, after):
+    return pl.pallas_call(
+        held_kernel,
+        in_specs=[pl.BlockSpec(memory_space=pl.ANY), pl.BlockSpec(memory_space=pltpu.VMEM)],
+        out_specs=pl.BlockSpec(memory_space=pltpu.VMEM),
+        out_shape=jax.ShapeDtypeStruct(value.shape, value.dtype),
+        name="held",
+    )(after, value)
 
 
 def reduce_blocks(near, direct, own, q):
@@ -168,8 +198,10 @@
     high_left = send(near[1], along_first(-1))
     high_right = send(direct[1], along_first(1))
     low_left = send(direct[2], along_first(-1))
-    low_right = send(direct[0] + low_right, along_first(1))
-    high_left = send(direct[3] + high_left, along_first(-1))
+    low_right, high_left = direct[0] + low_right, direct[3] + high_left
+    forwarded = high_left[0, :16, :128]
+    low_right = send(low_right, along_first(1))
+    high_left = send(high_left, along_first(-1))
     summed = jnp.concatenate(
         [plus(own[0], low_right, low_left), plus(own[1], high_left, high_right)]
     )
@@ -179,7 +211,7 @@
         return lax.dynamic_index_in_dim(array, (q + shift) % side, 0, keepdims=False)
 
     parts = [send(at(halved, shift), along_second(shift)) for shift in (1, 3, 2)]
-    return plus(at(summed, 0), *parts), summed[0, :8, :128]
+    return plus(at(summed, 0), *parts), forwarded, summed[0, :8, :128]
 
 
 def body(
@@ -227,7 +259,8 @@
         first_slot = jnp.where(first_live == 1, first_slot, -1)
         second_slot = jnp.where(second_live == 1, second_slot, -1)
         slot = jnp.arange(2 * slots, dtype=jnp.int32)[:, None]
-        select = (slot == jnp.concatenate([first_slot, second_slot])[None, :]).astype(bf16)
+        slot_of = jnp.concatenate([first_slot, second_slot])
+        select = (slot == slot_of[None, :]).astype(bf16)
 
         def pick(chosen, first, second):
             return jnp.dot(
@@ -253,12 +286,11 @@
         direct = down_pieces(others, tokens, coded_weight, block_exponent, bf16)
         direct, mine = lax.optimization_barrier((direct, columns(0)))
         own = down_pieces(mine, tokens, coded_weight, block_exponent, f32)
-
     with jax.named_scope("reduce_down"):
-        mixed, first_sum = reduce_blocks(near, direct, own, q)
+        mixed, _, first_sum = reduce_blocks(near, direct, own, q)
+
     flat_weight = draft_input_weight.reshape(3 * feature_slice, out_slice)
-    pair_weight = rounded_rows(flat_weight, 0, 2 * feature_slice, first_sum)
-    third_weight = rounded_rows(flat_weight, 2 * feature_slice, feature_slice, first_sum)
+    pair_weight, third_weight = rounded_weight(flat_weight, first_sum)
     upper_layer = (
         stream_input.astype(f32) + mixed.reshape(steps, rows, feature_slice)
     ).astype(bf16)
@@ -269,7 +301,69 @@
         chips = jnp.stack(turned(chips, x))
         others = send(chips, other_core())
 
+    with jax.named_scope("forward"):
+        by_replica = gathered.reshape(replicas, -1, 2 * feature_slice)
+        stride = by_replica.shape[1]
+        pairs, fronts = by_replica[:, : 2 * slots], by_replica[:, 2 * slots :]
+        fronts = jnp.concatenate(
+            [fronts[:, :, :feature_slice], fronts[:, :, feature_slice:]], axis=1
+        )
+
+        def replica_of(shift, half):
+            return 2 * ((p + shift) % side) + half
+
+        def pair_product(weight, shift, half):
+            rows_of = lax.dynamic_slice_in_dim(
+                gathered, replica_of(shift, half) * stride, 2 * slots, axis=0
+            )
+            return jnp.dot(rows_of, weight, preferred_element_type=f32)
+
+        def third_product(weight, shift, half):
+            rows_of = lax.dynamic_slice_in_dim(
+                thirds, replica_of(shift, half) * 2 * slots, 2 * slots, axis=0
+            )
+            return jnp.dot(rows_of, weight, preferred_element_type=f32)
+
+        def piece(total, kind):
+            return total.astype(kind).reshape(2, slots, out_slice)
+
+        far_pairs = [pair_product(pair_weight, 2, half) for half in range(2)]
+        others, fronts, far_pairs = lax.optimization_barrier((others, fronts, far_pairs))
+        backs = jnp.stack(
+            [jnp.where(c == 0, chips, others), jnp.where(c == 0, others, chips)], axis=1
+        ).reshape(replicas, slots, feature_slice)
+        thirds = jnp.concatenate([fronts, backs], axis=1).reshape(-1, feature_slice)
+        near = [
+            piece(far_pairs[half] + third_product(third_weight, 2, half), bf16)
+            for half in range(2)
+        ]
+        _, pair_weight, third_weight = lax.optimization_barrier(
+            (near, pair_weight, third_weight)
+        )
+        direct = [
+            piece(
+                pair_product(pair_weight, shift, half) + third_product(third_weight, shift, half),
+                bf16,
+            )
+            for shift in (1, 3)
+            for half in range(2)
+        ]
+        _, pair_weight, third_weight = lax.optimization_barrier(
+            (direct, pair_weight, third_weight)
+        )
+        own = [
+            piece(
+                pair_product(pair_weight, 0, half) + third_product(third_weight, 0, half), f32
+            )
+            for half in range(2)
+        ]
+
+    with jax.named_scope("reduce_draft"):
+        drafted, forwarded, _ = reduce_blocks(near, direct, own, q)
+
     with jax.named_scope("targets"):
+        slot_of = held(slot_of.reshape(1, -1), forwarded)
+        select = (slot == slot_of).astype(bf16)
         chosen = pick(select, upper_layer[0], upper_layer[1])
         parity = lax.axis_index("tensor") % 2
         even, odd = chosen[:slots], chosen[slots:]
@@ -283,68 +377,6 @@
                 taken = row_block(owner % cores, 2 * r + (t + turn) % 2)
                 routes.append((d, owner * tensors + taken))
             got.append(send(posted[turn], routes))
-
-    with jax.named_scope("forward"):
-        by_replica = gathered.reshape(replicas, -1, 2 * feature_slice)
-        stride = by_replica.shape[1]
-        pairs, fronts = by_replica[:, : 2 * slots], by_replica[:, 2 * slots :]
-        fronts = jnp.concatenate(
-            [fronts[:, :, :feature_slice], fronts[:, :, feature_slice:]], axis=1
-        )
-
-        def replica_of(shift, half):
-            return 2 * ((p + shift) % side) + half
-
-        def pair_product(weight, shift, half):
-            rows_of = lax.dynamic_slice_in_dim(
-                gathered, replica_of(shift, half) * stride, 2 * slots, axis=0
-            )
-            return jnp.dot(rows_of, weight, preferred_element_type=f32)
-
-        def third_product(weight, shift, half):
-            rows_of = lax.dynamic_slice_in_dim(
-                thirds, replica_of(shift, half) * 2 * slots, 2 * slots, axis=0
-            )
-            return jnp.dot(rows_of, weight, preferred_element_type=f32)
-
-        def piece(total, kind):
-            return total.astype(kind).reshape(2, slots, out_slice)
-
-        far_pairs = [pair_product(pair_weight, 2, half) for half in range(2)]
-        others, fronts, far_pairs, _ = lax.optimization_barrier(
-            (others, fronts, far_pairs, posted)
-        )
-        backs = jnp.stack(
-            [jnp.where(c == 0, chips, others), jnp.where(c == 0, others, chips)], axis=1
-        ).reshape(replicas, slots, feature_slice)
-        thirds = jnp.concatenate([fronts, backs], axis=1).reshape(-1, feature_slice)
-        near = [
-            piece(far_pairs[half] + third_product(third_weight, 2, half), bf16)
-            for half in range(2)
-        ]
-        _, got, pair_weight, third_weight = lax.optimization_barrier(
-            (near, got, pair_weight, third_weight)
-        )
-        direct = [
-            piece(
-                pair_product(pair_weight, shift, half) + third_product(third_weight, shift, half),
-                bf16,
-            )
-            for shift in (1, 3)
-            for half in range(2)
-        ]
-        _, pair_weight, third_weight = lax.optimization_barrier(
-            (direct, pair_weight, third_weight)
-        )
-        own = [
-            piece(
-                pair_product(pair_weight, 0, half) + third_product(third_weight, 0, half), f32
-            )
-            for half in range(2)
-        ]
-
-    with jax.named_scope("reduce_draft"):
-        drafted, _ = reduce_blocks(near, direct, own, q)
 
     with jax.named_scope("norm"):
         front_rows = q % 2 == 0
@@ -398,15 +430,13 @@
                 preferred_element_type=f32,
             )
 
-        upper_half, lower_half, previous_upper, following_lower = lax.optimization_barrier(
-            (upper_half, lower_half, previous_upper, following_lower)
-        )
         total = product([(0, 0), (0, 1)], [upper_half, lower_half])
         total = lax.optimization_barrier(
-            total + product([(3, 0), (1, 1)], [previous_upper, following_lower])
-        )
-        total = lax.optimization_barrier(
-            total + product([(3, 1), (1, 0)], [previous_lower, following_upper])
+            total
+            + product(
+                [(3, 0), (3, 1), (1, 0), (1, 1)],
+                [previous_upper, previous_lower, following_upper, following_lower],
+            )
         )
         total = total + product([(2, 0), (2, 1)], [low, high])
         new_weight = (flat_weight - step_rate * total).astype(bf16)

time: 181 us -> 183 us (1.011)
  starting transfers between devices: 67.1 us -> 60.3 us
  waiting for transfers between devices: 32.7 us -> 36.6 us
    ppermute x37, starting transfers between devices: 67.1 us -> 60.2 us  [send(): return lax.ppermute(array, mesh_axes, pairs)]
    ppermute x37, waiting for transfers between devices: 32.7 us -> 36.6 us  [send(): return lax.ppermute(array, mesh_axes, pairs)]
    add x5, other arithmetic: 3.35 us -> 5.31 us  [plus(): return functools.reduce(jnp.add, [term.astype(f32) for term in terms])]
    unnamed x40 -> x52, local copies, waits for them, and re-layouts: 2.98 us -> 4.4 us
    dot_general x4 -> x3, matrix products: 9.62 us -> 8.51 us  [product(): lax.dot_general(jnp.concatenate(inputs), jnp.concatenate(slopes), (((0,),...]
  transfers between devices with their start and end apart: 38 -> 38, of which waited for: 14 -> 19; matrix products, arithmetic and copies ran while one was open for 16% -> 17% of each run, Pallas kernels for 11% -> 12%
where the time goes in v1:
time: 183 us; the launch traced here: 181 us
  starting transfers between devices  60.3 us (33%)
  waiting for transfers between devices  36.6 us (20%)
  Pallas kernels  26.5 us (14%)
  matrix products  20.3 us (11%)
  between operations  14.9 us (8%)
  other arithmetic  13.4 us (7%)
  local copies, waits for them, and re-layouts  9.35 us (5%)
    ppermute x37, starting transfers between devices, send(): return lax.ppermute(array, mesh_axes, pairs)  60.2 us
    ppermute x37, waiting for transfers between devices, send(): return lax.ppermute(array, mesh_axes, pairs)  36.6 us
    pallas_call x3, Pallas kernels, down_pieces(): pl.pallas_call(down_kernel, grid_spec=pltpu.PrefetchScalarGridSpec(num_sc...  19 us
    dot_general x3, matrix products, product(): lax.dot_general(jnp.concatenate(inputs), jnp.concatenate(slopes), (((0,),...  8.51 us
    pallas_call x1, Pallas kernels, rounded_weight(): pl.pallas_call(functools.partial(round_kernel, pair_steps), grid=(6,), in...  6.29 us
    dot_general x8, matrix products, pair_product(): return jnp.dot(rows_of, weight, preferred_element_type=f32)  5.78 us
    add x5, other arithmetic, plus(): return functools.reduce(jnp.add, [term.astype(f32) for term in terms])  5.31 us
    dot_general x8, matrix products, third_product(): return jnp.dot(rows_of, weight, preferred_element_type=f32)  4.56 us
  transfers between devices with their start and end apart: 38, of which 19 were waited for; matrix products, arithmetic and copies ran while one was open for 17% of the time, Pallas kernels for 12%

profile of v1, /device:TPU:0, one launch (start us, length us, event | category | flops | bytes accessed | tf_op | source)
XLA Modules:
  0.0 181.3 jit_solution(7981193194971044699)
XLA Ops:
  7.8 5.4 %down_projection.3 = (bf16[2,256,512]{2,1,0:T(8,128)(2,1)}, bf16[2,256,512]{2,1,0:T(8,128)(2,1)}) custom-call(s32[4]{0:T(128)} %broadcast_select_fusion.17.blocks_ref, bf16[256,896]{1,0:T(8,128)(2,1)} %bitcast.122, bf16[896,8192]{1,0:T(8,128)(2,1)} %refs_1_.5, bf16[896,8192]{1,0:T(8,128)(2,1)} %refs_1_.5, s32[28,8192]{1,0:T(8,128)} %refs_3_.5, ...), custom_call_target="tpu_custom_call" | custom-call | flops 939524096 | bytes 5505024 | tf_op jit(solution)/shard_map/down/down_projection/pallas_call | solution.py:115
  15.2 4.2 %collective-permute-start.3 = (bf16[2,256,512]{2,1,0:T(8,128)(2,1)S(1)}, bf16[2,256,512]{2,1,0:T(8,128)(2,1)S(1)}, u32[]{:S(2)}, u32[]{:S(2)}) collective-permute-start(bf16[2,256,512]{2,1,0:T(8,128)(2,1)S(1)} %copy-done.19), channel_id=1, source_target_pairs={{0,12},{1,13},{2,14},{3,15},{4,0},{5,1},{6,2},{7,3},{8,4},{9,5},{1... | collective-permute-start | bytes 1572872 | tf_op jit(solution)/shard_map/reduce_down/ppermute | solution.py:57
  20.5 8.0 %down_projection.4 = (bf16[2,256,512]{2,1,0:T(8,128)(2,1)}, bf16[2,256,512]{2,1,0:T(8,128)(2,1)}, bf16[2,256,512]{2,1,0:T(8,128)(2,1)}, bf16[2,256,512]{2,1,0:T(8,128)(2,1)}) custom-call(s32[8]{0:T(128)} %pad_add_fusion.1.blocks_ref, bf16[256,896]{1,0:T(8,128)(2,1)} %bitcast.123, bf16[896,8192]{1,0:T(8,128)(2,1)} %refs_1_.5, bf16[896,8192]{1,0:T(8,128)(2,1)} %refs_1_.5, ...), custom_call_target="tpu_custom_call" | custom-call | flops 1879048192 | bytes 11010048 | tf_op jit(solution)/shard_map/down/down_projection/pallas_call | solution.py:115
  29.7 3.3 %collective-permute-start.4 = (bf16[2,256,512]{2,1,0:T(8,128)(2,1)S(1)}, bf16[2,256,512]{2,1,0:T(8,128)(2,1)S(1)}, u32[]{:S(2)}, u32[]{:S(2)}) collective-permute-start(bf16[2,256,512]{2,1,0:T(8,128)(2,1)S(1)} %add.415), channel_id=1, source_target_pairs={{0,12},{1,13},{2,14},{3,15},{4,0},{5,1},{6,2},{7,3},{8,4},{9,5},{1... | collective-permute-start | bytes 1572872 | tf_op jit(solution)/shard_map/reduce_down/ppermute | solution.py:57
  33.1 2.0 %collective-permute-start.2 = (bf16[2,256,512]{2,1,0:T(8,128)(2,1)}, bf16[2,256,512]{2,1,0:T(8,128)(2,1)S(1)}, u32[]{:S(2)}, u32[]{:S(2)}) collective-permute-start(bf16[2,256,512]{2,1,0:T(8,128)(2,1)} %get-tuple-element.41), channel_id=1, source_target_pairs={{0,12},{1,13},{2,14},{3,15},{4,0},{5,1},{6,2},{7,3},{8,4},{9,5},{1... | collective-permute-start | bytes 1572872 | tf_op jit(solution)/shard_map/reduce_down/ppermute | solution.py:57
  36.4 5.7 %down_projection.5 = (f32[2,256,512]{2,1,0:T(8,128)}, f32[2,256,512]{2,1,0:T(8,128)}) custom-call(s32[4]{0:T(128)} %get-tuple-element.37.blocks_ref, bf16[256,896]{1,0:T(8,128)(2,1)} %bitcast.124, bf16[896,8192]{1,0:T(8,128)(2,1)} %refs_1_.5, bf16[896,8192]{1,0:T(8,128)(2,1)} %refs_1_.5, s32[28,8192]{1,0:T(8,128)} %refs_3_.5, s32[28,8192]{1,0:T(8,128)} %refs_3_.5), custom_call_target="tpu_custom_call" | custom-call | flops 939524096 | bytes 5505024 | tf_op jit(solution)/shard_map/down/down_projection/pallas_call | solution.py:115
  52.3 2.0 %collective-permute-start.8 = (bf16[256,512]{1,0:T(8,128)(2,1)S(1)}, bf16[256,512]{1,0:T(8,128)(2,1)}, u32[]{:S(2)}, u32[]{:S(2)}) collective-permute-start(bf16[256,512]{1,0:T(8,128)(2,1)S(1)} %get-tuple-element.73), channel_id=1, source_target_pairs={{0,2},{1,3},{2,0},{3,1},{4,6},{5,7},{6,4},{7,5},{8,10},{9,11},{10,... | collective-permute-start | bytes 786440 | tf_op jit(solution)/shard_map/reduce_down/ppermute | solution.py:57
  54.3 2.4 %collective-permute-done.6 = bf16[256,512]{1,0:T(8,128)(2,1)S(1)} collective-permute-done((bf16[256,512]{1,0:T(8,128)(2,1)S(1)}, bf16[256,512]{1,0:T(8,128)(2,1)S(1)}, u32[]{:S(2)}, u32[]{:S(2)}) %collective-permute-start.6) | collective-permute-done | bytes 262176 | tf_op jit(solution)/shard_map/reduce_down/ppermute | solution.py:57
  57.0 3.8 %collective-permute-done.8 = bf16[256,512]{1,0:T(8,128)(2,1)} collective-permute-done((bf16[256,512]{1,0:T(8,128)(2,1)S(1)}, bf16[256,512]{1,0:T(8,128)(2,1)}, u32[]{:S(2)}, u32[]{:S(2)}) %collective-permute-start.8) | collective-permute-done | bytes 262176 | tf_op jit(solution)/shard_map/reduce_down/ppermute | solution.py:57
  62.3 3.1 %collective-permute-start.10 = (bf16[96,512]{1,0:T(8,128)(2,1)S(1)}, bf16[96,512]{1,0:T(8,128)(2,1)S(1)}, u32[]{:S(2)}, u32[]{:S(2)}) collective-permute-start(bf16[96,512]{1,0:T(8,128)(2,1)S(1)} %convolution_convert_fusion.2), channel_id=1, source_target_pairs={{0,64},{1,65},{2,66},{3,67},{4,68},{5,69},{6,70},{7,71},{8,72},{9,... | collective-permute-start | bytes 294920 | tf_op jit(solution)/shard_map/back/ppermute | solution.py:57
  66.1 2.6 %collective-permute-start.9 = (bf16[96,512]{1,0:T(8,128)(2,1)S(1)}, bf16[96,512]{1,0:T(8,128)(2,1)S(1)}, u32[]{:S(2)}, u32[]{:S(2)}) collective-permute-start(bf16[96,512]{1,0:T(8,128)(2,1)S(1)} %convolution_convert_fusion.2), channel_id=1, source_target_pairs={{0,96},{1,97},{2,98},{3,99},{4,100},{5,101},{6,102},{7,103},{8,104... | collective-permute-start | bytes 294920 | tf_op jit(solution)/shard_map/back/ppermute | solution.py:57
  69.3 6.3 %round_weight.1 = (bf16[1024,1024]{1,0:T(8,128)(2,1)}, bf16[512,1024]{1,0:T(8,128)(2,1)}) custom-call(f32[8,128]{1,0:T(8,128)} %slice_bitcast_fusion.3.after_ref, f32[1536,1024]{1,0:T(8,128)} %bitcast.106), custom_call_target="tpu_custom_call" | custom-call | flops 1572864 | bytes 9437184 | tf_op jit(solution)/shard_map/round_weight/pallas_call | solution.py:159
  77.4 1.7 fusion.79
  83.7 2.8 %collective-permute-start.16 = (bf16[2,96,1024]{2,1,0:T(8,128)(2,1)S(1)}, bf16[2,96,1024]{2,1,0:T(8,128)(2,1)S(1)}, u32[]{:S(2)}, u32[]{:S(2)}) collective-permute-start(bf16[2,96,1024]{2,1,0:T(8,128)(2,1)S(1)} %bitcast.133), channel_id=1, source_target_pairs={{0,12},{1,13},{2,14},{3,15},{4,0},{5,1},{6,2},{7,3},{8,4},{9,5},{1... | collective-permute-start | bytes 1179656 | tf_op jit(solution)/shard_map/reduce_draft/ppermute | solution.py:57
  96.0 2.4 %collective-permute-start.17 = (bf16[2,96,1024]{2,1,0:T(8,128)(2,1)S(1)}, bf16[2,96,1024]{2,1,0:T(8,128)(2,1)S(1)}, u32[]{:S(2)}, u32[]{:S(2)}) collective-permute-start(bf16[2,96,1024]{2,1,0:T(8,128)(2,1)S(1)} %add.468), channel_id=1, source_target_pairs={{0,12},{1,13},{2,14},{3,15},{4,0},{5,1},{6,2},{7,3},{8,4},{9,5},{1... | collective-permute-start | bytes 1179656 | tf_op jit(solution)/shard_map/reduce_draft/ppermute | solution.py:57
  104.2 5.1 %collective-permute-done.14 = bf16[2,96,1024]{2,1,0:T(8,128)(2,1)} collective-permute-done((bf16[2,96,1024]{2,1,0:T(8,128)(2,1)}, bf16[2,96,1024]{2,1,0:T(8,128)(2,1)}, u32[]{:S(2)}, u32[]{:S(2)}) %collective-permute-start.14) | collective-permute-done | bytes 393248 | tf_op jit(solution)/shard_map/reduce_draft/ppermute | solution.py:57
  112.2 1.8 collective-permute-start.20
  114.4 3.3 %collective-permute-done.19 = bf16[96,1024]{1,0:T(8,128)(2,1)S(1)} collective-permute-done((bf16[96,1024]{1,0:T(8,128)(2,1)S(1)}, bf16[96,1024]{1,0:T(8,128)(2,1)S(1)}, u32[]{:S(2)}, u32[]{:S(2)}) %collective-permute-start.19) | collective-permute-done | bytes 196640 | tf_op jit(solution)/shard_map/reduce_draft/ppermute | solution.py:57
  117.7 1.9 %collective-permute-done.20 = bf16[96,1024]{1,0:T(8,128)(2,1)S(1)} collective-permute-done((bf16[96,1024]{1,0:T(8,128)(2,1)S(1)}, bf16[96,1024]{1,0:T(8,128)(2,1)S(1)}, u32[]{:S(2)}, u32[]{:S(2)}) %collective-permute-start.20) | collective-permute-done | bytes 196640 | tf_op jit(solution)/shard_map/reduce_draft/ppermute | solution.py:57
  122.9 3.0 %collective-permute-start.26 = (f32[3,96]{1,0:T(4,128)S(1)}, f32[3,96]{1,0:T(4,128)S(1)}, u32[]{:S(2)}, u32[]{:S(2)}) collective-permute-start(f32[3,96]{1,0:T(4,128)S(1)} %fusion.127), channel_id=1, source_target_pairs={{0,64},{1,65},{2,66},{3,67},{4,68},{5,69},{6,70},{7,71},{8,72},{9,... | collective-permute-start | bytes 3464 | tf_op jit(solution)/shard_map/norm/ppermute | solution.py:57
  129.7 7.7 %collective-permute-start.28 = (bf16[96,1024]{1,0:T(8,128)(2,1)S(1)}, bf16[96,1024]{1,0:T(8,128)(2,1)S(1)}, u32[]{:S(2)}, u32[]{:S(2)}) collective-permute-start(bf16[96,1024]{1,0:T(8,128)(2,1)S(1)} %fusion.61), channel_id=1, source_target_pairs={{0,3},{1,0},{2,1},{3,2},{4,7},{5,4},{6,5},{7,6},{8,11},{9,8},{10,9... | collective-permute-start | bytes 589832 | tf_op jit(solution)/shard_map/gather_slope/ppermute | solution.py:57
  138.3 2.3 %slice.71 = bf16[8,192,1024]{2,1,0:T(8,128)(2,1)S(1)} slice(bf16[8,240,1024]{2,1,0:T(8,128)(2,1)} %bitcast.121), slice={[0:8], [0:192], [0:1024]} | slice | bytes 6291456 | tf_op jit(solution)/shard_map/forward/slice | solution.py:307
  140.6 2.0 %collective-permute-done.28 = bf16[96,1024]{1,0:T(8,128)(2,1)S(1)} collective-permute-done((bf16[96,1024]{1,0:T(8,128)(2,1)S(1)}, bf16[96,1024]{1,0:T(8,128)(2,1)S(1)}, u32[]{:S(2)}, u32[]{:S(2)}) %collective-permute-start.28) | collective-permute-done | bytes 196640 | tf_op jit(solution)/shard_map/gather_slope/ppermute | solution.py:57
  142.7 2.0 %collective-permute-done.29 = bf16[96,1024]{1,0:T(8,128)(2,1)S(1)} collective-permute-done((bf16[96,1024]{1,0:T(8,128)(2,1)S(1)}, bf16[96,1024]{1,0:T(8,128)(2,1)S(1)}, u32[]{:S(2)}, u32[]{:S(2)}) %collective-permute-start.29) | collective-permute-done | bytes 196640 | tf_op jit(solution)/shard_map/gather_slope/ppermute | solution.py:57
  146.5 5.2 %collective-permute-start.33 = (bf16[192,1024]{1,0:T(8,128)(2,1)S(1)}, bf16[192,1024]{1,0:T(8,128)(2,1)S(1)}, u32[]{:S(2)}, u32[]{:S(2)}) collective-permute-start(bf16[192,1024]{1,0:T(8,128)(2,1)S(1)} %pad_maximum_fusion.6), channel_id=1, source_target_pairs={{0,12},{1,13},{2,14},{3,15},{4,0},{5,1},{6,2},{7,3},{8,4},{9,5},{1... | collective-permute-start | bytes 1179656 | tf_op jit(solution)/shard_map/gather_slope/ppermute | solution.py:57
  151.8 3.2 %collective-permute-start.34 = (bf16[192,1024]{1,0:T(8,128)(2,1)S(1)}, bf16[192,1024]{1,0:T(8,128)(2,1)S(1)}, u32[]{:S(2)}, u32[]{:S(2)}) collective-permute-start(bf16[192,1024]{1,0:T(8,128)(2,1)S(1)} %pad_maximum_fusion.7), channel_id=1, source_target_pairs={{0,12},{1,13},{2,14},{3,15},{4,0},{5,1},{6,2},{7,3},{8,4},{9,5},{1... | collective-permute-start | bytes 1179656 | tf_op jit(solution)/shard_map/gather_slope/ppermute | solution.py:57
  155.5 1.9 %collective-permute-done.31 = bf16[192,1024]{1,0:T(8,128)(2,1)S(1)} collective-permute-done((bf16[192,1024]{1,0:T(8,128)(2,1)S(1)}, bf16[192,1024]{1,0:T(8,128)(2,1)S(1)}, u32[]{:S(2)}, u32[]{:S(2)}) %collective-permute-start.31) | collective-permute-done | bytes 393248 | tf_op jit(solution)/shard_map/gather_slope/ppermute | solution.py:57
  157.4 3.8 %collective-permute-done.34 = bf16[192,1024]{1,0:T(8,128)(2,1)S(1)} collective-permute-done((bf16[192,1024]{1,0:T(8,128)(2,1)S(1)}, bf16[192,1024]{1,0:T(8,128)(2,1)S(1)}, u32[]{:S(2)}, u32[]{:S(2)}) %collective-permute-start.34) | collective-permute-done | bytes 393248 | tf_op jit(solution)/shard_map/gather_slope/ppermute | solution.py:57
  161.2 3.7 %collective-permute-start.36 = (bf16[192,1024]{1,0:T(8,128)(2,1)S(1)}, bf16[192,1024]{1,0:T(8,128)(2,1)S(1)}, u32[]{:S(2)}, u32[]{:S(2)}) collective-permute-start(bf16[192,1024]{1,0:T(8,128)(2,1)S(1)} %collective-permute-done.34), channel_id=1, source_target_pairs={{0,12},{1,13},{2,14},{3,15},{4,0},{5,1},{6,2},{7,3},{8,4},{9,5},{1... | collective-permute-start | bytes 1179656 | tf_op jit(solution)/shard_map/gather_slope/ppermute | solution.py:57
  164.9 2.7 %fusion = f32[1536,1024]{1,0:T(8,128)S(1)} fusion(bf16[192,1536]{1,0:T(8,128)(2,1)S(1)} %get-tuple-element.69, bf16[192,1536]{1,0:T(8,128)(2,1)S(1)} %get-tuple-element.67, bf16[192,1536]{1,0:T(8,128)(2,1)S(1)} %get-tuple-element.66, bf16[192,1536]{1,0:T(8,128)(2,1)S(1)} %get-tuple-element.65, bf16[192,1024]{1,0:T(8,128)(2,1)S(1)} %collective-permute-done.34, ...), kind=kOutput, calls=%fused_computation.21 | convolution fusion | flops 2431647744 | bytes 10223616 | tf_op jit(solution)/shard_map/step/dot_general | solution.py:426
  167.6 1.9 %convolution_add_fusion = f32[1536,1024]{1,0:T(8,128)S(1)} fusion(f32[1536,1024]{1,0:T(8,128)S(1)} %fusion, bf16[192,1536]{1,0:T(8,128)(2,1)S(1)} %get-tuple-element.64, bf16[192,1536]{1,0:T(8,128)(2,1)S(1)} %get-tuple-element.63, bf16[96,1024]{1,0:T(8,128)(2,1)S(1)} %get-tuple-element.78, bf16[96,1024]{1,0:T(8,128)(2,1)S(1)} %get-tuple-element.77, ...), kind=kOutput, calls=%fused_computation.17 | convolution fusion | flops 1215037440 | bytes 14548992 | tf_op jit(solution)/shard_map/step/dot_general | solution.py:426
  170.5 4.0 %subtract_convert_fusion = bf16[1536,1024]{1,0:T(8,128)(2,1)} fusion(f32[1536,1024]{1,0:T(8,128)S(1)} %bitcast.109, f32[1536,1024]{1,0:T(8,128)S(1)} %convolution_add_fusion, bf16[192,1536]{1,0:T(8,128)(2,1)S(1)} %get-tuple-element.68, bf16[192,1536]{1,0:T(8,128)(2,1)S(1)} %get-tuple-element.62, bf16[192,1024]{1,0:T(8,128)(2,1)S(1)} %collective-permute-done.36, ...), kind=kOutput, calls=%fused_computation.16 | convolution fusion | flops 1218183168 | bytes 17694720 | tf_op jit(solution)/shard_map/step/dot_general | solution.py:426
  (179 shorter events, 55.4 us)
Async XLA Ops:
  7.2 68.7 %all-gather.2.cloned.1.call-start = ((), (), s32[]{:S(2)}) async-start(), calls=%async_computation | async-start | bytes 4423680 | tf_op jit(solution)/shard_map/all_gather | solution.py:280
  15.2 13.4 %collective-permute-start.3 = (bf16[2,256,512]{2,1,0:T(8,128)(2,1)S(1)}, bf16[2,256,512]{2,1,0:T(8,128)(2,1)S(1)}, u32[]{:S(2)}, u32[]{:S(2)}) collective-permute-start(bf16[2,256,512]{2,1,0:T(8,128)(2,1)S(1)} %copy-done.19), channel_id=1, source_target_pairs={{0,12},{1,13},{2,14},{3,15},{4,0},{5,1},{6,2},{7,3},{8,4},{9,5},{1... | collective-permute-start | bytes 1572872 | tf_op jit(solution)/shard_map/reduce_down/ppermute | solution.py:57
  19.4 15.7 %collective-permute-start = (bf16[2,256,512]{2,1,0:T(8,128)(2,1)S(1)}, bf16[2,256,512]{2,1,0:T(8,128)(2,1)S(1)}, u32[]{:S(2)}, u32[]{:S(2)}) collective-permute-start(bf16[2,256,512]{2,1,0:T(8,128)(2,1)S(1)} %copy-done.18), channel_id=1, source_target_pairs={{0,4},{1,5},{2,6},{3,7},{4,8},{5,9},{6,10},{7,11},{8,12},{9,13},{1... | collective-permute-start | bytes 1572872 | tf_op jit(solution)/shard_map/reduce_down/ppermute | solution.py:57
  28.5 13.6 %collective-permute-start.5 = (bf16[2,256,512]{2,1,0:T(8,128)(2,1)}, bf16[2,256,512]{2,1,0:T(8,128)(2,1)S(1)}, u32[]{:S(2)}, u32[]{:S(2)}) collective-permute-start(bf16[2,256,512]{2,1,0:T(8,128)(2,1)} %get-tuple-element.45), channel_id=1, source_target_pairs={{0,4},{1,5},{2,6},{3,7},{4,8},{5,9},{6,10},{7,11},{8,12},{9,13},{1... | collective-permute-start | bytes 1572872 | tf_op jit(solution)/shard_map/reduce_down/ppermute | solution.py:57
  29.7 12.4 %collective-permute-start.4 = (bf16[2,256,512]{2,1,0:T(8,128)(2,1)S(1)}, bf16[2,256,512]{2,1,0:T(8,128)(2,1)S(1)}, u32[]{:S(2)}, u32[]{:S(2)}) collective-permute-start(bf16[2,256,512]{2,1,0:T(8,128)(2,1)S(1)} %add.415), channel_id=1, source_target_pairs={{0,12},{1,13},{2,14},{3,15},{4,0},{5,1},{6,2},{7,3},{8,4},{9,5},{1... | collective-permute-start | bytes 1572872 | tf_op jit(solution)/shard_map/reduce_down/ppermute | solution.py:57
  33.1 12.4 %collective-permute-start.2 = (bf16[2,256,512]{2,1,0:T(8,128)(2,1)}, bf16[2,256,512]{2,1,0:T(8,128)(2,1)S(1)}, u32[]{:S(2)}, u32[]{:S(2)}) collective-permute-start(bf16[2,256,512]{2,1,0:T(8,128)(2,1)} %get-tuple-element.41), channel_id=1, source_target_pairs={{0,12},{1,13},{2,14},{3,15},{4,0},{5,1},{6,2},{7,3},{8,4},{9,5},{1... | collective-permute-start | bytes 1572872 | tf_op jit(solution)/shard_map/reduce_down/ppermute | solution.py:57
  36.3 10.5 %collective-permute-start.1 = (bf16[2,256,512]{2,1,0:T(8,128)(2,1)S(1)}, bf16[2,256,512]{2,1,0:T(8,128)(2,1)S(1)}, u32[]{:S(2)}, u32[]{:S(2)}) collective-permute-start(bf16[2,256,512]{2,1,0:T(8,128)(2,1)S(1)} %add.412), channel_id=1, source_target_pairs={{0,4},{1,5},{2,6},{3,7},{4,8},{5,9},{6,10},{7,11},{8,12},{9,13},{1... | collective-permute-start | bytes 1572872 | tf_op jit(solution)/shard_map/reduce_down/ppermute | solution.py:57
  49.0 7.7 %collective-permute-start.6 = (bf16[256,512]{1,0:T(8,128)(2,1)S(1)}, bf16[256,512]{1,0:T(8,128)(2,1)S(1)}, u32[]{:S(2)}, u32[]{:S(2)}) collective-permute-start(bf16[256,512]{1,0:T(8,128)(2,1)S(1)} %get-tuple-element.72), channel_id=1, source_target_pairs={{0,1},{1,2},{2,3},{3,0},{4,5},{5,6},{6,7},{7,4},{8,9},{9,10},{10,1... | collective-permute-start | bytes 786440 | tf_op jit(solution)/shard_map/reduce_down/ppermute | solution.py:57
  52.3 8.5 %collective-permute-start.8 = (bf16[256,512]{1,0:T(8,128)(2,1)S(1)}, bf16[256,512]{1,0:T(8,128)(2,1)}, u32[]{:S(2)}, u32[]{:S(2)}) collective-permute-start(bf16[256,512]{1,0:T(8,128)(2,1)S(1)} %get-tuple-element.73), channel_id=1, source_target_pairs={{0,2},{1,3},{2,0},{3,1},{4,6},{5,7},{6,4},{7,5},{8,10},{9,11},{10,... | collective-permute-start | bytes 786440 | tf_op jit(solution)/shard_map/reduce_down/ppermute | solution.py:57
  62.3 13.3 %collective-permute-start.10 = (bf16[96,512]{1,0:T(8,128)(2,1)S(1)}, bf16[96,512]{1,0:T(8,128)(2,1)S(1)}, u32[]{:S(2)}, u32[]{:S(2)}) collective-permute-start(bf16[96,512]{1,0:T(8,128)(2,1)S(1)} %convolution_convert_fusion.2), channel_id=1, source_target_pairs={{0,64},{1,65},{2,66},{3,67},{4,68},{5,69},{6,70},{7,71},{8,72},{9,... | collective-permute-start | bytes 294920 | tf_op jit(solution)/shard_map/back/ppermute | solution.py:57
  65.4 10.1 %collective-permute-start.11 = (bf16[96,512]{1,0:T(8,128)(2,1)S(1)}, bf16[96,512]{1,0:T(8,128)(2,1)S(1)}, u32[]{:S(2)}, u32[]{:S(2)}) collective-permute-start(bf16[96,512]{1,0:T(8,128)(2,1)S(1)} %convolution_convert_fusion.2), channel_id=1, source_target_pairs={{0,32},{1,33},{2,34},{3,35},{4,36},{5,37},{6,38},{7,39},{8,40},{9,... | collective-permute-start | bytes 294920 | tf_op jit(solution)/shard_map/back/ppermute | solution.py:57
  66.1 9.5 %collective-permute-start.9 = (bf16[96,512]{1,0:T(8,128)(2,1)S(1)}, bf16[96,512]{1,0:T(8,128)(2,1)S(1)}, u32[]{:S(2)}, u32[]{:S(2)}) collective-permute-start(bf16[96,512]{1,0:T(8,128)(2,1)S(1)} %convolution_convert_fusion.2), channel_id=1, source_target_pairs={{0,96},{1,97},{2,98},{3,99},{4,100},{5,101},{6,102},{7,103},{8,104... | collective-permute-start | bytes 294920 | tf_op jit(solution)/shard_map/back/ppermute | solution.py:57
  82.8 16.3 %collective-permute-start.13 = (bf16[2,96,1024]{2,1,0:T(8,128)(2,1)S(1)}, bf16[2,96,1024]{2,1,0:T(8,128)(2,1)S(1)}, u32[]{:S(2)}, u32[]{:S(2)}) collective-permute-start(bf16[2,96,1024]{2,1,0:T(8,128)(2,1)S(1)} %bitcast.132), channel_id=1, source_target_pairs={{0,4},{1,5},{2,6},{3,7},{4,8},{5,9},{6,10},{7,11},{8,12},{9,13},{1... | collective-permute-start | bytes 1179656 | tf_op jit(solution)/shard_map/reduce_draft/ppermute | solution.py:57
  83.7 12.2 %collective-permute-start.16 = (bf16[2,96,1024]{2,1,0:T(8,128)(2,1)S(1)}, bf16[2,96,1024]{2,1,0:T(8,128)(2,1)S(1)}, u32[]{:S(2)}, u32[]{:S(2)}) collective-permute-start(bf16[2,96,1024]{2,1,0:T(8,128)(2,1)S(1)} %bitcast.133), channel_id=1, source_target_pairs={{0,12},{1,13},{2,14},{3,15},{4,0},{5,1},{6,2},{7,3},{8,4},{9,5},{1... | collective-permute-start | bytes 1179656 | tf_op jit(solution)/shard_map/reduce_draft/ppermute | solution.py:57
  88.2 14.5 %collective-permute-start.15 = (bf16[2,96,1024]{2,1,0:T(8,128)(2,1)}, bf16[2,96,1024]{2,1,0:T(8,128)(2,1)S(1)}, u32[]{:S(2)}, u32[]{:S(2)}) collective-permute-start(bf16[2,96,1024]{2,1,0:T(8,128)(2,1)} %bitcast.23), channel_id=1, source_target_pairs={{0,12},{1,13},{2,14},{3,15},{4,0},{5,1},{6,2},{7,3},{8,4},{9,5},{1... | collective-permute-start | bytes 1179656 | tf_op jit(solution)/shard_map/reduce_draft/ppermute | solution.py:57
  91.1 19.3 %collective-permute-start.18 = (bf16[2,96,1024]{2,1,0:T(8,128)(2,1)}, bf16[2,96,1024]{2,1,0:T(8,128)(2,1)S(1)}, u32[]{:S(2)}, u32[]{:S(2)}) collective-permute-start(bf16[2,96,1024]{2,1,0:T(8,128)(2,1)} %bitcast.22), channel_id=1, source_target_pairs={{0,4},{1,5},{2,6},{3,7},{4,8},{5,9},{6,10},{7,11},{8,12},{9,13},{1... | collective-permute-start | bytes 1179656 | tf_op jit(solution)/shard_map/reduce_draft/ppermute | solution.py:57
  96.0 14.4 %collective-permute-start.17 = (bf16[2,96,1024]{2,1,0:T(8,128)(2,1)S(1)}, bf16[2,96,1024]{2,1,0:T(8,128)(2,1)S(1)}, u32[]{:S(2)}, u32[]{:S(2)}) collective-permute-start(bf16[2,96,1024]{2,1,0:T(8,128)(2,1)S(1)} %add.468), channel_id=1, source_target_pairs={{0,12},{1,13},{2,14},{3,15},{4,0},{5,1},{6,2},{7,3},{8,4},{9,5},{1... | collective-permute-start | bytes 1179656 | tf_op jit(solution)/shard_map/reduce_draft/ppermute | solution.py:57
  99.9 9.3 %collective-permute-start.14 = (bf16[2,96,1024]{2,1,0:T(8,128)(2,1)}, bf16[2,96,1024]{2,1,0:T(8,128)(2,1)}, u32[]{:S(2)}, u32[]{:S(2)}) collective-permute-start(bf16[2,96,1024]{2,1,0:T(8,128)(2,1)} %add.463), channel_id=1, source_target_pairs={{0,4},{1,5},{2,6},{3,7},{4,8},{5,9},{6,10},{7,11},{8,12},{9,13},{1... | collective-permute-start | bytes 1179656 | tf_op jit(solution)/shard_map/reduce_draft/ppermute | solution.py:57
  102.0 12.4 %collective-permute-start.22 = (bf16[96,512]{1,0:T(8,128)(2,1)S(1)}, bf16[96,512]{1,0:T(8,128)(2,1)S(1)}, u32[]{:S(2)}, u32[]{:S(2)}) collective-permute-start(bf16[96,512]{1,0:T(8,128)(2,1)S(1)} %get-tuple-element.92), channel_id=1, source_target_pairs={{0,0},{1,1},{2,16},{3,20},{4,32},{5,33},{6,48},{7,52},{8,64},{9,65... | collective-permute-start | bytes 294920 | tf_op jit(solution)/shard_map/targets/ppermute | solution.py:57
  102.7 11.7 %collective-permute-start.23 = (bf16[96,512]{1,0:T(8,128)(2,1)S(1)}, bf16[96,512]{1,0:T(8,128)(2,1)S(1)}, u32[]{:S(2)}, u32[]{:S(2)}) collective-permute-start(bf16[96,512]{1,0:T(8,128)(2,1)S(1)} %get-tuple-element.93), channel_id=1, source_target_pairs={{0,1},{1,0},{2,20},{3,16},{4,33},{5,32},{6,52},{7,48},{8,65},{9,64... | collective-permute-start | bytes 294920 | tf_op jit(solution)/shard_map/targets/ppermute | solution.py:57
  110.7 6.9 %collective-permute-start.19 = (bf16[96,1024]{1,0:T(8,128)(2,1)S(1)}, bf16[96,1024]{1,0:T(8,128)(2,1)S(1)}, u32[]{:S(2)}, u32[]{:S(2)}) collective-permute-start(bf16[96,1024]{1,0:T(8,128)(2,1)S(1)} %get-tuple-element.79), channel_id=1, source_target_pairs={{0,1},{1,2},{2,3},{3,0},{4,5},{5,6},{6,7},{7,4},{8,9},{9,10},{10,1... | collective-permute-start | bytes 589832 | tf_op jit(solution)/shard_map/reduce_draft/ppermute | solution.py:57
  112.2 7.4 %collective-permute-start.20 = (bf16[96,1024]{1,0:T(8,128)(2,1)S(1)}, bf16[96,1024]{1,0:T(8,128)(2,1)S(1)}, u32[]{:S(2)}, u32[]{:S(2)}) collective-permute-start(bf16[96,1024]{1,0:T(8,128)(2,1)S(1)} %get-tuple-element.81), channel_id=1, source_target_pairs={{0,3},{1,0},{2,1},{3,2},{4,7},{5,4},{6,5},{7,6},{8,11},{9,8},{10,9... | collective-permute-start | bytes 589832 | tf_op jit(solution)/shard_map/reduce_draft/ppermute | solution.py:57
  114.0 7.2 %collective-permute-start.21 = (bf16[96,1024]{1,0:T(8,128)(2,1)S(1)}, bf16[96,1024]{1,0:T(8,128)(2,1)S(1)}, u32[]{:S(2)}, u32[]{:S(2)}) collective-permute-start(bf16[96,1024]{1,0:T(8,128)(2,1)S(1)} %get-tuple-element.80), channel_id=1, source_target_pairs={{0,2},{1,3},{2,0},{3,1},{4,6},{5,7},{6,4},{7,5},{8,10},{9,11},{10,... | collective-permute-start | bytes 589832 | tf_op jit(solution)/shard_map/reduce_draft/ppermute | solution.py:57
  129.7 12.9 %collective-permute-start.28 = (bf16[96,1024]{1,0:T(8,128)(2,1)S(1)}, bf16[96,1024]{1,0:T(8,128)(2,1)S(1)}, u32[]{:S(2)}, u32[]{:S(2)}) collective-permute-start(bf16[96,1024]{1,0:T(8,128)(2,1)S(1)} %fusion.61), channel_id=1, source_target_pairs={{0,3},{1,0},{2,1},{3,2},{4,7},{5,4},{6,5},{7,6},{8,11},{9,8},{10,9... | collective-permute-start | bytes 589832 | tf_op jit(solution)/shard_map/gather_slope/ppermute | solution.py:57
  137.4 7.3 %collective-permute-start.29 = (bf16[96,1024]{1,0:T(8,128)(2,1)S(1)}, bf16[96,1024]{1,0:T(8,128)(2,1)S(1)}, u32[]{:S(2)}, u32[]{:S(2)}) collective-permute-start(bf16[96,1024]{1,0:T(8,128)(2,1)S(1)} %fusion.61), channel_id=1, source_target_pairs={{0,2},{1,3},{2,0},{3,1},{4,6},{5,7},{6,4},{7,5},{8,10},{9,11},{10,... | collective-permute-start | bytes 589832 | tf_op jit(solution)/shard_map/gather_slope/ppermute | solution.py:57
  137.4 9.0 %collective-permute-start.30 = (bf16[96,1024]{1,0:T(8,128)(2,1)S(1)}, bf16[96,1024]{1,0:T(8,128)(2,1)S(1)}, u32[]{:S(2)}, u32[]{:S(2)}) collective-permute-start(bf16[96,1024]{1,0:T(8,128)(2,1)S(1)} %fusion.61), channel_id=1, source_target_pairs={{0,1},{1,2},{2,3},{3,0},{4,5},{5,6},{6,7},{7,4},{8,9},{9,10},{10,1... | collective-permute-start | bytes 589832 | tf_op jit(solution)/shard_map/gather_slope/ppermute | solution.py:57
  146.5 10.9 %collective-permute-start.31 = (bf16[192,1024]{1,0:T(8,128)(2,1)S(1)}, bf16[192,1024]{1,0:T(8,128)(2,1)S(1)}, u32[]{:S(2)}, u32[]{:S(2)}) collective-permute-start(bf16[192,1024]{1,0:T(8,128)(2,1)S(1)} %pad_maximum_fusion.6), channel_id=1, source_target_pairs={{0,4},{1,5},{2,6},{3,7},{4,8},{5,9},{6,10},{7,11},{8,12},{9,13},{1... | collective-permute-start | bytes 1179656 | tf_op jit(solution)/shard_map/gather_slope/ppermute | solution.py:57
  146.5 18.4 %collective-permute-start.33 = (bf16[192,1024]{1,0:T(8,128)(2,1)S(1)}, bf16[192,1024]{1,0:T(8,128)(2,1)S(1)}, u32[]{:S(2)}, u32[]{:S(2)}) collective-permute-start(bf16[192,1024]{1,0:T(8,128)(2,1)S(1)} %pad_maximum_fusion.6), channel_id=1, source_target_pairs={{0,12},{1,13},{2,14},{3,15},{4,0},{5,1},{6,2},{7,3},{8,4},{9,5},{1... | collective-permute-start | bytes 1179656 | tf_op jit(solution)/shard_map/gather_slope/ppermute | solution.py:57
  151.7 13.2 %collective-permute-start.32 = (bf16[192,1024]{1,0:T(8,128)(2,1)S(1)}, bf16[192,1024]{1,0:T(8,128)(2,1)S(1)}, u32[]{:S(2)}, u32[]{:S(2)}) collective-permute-start(bf16[192,1024]{1,0:T(8,128)(2,1)S(1)} %pad_maximum_fusion.7), channel_id=1, source_target_pairs={{0,4},{1,5},{2,6},{3,7},{4,8},{5,9},{6,10},{7,11},{8,12},{9,13},{1... | collective-permute-start | bytes 1179656 | tf_op jit(solution)/shard_map/gather_slope/ppermute | solution.py:57
  151.8 9.4 %collective-permute-start.34 = (bf16[192,1024]{1,0:T(8,128)(2,1)S(1)}, bf16[192,1024]{1,0:T(8,128)(2,1)S(1)}, u32[]{:S(2)}, u32[]{:S(2)}) collective-permute-start(bf16[192,1024]{1,0:T(8,128)(2,1)S(1)} %pad_maximum_fusion.7), channel_id=1, source_target_pairs={{0,12},{1,13},{2,14},{3,15},{4,0},{5,1},{6,2},{7,3},{8,4},{9,5},{1... | collective-permute-start | bytes 1179656 | tf_op jit(solution)/shard_map/gather_slope/ppermute | solution.py:57
  157.4 12.1 %collective-permute-start.35 = (bf16[192,1024]{1,0:T(8,128)(2,1)S(1)}, bf16[192,1024]{1,0:T(8,128)(2,1)S(1)}, u32[]{:S(2)}, u32[]{:S(2)}) collective-permute-start(bf16[192,1024]{1,0:T(8,128)(2,1)S(1)} %collective-permute-done.31), channel_id=1, source_target_pairs={{0,4},{1,5},{2,6},{3,7},{4,8},{5,9},{6,10},{7,11},{8,12},{9,13},{1... | collective-permute-start | bytes 1179656 | tf_op jit(solution)/shard_map/gather_slope/ppermute | solution.py:57
  161.2 9.0 %collective-permute-start.36 = (bf16[192,1024]{1,0:T(8,128)(2,1)S(1)}, bf16[192,1024]{1,0:T(8,128)(2,1)S(1)}, u32[]{:S(2)}, u32[]{:S(2)}) collective-permute-start(bf16[192,1024]{1,0:T(8,128)(2,1)S(1)} %collective-permute-done.34), channel_id=1, source_target_pairs={{0,12},{1,13},{2,14},{3,15},{4,0},{5,1},{6,2},{7,3},{8,4},{9,5},{1... | collective-permute-start | bytes 1179656 | tf_op jit(solution)/shard_map/gather_slope/ppermute | solution.py:57
  (32 other events, 185.6 us)
Sparse Core Ops, SparseCore 0:
  15.3 33.4 all-gather.1

commit v2 on v0

--- a/solution.py
+++ b/solution.py
@@ -140,27 +140,48 @@
     )(blocks, tokens, coded_weight, coded_weight, block_exponent, block_exponent)
 
 
-def round_kernel(after_ref, wide_ref, out_ref):
-    out_ref[...] = wide_ref[...].astype(bf16)
-
-
-def rounded_rows(wide, start, count, after):
-    step, columns = min(256, count), wide.shape[1]
+def round_kernel(after_ref, upper_ref, lower_ref, out_ref):
+    half = upper_ref.shape[0]
+    out_ref[:half] = upper_ref[...].astype(bf16)
+    out_ref[half:] = lower_ref[...].astype(bf16)
+
+
+def rounded_layers(wide, layers, start, after):
+    rows, columns = wide.shape
+    step = rows // 3
+
+    def half_layer(half):
+        return pl.BlockSpec((step // 2, columns), lambda i: (2 * (start + i) + half, 0))
+
     return pl.pallas_call(
         round_kernel,
-        grid=(count // step,),
-        in_specs=[
-            pl.BlockSpec(memory_space=pl.ANY),
-            pl.BlockSpec((step, columns), lambda i: (start // step + i, 0)),
-        ],
+        grid=(layers,),
+        in_specs=[pl.BlockSpec(memory_space=pl.ANY), half_layer(0), half_layer(1)],
         out_specs=pl.BlockSpec((step, columns), lambda i: (i, 0)),
-        out_shape=jax.ShapeDtypeStruct((count, columns), bf16),
+        out_shape=jax.ShapeDtypeStruct((step * layers, columns), bf16),
         compiler_params=pltpu.CompilerParams(vmem_limit_bytes=vmem),
         cost_estimate=pl.CostEstimate(
-            flops=count * columns, bytes_accessed=6 * count * columns, transcendentals=0
+            flops=layers * step * columns,
+            bytes_accessed=6 * layers * step * columns,
+            transcendentals=0,
         ),
         name="round_weight",
-    )(after, wide)
+    )(after, wide, wide)
+
+
+def together_kernel(first_ref, second_ref, first_out_ref, second_out_ref):
+    first_out_ref[...] = first_ref[...]
+    second_out_ref[...] = second_ref[...]
+
+
+def together(first, second):
+    return pl.pallas_call(
+        together_kernel,
+        in_specs=[pl.BlockSpec(memory_space=pltpu.VMEM)] * 2,
+        out_specs=[pl.BlockSpec(memory_space=pltpu.VMEM)] * 2,
+        out_shape=[jax.ShapeDtypeStruct(a.shape, a.dtype) for a in (first, second)],
+        name="together",
+    )(first, second)
 
 
 def reduce_blocks(near, direct, own, q):
@@ -168,8 +189,9 @@
     high_left = send(near[1], along_first(-1))
     high_right = send(direct[1], along_first(1))
     low_left = send(direct[2], along_first(-1))
-    low_right = send(direct[0] + low_right, along_first(1))
-    high_left = send(direct[3] + high_left, along_first(-1))
+    low_right, high_left = direct[0] + low_right, direct[3] + high_left
+    low_right = send(low_right, along_first(1))
+    high_left = send(high_left, along_first(-1))
     summed = jnp.concatenate(
         [plus(own[0], low_right, low_left), plus(own[1], high_left, high_right)]
     )
@@ -227,7 +249,8 @@
         first_slot = jnp.where(first_live == 1, first_slot, -1)
         second_slot = jnp.where(second_live == 1, second_slot, -1)
         slot = jnp.arange(2 * slots, dtype=jnp.int32)[:, None]
-        select = (slot == jnp.concatenate([first_slot, second_slot])[None, :]).astype(bf16)
+        slot_of = jnp.concatenate([first_slot, second_slot])
+        select = (slot == slot_of[None, :]).astype(bf16)
 
         def pick(chosen, first, second):
             return jnp.dot(
@@ -253,12 +276,12 @@
         direct = down_pieces(others, tokens, coded_weight, block_exponent, bf16)
         direct, mine = lax.optimization_barrier((direct, columns(0)))
         own = down_pieces(mine, tokens, coded_weight, block_exponent, f32)
-
     with jax.named_scope("reduce_down"):
         mixed, first_sum = reduce_blocks(near, direct, own, q)
+
     flat_weight = draft_input_weight.reshape(3 * feature_slice, out_slice)
-    pair_weight = rounded_rows(flat_weight, 0, 2 * feature_slice, first_sum)
-    third_weight = rounded_rows(flat_weight, 2 * feature_slice, feature_slice, first_sum)
+    pair_weight = rounded_layers(flat_weight, 2, 0, first_sum)
+    third_weight = rounded_layers(flat_weight, 1, 2, first_sum)
     upper_layer = (
         stream_input.astype(f32) + mixed.reshape(steps, rows, feature_slice)
     ).astype(bf16)
@@ -310,7 +333,9 @@
         def piece(total, kind):
             return total.astype(kind).reshape(2, slots, out_slice)
 
-        far_pairs = [pair_product(pair_weight, 2, half) for half in range(2)]
+        far_pairs = [
+            pair_product(pair_weight, shift, half) for shift in (2, 1, 3) for half in range(2)
+        ]
         others, fronts, far_pairs, _ = lax.optimization_barrier(
             (others, fronts, far_pairs, posted)
         )
@@ -326,12 +351,8 @@
             (near, got, pair_weight, third_weight)
         )
         direct = [
-            piece(
-                pair_product(pair_weight, shift, half) + third_product(third_weight, shift, half),
-                bf16,
-            )
-            for shift in (1, 3)
-            for half in range(2)
+            piece(far_pairs[2 + k] + third_product(third_weight, (1, 3)[k // 2], k % 2), bf16)
+            for k in range(4)
         ]
         _, pair_weight, third_weight = lax.optimization_barrier(
             (direct, pair_weight, third_weight)
@@ -376,8 +397,9 @@
         upper_half, lower_half = jnp.concatenate(ring[:2]), jnp.concatenate(ring[2:])
         previous_upper = send(upper_half, along_first(1))
         following_lower = send(lower_half, along_first(-1))
-        previous_lower = send(lower_half, along_first(1))
-        following_upper = send(upper_half, along_first(-1))
+        upper_again, lower_again = together(upper_half, lower_half)
+        previous_lower = send(lower_again, along_first(1))
+        following_upper = send(upper_again, along_first(-1))
         low = send(previous_upper, along_first(1))
         high = send(following_lower, along_first(-1))
 
@@ -398,15 +420,13 @@
                 preferred_element_type=f32,
             )
 
-        upper_half, lower_half, previous_upper, following_lower = lax.optimization_barrier(
-            (upper_half, lower_half, previous_upper, following_lower)
-        )
         total = product([(0, 0), (0, 1)], [upper_half, lower_half])
         total = lax.optimization_barrier(
-            total + product([(3, 0), (1, 1)], [previous_upper, following_lower])
-        )
-        total = lax.optimization_barrier(
-            total + product([(3, 1), (1, 0)], [previous_lower, following_upper])
+            total
+            + product(
+                [(3, 0), (3, 1), (1, 0), (1, 1)],
+                [previous_upper, previous_lower, following_upper, following_lower],
+            )
         )
         total = total + product([(2, 0), (2, 1)], [low, high])
         new_weight = (flat_weight - step_rate * total).astype(bf16)

time: 181 us -> 178 us (0.983)
  waiting for transfers between devices: 32.7 us -> 26.3 us
  other arithmetic: 12.3 us -> 15.7 us
  starting transfers between devices: 67.1 us -> 64.1 us
    ppermute x37, waiting for transfers between devices: 32.7 us -> 26.3 us  [send(): return lax.ppermute(array, mesh_axes, pairs)]
    ppermute x37, starting transfers between devices: 67.1 us -> 64.1 us  [send(): return lax.ppermute(array, mesh_axes, pairs)]
    unnamed x40 -> x52, local copies, waits for them, and re-layouts: 2.98 us -> 4.48 us
    pallas_call x2 -> x3, Pallas kernels: 6.62 us -> 7.92 us  [the longest x2 5.89 us: rounded_layers(): pl.pallas_call(round_kernel, grid=(layers,), in_specs=[pl.BlockSpec(memor...]
    dot_general x4 -> x3, matrix products: 9.62 us -> 9.59 us  [product(): lax.dot_general(jnp.concatenate(inputs), jnp.concatenate(slopes), (((0,),...]
  transfers between devices with their start and end apart: 38 -> 38, of which waited for: 14 -> 17; matrix products, arithmetic and copies ran while one was open for 16% -> 18% of each run, Pallas kernels for 11% -> 12%
where the time goes in v2:
time: 178 us; the launch traced here: 177 us
  starting transfers between devices  64.1 us (36%)
  Pallas kernels  27 us (15%)
  waiting for transfers between devices  26.3 us (15%)
  matrix products  19.1 us (11%)
  other arithmetic  15.7 us (9%)
  between operations  14.9 us (8%)
  local copies, waits for them, and re-layouts  9.69 us (5%)
    ppermute x37, starting transfers between devices, send(): return lax.ppermute(array, mesh_axes, pairs)  64.1 us
    ppermute x37, waiting for transfers between devices, send(): return lax.ppermute(array, mesh_axes, pairs)  26.3 us
    pallas_call x3, Pallas kernels, down_pieces(): pl.pallas_call(down_kernel, grid_spec=pltpu.PrefetchScalarGridSpec(num_sc...  19 us
    dot_general x3, matrix products, product(): lax.dot_general(jnp.concatenate(inputs), jnp.concatenate(slopes), (((0,),...  9.59 us
    pallas_call x2, Pallas kernels, rounded_layers(): pl.pallas_call(round_kernel, grid=(layers,), in_specs=[pl.BlockSpec(memor...  5.89 us
    dot_general x8, matrix products, pair_product(): return jnp.dot(rows_of, weight, preferred_element_type=f32)  5.72 us
    unnamed x52, local copies, waits for them, and re-layouts  4.48 us
  transfers between devices with their start and end apart: 38, of which 17 were waited for; matrix products, arithmetic and copies ran while one was open for 18% of the time, Pallas kernels for 12%

profile of v2, /device:TPU:0, one launch (start us, length us, event | category | flops | bytes accessed | tf_op | source)
XLA Modules:
  0.0 176.8 jit_solution(5785345464605207476)
XLA Ops:
  7.8 5.3 %down_projection.3 = (bf16[2,256,512]{2,1,0:T(8,128)(2,1)}, bf16[2,256,512]{2,1,0:T(8,128)(2,1)}) custom-call(s32[4]{0:T(128)} %broadcast_select_fusion.17.blocks_ref, bf16[256,896]{1,0:T(8,128)(2,1)} %bitcast.121, bf16[896,8192]{1,0:T(8,128)(2,1)} %refs_1_.5, bf16[896,8192]{1,0:T(8,128)(2,1)} %refs_1_.5, s32[28,8192]{1,0:T(8,128)} %refs_3_.5, ...), custom_call_target="tpu_custom_call" | custom-call | flops 939524096 | bytes 5505024 | tf_op jit(solution)/shard_map/down/down_projection/pallas_call | solution.py:115
  15.2 4.2 %collective-permute-start.3 = (bf16[2,256,512]{2,1,0:T(8,128)(2,1)S(1)}, bf16[2,256,512]{2,1,0:T(8,128)(2,1)S(1)}, u32[]{:S(2)}, u32[]{:S(2)}) collective-permute-start(bf16[2,256,512]{2,1,0:T(8,128)(2,1)S(1)} %copy-done.19), channel_id=1, source_target_pairs={{0,12},{1,13},{2,14},{3,15},{4,0},{5,1},{6,2},{7,3},{8,4},{9,5},{1... | collective-permute-start | bytes 1572872 | tf_op jit(solution)/shard_map/reduce_down/ppermute | solution.py:57
  20.5 8.0 %down_projection.4 = (bf16[2,256,512]{2,1,0:T(8,128)(2,1)}, bf16[2,256,512]{2,1,0:T(8,128)(2,1)}, bf16[2,256,512]{2,1,0:T(8,128)(2,1)}, bf16[2,256,512]{2,1,0:T(8,128)(2,1)}) custom-call(s32[8]{0:T(128)} %pad_add_fusion.1.blocks_ref, bf16[256,896]{1,0:T(8,128)(2,1)} %bitcast.122, bf16[896,8192]{1,0:T(8,128)(2,1)} %refs_1_.5, bf16[896,8192]{1,0:T(8,128)(2,1)} %refs_1_.5, ...), custom_call_target="tpu_custom_call" | custom-call | flops 1879048192 | bytes 11010048 | tf_op jit(solution)/shard_map/down/down_projection/pallas_call | solution.py:115
  29.7 3.3 %collective-permute-start.4 = (bf16[2,256,512]{2,1,0:T(8,128)(2,1)S(1)}, bf16[2,256,512]{2,1,0:T(8,128)(2,1)S(1)}, u32[]{:S(2)}, u32[]{:S(2)}) collective-permute-start(bf16[2,256,512]{2,1,0:T(8,128)(2,1)S(1)} %add.415), channel_id=1, source_target_pairs={{0,12},{1,13},{2,14},{3,15},{4,0},{5,1},{6,2},{7,3},{8,4},{9,5},{1... | collective-permute-start | bytes 1572872 | tf_op jit(solution)/shard_map/reduce_down/ppermute | solution.py:57
  33.1 2.0 %collective-permute-start.2 = (bf16[2,256,512]{2,1,0:T(8,128)(2,1)}, bf16[2,256,512]{2,1,0:T(8,128)(2,1)S(1)}, u32[]{:S(2)}, u32[]{:S(2)}) collective-permute-start(bf16[2,256,512]{2,1,0:T(8,128)(2,1)} %get-tuple-element.47), channel_id=1, source_target_pairs={{0,12},{1,13},{2,14},{3,15},{4,0},{5,1},{6,2},{7,3},{8,4},{9,5},{1... | collective-permute-start | bytes 1572872 | tf_op jit(solution)/shard_map/reduce_down/ppermute | solution.py:57
  36.5 5.7 %down_projection.5 = (f32[2,256,512]{2,1,0:T(8,128)}, f32[2,256,512]{2,1,0:T(8,128)}) custom-call(s32[4]{0:T(128)} %get-tuple-element.43.blocks_ref, bf16[256,896]{1,0:T(8,128)(2,1)} %bitcast.123, bf16[896,8192]{1,0:T(8,128)(2,1)} %refs_1_.5, bf16[896,8192]{1,0:T(8,128)(2,1)} %refs_1_.5, s32[28,8192]{1,0:T(8,128)} %refs_3_.5, s32[28,8192]{1,0:T(8,128)} %refs_3_.5), custom_call_target="tpu_custom_call" | custom-call | flops 939524096 | bytes 5505024 | tf_op jit(solution)/shard_map/down/down_projection/pallas_call | solution.py:115
  43.7 1.8 %collective-permute-done.2 = bf16[2,256,512]{2,1,0:T(8,128)(2,1)S(1)} collective-permute-done((bf16[2,256,512]{2,1,0:T(8,128)(2,1)}, bf16[2,256,512]{2,1,0:T(8,128)(2,1)S(1)}, u32[]{:S(2)}, u32[]{:S(2)}) %collective-permute-start.2) | collective-permute-done | bytes 524320 | tf_op jit(solution)/shard_map/reduce_down/ppermute | solution.py:57
  52.3 2.0 %collective-permute-start.8 = (bf16[256,512]{1,0:T(8,128)(2,1)S(1)}, bf16[256,512]{1,0:T(8,128)(2,1)S(1)}, u32[]{:S(2)}, u32[]{:S(2)}) collective-permute-start(bf16[256,512]{1,0:T(8,128)(2,1)S(1)} %get-tuple-element.85), channel_id=1, source_target_pairs={{0,2},{1,3},{2,0},{3,1},{4,6},{5,7},{6,4},{7,5},{8,10},{9,11},{10,... | collective-permute-start | bytes 786440 | tf_op jit(solution)/shard_map/reduce_down/ppermute | solution.py:57
  54.9 2.6 %round_weight.3 = bf16[512,1024]{1,0:T(8,128)(2,1)} custom-call(f32[8,128]{1,0:T(8,128)} %slice_bitcast_fusion.2.after_ref, f32[1536,1024]{1,0:T(8,128)} %bitcast.100, f32[1536,1024]{1,0:T(8,128)} %bitcast.101), custom_call_target="tpu_custom_call" | custom-call | flops 524288 | bytes 3145728 | tf_op jit(solution)/shard_map/round_weight/pallas_call | solution.py:156
  57.5 3.2 %round_weight.2 = bf16[1024,1024]{1,0:T(8,128)(2,1)} custom-call(f32[8,128]{1,0:T(8,128)} %slice_bitcast_fusion.2.after_ref, f32[1536,1024]{1,0:T(8,128)} %bitcast.102, f32[1536,1024]{1,0:T(8,128)} %bitcast.103), custom_call_target="tpu_custom_call" | custom-call | flops 1048576 | bytes 6291456 | tf_op jit(solution)/shard_map/round_weight/pallas_call | solution.py:156
  62.7 3.1 %collective-permute-start.10 = (bf16[96,512]{1,0:T(8,128)(2,1)S(1)}, bf16[96,512]{1,0:T(8,128)(2,1)S(1)}, u32[]{:S(2)}, u32[]{:S(2)}) collective-permute-start(bf16[96,512]{1,0:T(8,128)(2,1)S(1)} %convolution_convert_fusion.2), channel_id=1, source_target_pairs={{0,64},{1,65},{2,66},{3,67},{4,68},{5,69},{6,70},{7,71},{8,72},{9,... | collective-permute-start | bytes 294920 | tf_op jit(solution)/shard_map/back/ppermute | solution.py:57
  66.4 2.6 %collective-permute-start.9 = (bf16[96,512]{1,0:T(8,128)(2,1)S(1)}, bf16[96,512]{1,0:T(8,128)(2,1)S(1)}, u32[]{:S(2)}, u32[]{:S(2)}) collective-permute-start(bf16[96,512]{1,0:T(8,128)(2,1)S(1)} %convolution_convert_fusion.2), channel_id=1, source_target_pairs={{0,96},{1,97},{2,98},{3,99},{4,100},{5,101},{6,102},{7,103},{8,104... | collective-permute-start | bytes 294920 | tf_op jit(solution)/shard_map/back/ppermute | solution.py:57
  82.5 1.9 %collective-permute-start.15 = (bf16[2,96,1024]{2,1,0:T(8,128)(2,1)S(1)}, bf16[2,96,1024]{2,1,0:T(8,128)(2,1)S(1)}, u32[]{:S(2)}, u32[]{:S(2)}) collective-permute-start(bf16[2,96,1024]{2,1,0:T(8,128)(2,1)S(1)} %bitcast.134), channel_id=1, source_target_pairs={{0,4},{1,5},{2,6},{3,7},{4,8},{5,9},{6,10},{7,11},{8,12},{9,13},{1... | collective-permute-start | bytes 1179656 | tf_op jit(solution)/shard_map/reduce_draft/ppermute | solution.py:57
  84.6 4.3 %collective-permute-start.18 = (bf16[2,96,1024]{2,1,0:T(8,128)(2,1)S(1)}, bf16[2,96,1024]{2,1,0:T(8,128)(2,1)S(1)}, u32[]{:S(2)}, u32[]{:S(2)}) collective-permute-start(bf16[2,96,1024]{2,1,0:T(8,128)(2,1)S(1)} %bitcast.131), channel_id=1, source_target_pairs={{0,12},{1,13},{2,14},{3,15},{4,0},{5,1},{6,2},{7,3},{8,4},{9,5},{1... | collective-permute-start | bytes 1179656 | tf_op jit(solution)/shard_map/reduce_draft/ppermute | solution.py:57
  90.6 2.1 %collective-permute-start.17 = (bf16[2,96,1024]{2,1,0:T(8,128)(2,1)S(1)}, bf16[2,96,1024]{2,1,0:T(8,128)(2,1)S(1)}, u32[]{:S(2)}, u32[]{:S(2)}) collective-permute-start(bf16[2,96,1024]{2,1,0:T(8,128)(2,1)S(1)} %bitcast.133), channel_id=1, source_target_pairs={{0,12},{1,13},{2,14},{3,15},{4,0},{5,1},{6,2},{7,3},{8,4},{9,5},{1... | collective-permute-start | bytes 1179656 | tf_op jit(solution)/shard_map/reduce_draft/ppermute | solution.py:57
  95.8 2.7 %collective-permute-start.19 = (bf16[2,96,1024]{2,1,0:T(8,128)(2,1)S(1)}, bf16[2,96,1024]{2,1,0:T(8,128)(2,1)S(1)}, u32[]{:S(2)}, u32[]{:S(2)}) collective-permute-start(bf16[2,96,1024]{2,1,0:T(8,128)(2,1)S(1)} %add.472), channel_id=1, source_target_pairs={{0,12},{1,13},{2,14},{3,15},{4,0},{5,1},{6,2},{7,3},{8,4},{9,5},{1... | collective-permute-start | bytes 1179656 | tf_op jit(solution)/shard_map/reduce_draft/ppermute | solution.py:57
  99.7 6.4 %collective-permute-done.16 = bf16[2,96,1024]{2,1,0:T(8,128)(2,1)S(1)} collective-permute-done((bf16[2,96,1024]{2,1,0:T(8,128)(2,1)S(1)}, bf16[2,96,1024]{2,1,0:T(8,128)(2,1)S(1)}, u32[]{:S(2)}, u32[]{:S(2)}) %collective-permute-start.16) | collective-permute-done | bytes 393248 | tf_op jit(solution)/shard_map/reduce_draft/ppermute | solution.py:57
  107.9 1.9 %collective-permute-start.22 = (bf16[96,1024]{1,0:T(8,128)(2,1)S(1)}, bf16[96,1024]{1,0:T(8,128)(2,1)S(1)}, u32[]{:S(2)}, u32[]{:S(2)}) collective-permute-start(bf16[96,1024]{1,0:T(8,128)(2,1)S(1)} %get-tuple-element.93), channel_id=1, source_target_pairs={{0,3},{1,0},{2,1},{3,2},{4,7},{5,4},{6,5},{7,6},{8,11},{9,8},{10,9... | collective-permute-start | bytes 589832 | tf_op jit(solution)/shard_map/reduce_draft/ppermute | solution.py:57
  111.3 2.2 %collective-permute-done.21 = bf16[96,1024]{1,0:T(8,128)(2,1)S(1)} collective-permute-done((bf16[96,1024]{1,0:T(8,128)(2,1)S(1)}, bf16[96,1024]{1,0:T(8,128)(2,1)S(1)}, u32[]{:S(2)}, u32[]{:S(2)}) %collective-permute-start.21) | collective-permute-done | bytes 196640 | tf_op jit(solution)/shard_map/reduce_draft/ppermute | solution.py:57
  113.6 3.5 %collective-permute-done.23 = bf16[96,1024]{1,0:T(8,128)(2,1)S(1)} collective-permute-done((bf16[96,1024]{1,0:T(8,128)(2,1)S(1)}, bf16[96,1024]{1,0:T(8,128)(2,1)S(1)}, u32[]{:S(2)}, u32[]{:S(2)}) %collective-permute-start.23) | collective-permute-done | bytes 196640 | tf_op jit(solution)/shard_map/reduce_draft/ppermute | solution.py:57
  119.6 2.7 %collective-permute-start.27 = (f32[3,96]{1,0:T(4,128)S(1)}, f32[3,96]{1,0:T(4,128)S(1)}, u32[]{:S(2)}, u32[]{:S(2)}) collective-permute-start(f32[3,96]{1,0:T(4,128)S(1)} %fusion.128), channel_id=1, source_target_pairs={{0,96},{1,97},{2,98},{3,99},{4,100},{5,101},{6,102},{7,103},{8,104... | collective-permute-start | bytes 3464 | tf_op jit(solution)/shard_map/norm/ppermute | solution.py:57
  124.9 7.2 %collective-permute-start.28 = (bf16[96,1024]{1,0:T(8,128)(2,1)S(1)}, bf16[96,1024]{1,0:T(8,128)(2,1)S(1)}, u32[]{:S(2)}, u32[]{:S(2)}) collective-permute-start(bf16[96,1024]{1,0:T(8,128)(2,1)S(1)} %fusion.57), channel_id=1, source_target_pairs={{0,3},{1,0},{2,1},{3,2},{4,7},{5,4},{6,5},{7,6},{8,11},{9,8},{10,9... | collective-permute-start | bytes 589832 | tf_op jit(solution)/shard_map/gather_slope/ppermute | solution.py:57
  133.5 2.4 %slice.67 = bf16[8,192,1024]{2,1,0:T(8,128)(2,1)S(1)} slice(bf16[8,240,1024]{2,1,0:T(8,128)(2,1)} %bitcast.120), slice={[0:8], [0:192], [0:1024]} | slice | bytes 6291456 | tf_op jit(solution)/shard_map/forward/slice | solution.py:313
  137.4 2.1 %collective-permute-done.29 = bf16[96,1024]{1,0:T(8,128)(2,1)} collective-permute-done((bf16[96,1024]{1,0:T(8,128)(2,1)S(1)}, bf16[96,1024]{1,0:T(8,128)(2,1)}, u32[]{:S(2)}, u32[]{:S(2)}) %collective-permute-start.29) | collective-permute-done | bytes 196640 | tf_op jit(solution)/shard_map/gather_slope/ppermute | solution.py:57
  139.4 1.8 %collective-permute-done.30 = bf16[96,1024]{1,0:T(8,128)(2,1)} collective-permute-done((bf16[96,1024]{1,0:T(8,128)(2,1)S(1)}, bf16[96,1024]{1,0:T(8,128)(2,1)}, u32[]{:S(2)}, u32[]{:S(2)}) %collective-permute-start.30) | collective-permute-done | bytes 196640 | tf_op jit(solution)/shard_map/gather_slope/ppermute | solution.py:57
  144.3 2.0 %together.1 = (bf16[192,1024]{1,0:T(8,128)(2,1)}, bf16[192,1024]{1,0:T(8,128)(2,1)}) custom-call(bf16[192,1024]{1,0:T(8,128)(2,1)} %pad_maximum_fusion.6.first_ref, bf16[192,1024]{1,0:T(8,128)(2,1)} %pad_maximum_fusion.7.second_ref), custom_call_target="tpu_custom_call" | custom-call | tf_op jit(solution)/shard_map/gather_slope/together/pallas_call | solution.py:178
  146.3 3.2 %collective-permute-start.34 = (bf16[192,1024]{1,0:T(8,128)(2,1)}, bf16[192,1024]{1,0:T(8,128)(2,1)S(1)}, u32[]{:S(2)}, u32[]{:S(2)}) collective-permute-start(bf16[192,1024]{1,0:T(8,128)(2,1)} %pad_maximum_fusion.7.second_ref), channel_id=1, source_target_pairs={{0,12},{1,13},{2,14},{3,15},{4,0},{5,1},{6,2},{7,3},{8,4},{9,5},{1... | collective-permute-start | bytes 1179656 | tf_op jit(solution)/shard_map/gather_slope/ppermute | solution.py:57
  149.5 3.2 %collective-permute-start.33 = (bf16[192,1024]{1,0:T(8,128)(2,1)}, bf16[192,1024]{1,0:T(8,128)(2,1)S(1)}, u32[]{:S(2)}, u32[]{:S(2)}) collective-permute-start(bf16[192,1024]{1,0:T(8,128)(2,1)} %get-tuple-element.67), channel_id=1, source_target_pairs={{0,12},{1,13},{2,14},{3,15},{4,0},{5,1},{6,2},{7,3},{8,4},{9,5},{1... | collective-permute-start | bytes 1179656 | tf_op jit(solution)/shard_map/gather_slope/ppermute | solution.py:57
  155.1 3.6 %collective-permute-start.36 = (bf16[192,1024]{1,0:T(8,128)(2,1)S(1)}, bf16[192,1024]{1,0:T(8,128)(2,1)S(1)}, u32[]{:S(2)}, u32[]{:S(2)}) collective-permute-start(bf16[192,1024]{1,0:T(8,128)(2,1)S(1)} %collective-permute-done.34), channel_id=1, source_target_pairs={{0,12},{1,13},{2,14},{3,15},{4,0},{5,1},{6,2},{7,3},{8,4},{9,5},{1... | collective-permute-start | bytes 1179656 | tf_op jit(solution)/shard_map/gather_slope/ppermute | solution.py:57
  159.3 3.7 %fusion = f32[1536,1024]{1,0:T(8,128)S(1)} fusion(bf16[192,1536]{1,0:T(8,128)(2,1)S(1)} %get-tuple-element.81, bf16[192,1536]{1,0:T(8,128)(2,1)S(1)} %get-tuple-element.79, bf16[192,1536]{1,0:T(8,128)(2,1)S(1)} %get-tuple-element.78, bf16[192,1536]{1,0:T(8,128)(2,1)S(1)} %get-tuple-element.77, bf16[192,1024]{1,0:T(8,128)(2,1)S(1)} %collective-permute-done.34, ...), kind=kOutput, calls=%fused_computation.21 | convolution fusion | flops 2431647744 | bytes 10223616 | tf_op jit(solution)/shard_map/step/dot_general | solution.py:416
  163.1 1.9 %convolution_add_fusion = f32[1536,1024]{1,0:T(8,128)S(1)} fusion(f32[1536,1024]{1,0:T(8,128)S(1)} %fusion, bf16[192,1536]{1,0:T(8,128)(2,1)S(1)} %get-tuple-element.76, bf16[192,1536]{1,0:T(8,128)(2,1)S(1)} %get-tuple-element.75, bf16[96,1024]{1,0:T(8,128)(2,1)S(1)} %copy-done.8, bf16[96,1024]{1,0:T(8,128)(2,1)S(1)} %copy-done.6, ...), kind=kOutput, calls=%fused_computation.17 | convolution fusion | flops 1215037440 | bytes 14548992 | tf_op jit(solution)/shard_map/step/dot_general | solution.py:416
  166.0 4.0 %subtract_convert_fusion = bf16[1536,1024]{1,0:T(8,128)(2,1)} fusion(f32[1536,1024]{1,0:T(8,128)S(1)} %bitcast.106, f32[1536,1024]{1,0:T(8,128)S(1)} %convolution_add_fusion, bf16[192,1536]{1,0:T(8,128)(2,1)S(1)} %get-tuple-element.80, bf16[192,1536]{1,0:T(8,128)(2,1)S(1)} %get-tuple-element.74, bf16[192,1024]{1,0:T(8,128)(2,1)S(1)} %collective-permute-done.36, ...), kind=kOutput, calls=%fused_computation.16 | convolution fusion | flops 1218183168 | bytes 17694720 | tf_op jit(solution)/shard_map/step/dot_general | solution.py:416
  (183 shorter events, 55.1 us)
Async XLA Ops:
  7.2 66.8 %all-gather.2.cloned.1.call-start = ((), (), s32[]{:S(2)}) async-start(), calls=%async_computation | async-start | bytes 4423680 | tf_op jit(solution)/shard_map/all_gather | solution.py:270
  15.2 13.4 %collective-permute-start.3 = (bf16[2,256,512]{2,1,0:T(8,128)(2,1)S(1)}, bf16[2,256,512]{2,1,0:T(8,128)(2,1)S(1)}, u32[]{:S(2)}, u32[]{:S(2)}) collective-permute-start(bf16[2,256,512]{2,1,0:T(8,128)(2,1)S(1)} %copy-done.19), channel_id=1, source_target_pairs={{0,12},{1,13},{2,14},{3,15},{4,0},{5,1},{6,2},{7,3},{8,4},{9,5},{1... | collective-permute-start | bytes 1572872 | tf_op jit(solution)/shard_map/reduce_down/ppermute | solution.py:57
  19.4 15.7 %collective-permute-start = (bf16[2,256,512]{2,1,0:T(8,128)(2,1)}, bf16[2,256,512]{2,1,0:T(8,128)(2,1)S(1)}, u32[]{:S(2)}, u32[]{:S(2)}) collective-permute-start(bf16[2,256,512]{2,1,0:T(8,128)(2,1)} %get-tuple-element.46), channel_id=1, source_target_pairs={{0,4},{1,5},{2,6},{3,7},{4,8},{5,9},{6,10},{7,11},{8,12},{9,13},{1... | collective-permute-start | bytes 1572872 | tf_op jit(solution)/shard_map/reduce_down/ppermute | solution.py:57
  28.6 13.6 %collective-permute-start.5 = (bf16[2,256,512]{2,1,0:T(8,128)(2,1)}, bf16[2,256,512]{2,1,0:T(8,128)(2,1)S(1)}, u32[]{:S(2)}, u32[]{:S(2)}) collective-permute-start(bf16[2,256,512]{2,1,0:T(8,128)(2,1)} %get-tuple-element.51), channel_id=1, source_target_pairs={{0,4},{1,5},{2,6},{3,7},{4,8},{5,9},{6,10},{7,11},{8,12},{9,13},{1... | collective-permute-start | bytes 1572872 | tf_op jit(solution)/shard_map/reduce_down/ppermute | solution.py:57
  29.7 12.4 %collective-permute-start.4 = (bf16[2,256,512]{2,1,0:T(8,128)(2,1)S(1)}, bf16[2,256,512]{2,1,0:T(8,128)(2,1)S(1)}, u32[]{:S(2)}, u32[]{:S(2)}) collective-permute-start(bf16[2,256,512]{2,1,0:T(8,128)(2,1)S(1)} %add.415), channel_id=1, source_target_pairs={{0,12},{1,13},{2,14},{3,15},{4,0},{5,1},{6,2},{7,3},{8,4},{9,5},{1... | collective-permute-start | bytes 1572872 | tf_op jit(solution)/shard_map/reduce_down/ppermute | solution.py:57
  33.1 12.4 %collective-permute-start.2 = (bf16[2,256,512]{2,1,0:T(8,128)(2,1)}, bf16[2,256,512]{2,1,0:T(8,128)(2,1)S(1)}, u32[]{:S(2)}, u32[]{:S(2)}) collective-permute-start(bf16[2,256,512]{2,1,0:T(8,128)(2,1)} %get-tuple-element.47), channel_id=1, source_target_pairs={{0,12},{1,13},{2,14},{3,15},{4,0},{5,1},{6,2},{7,3},{8,4},{9,5},{1... | collective-permute-start | bytes 1572872 | tf_op jit(solution)/shard_map/reduce_down/ppermute | solution.py:57
  36.3 10.6 %collective-permute-start.1 = (bf16[2,256,512]{2,1,0:T(8,128)(2,1)S(1)}, bf16[2,256,512]{2,1,0:T(8,128)(2,1)}, u32[]{:S(2)}, u32[]{:S(2)}) collective-permute-start(bf16[2,256,512]{2,1,0:T(8,128)(2,1)S(1)} %add.412), channel_id=1, source_target_pairs={{0,4},{1,5},{2,6},{3,7},{4,8},{5,9},{6,10},{7,11},{8,12},{9,13},{1... | collective-permute-start | bytes 1572872 | tf_op jit(solution)/shard_map/reduce_down/ppermute | solution.py:57
  49.0 11.7 %collective-permute-start.6 = (bf16[256,512]{1,0:T(8,128)(2,1)}, bf16[256,512]{1,0:T(8,128)(2,1)S(1)}, u32[]{:S(2)}, u32[]{:S(2)}) collective-permute-start(bf16[256,512]{1,0:T(8,128)(2,1)} %get-tuple-element.84), channel_id=1, source_target_pairs={{0,1},{1,2},{2,3},{3,0},{4,5},{5,6},{6,7},{7,4},{8,9},{9,10},{10,1... | collective-permute-start | bytes 786440 | tf_op jit(solution)/shard_map/reduce_down/ppermute | solution.py:57
  50.6 10.2 %collective-permute-start.7 = (bf16[256,512]{1,0:T(8,128)(2,1)S(1)}, bf16[256,512]{1,0:T(8,128)(2,1)S(1)}, u32[]{:S(2)}, u32[]{:S(2)}) collective-permute-start(bf16[256,512]{1,0:T(8,128)(2,1)S(1)} %get-tuple-element.86), channel_id=1, source_target_pairs={{0,3},{1,0},{2,1},{3,2},{4,7},{5,4},{6,5},{7,6},{8,11},{9,8},{10,9... | collective-permute-start | bytes 786440 | tf_op jit(solution)/shard_map/reduce_down/ppermute | solution.py:57
  52.3 8.6 %collective-permute-start.8 = (bf16[256,512]{1,0:T(8,128)(2,1)S(1)}, bf16[256,512]{1,0:T(8,128)(2,1)S(1)}, u32[]{:S(2)}, u32[]{:S(2)}) collective-permute-start(bf16[256,512]{1,0:T(8,128)(2,1)S(1)} %get-tuple-element.85), channel_id=1, source_target_pairs={{0,2},{1,3},{2,0},{3,1},{4,6},{5,7},{6,4},{7,5},{8,10},{9,11},{10,... | collective-permute-start | bytes 786440 | tf_op jit(solution)/shard_map/reduce_down/ppermute | solution.py:57
  62.7 9.5 %collective-permute-start.10 = (bf16[96,512]{1,0:T(8,128)(2,1)S(1)}, bf16[96,512]{1,0:T(8,128)(2,1)S(1)}, u32[]{:S(2)}, u32[]{:S(2)}) collective-permute-start(bf16[96,512]{1,0:T(8,128)(2,1)S(1)} %convolution_convert_fusion.2), channel_id=1, source_target_pairs={{0,64},{1,65},{2,66},{3,67},{4,68},{5,69},{6,70},{7,71},{8,72},{9,... | collective-permute-start | bytes 294920 | tf_op jit(solution)/shard_map/back/ppermute | solution.py:57
  65.8 6.4 %collective-permute-start.11 = (bf16[96,512]{1,0:T(8,128)(2,1)S(1)}, bf16[96,512]{1,0:T(8,128)(2,1)S(1)}, u32[]{:S(2)}, u32[]{:S(2)}) collective-permute-start(bf16[96,512]{1,0:T(8,128)(2,1)S(1)} %convolution_convert_fusion.2), channel_id=1, source_target_pairs={{0,32},{1,33},{2,34},{3,35},{4,36},{5,37},{6,38},{7,39},{8,40},{9,... | collective-permute-start | bytes 294920 | tf_op jit(solution)/shard_map/back/ppermute | solution.py:57
  69.9 19.0 %collective-permute-start.13 = (bf16[96,512]{1,0:T(8,128)(2,1)}, bf16[96,512]{1,0:T(8,128)(2,1)S(1)}, u32[]{:S(2)}, u32[]{:S(2)}) collective-permute-start(bf16[96,512]{1,0:T(8,128)(2,1)} %get-tuple-element.105), channel_id=1, source_target_pairs={{0,0},{1,1},{2,16},{3,20},{4,32},{5,33},{6,48},{7,52},{8,64},{9,65... | collective-permute-start | bytes 294920 | tf_op jit(solution)/shard_map/targets/ppermute | solution.py:57
  71.5 17.4 %collective-permute-start.14 = (bf16[96,512]{1,0:T(8,128)(2,1)}, bf16[96,512]{1,0:T(8,128)(2,1)S(1)}, u32[]{:S(2)}, u32[]{:S(2)}) collective-permute-start(bf16[96,512]{1,0:T(8,128)(2,1)} %get-tuple-element.104), channel_id=1, source_target_pairs={{0,1},{1,0},{2,20},{3,16},{4,33},{5,32},{6,52},{7,48},{8,65},{9,64... | collective-permute-start | bytes 294920 | tf_op jit(solution)/shard_map/targets/ppermute | solution.py:57
  72.3 7.7 %collective-permute-start.12 = (bf16[4,96,512]{2,1,0:T(8,128)(2,1)S(1)}, bf16[4,96,512]{2,1,0:T(8,128)(2,1)S(1)}, u32[]{:S(2)}, u32[]{:S(2)}) collective-permute-start(bf16[4,96,512]{2,1,0:T(8,128)(2,1)S(1)} %pad_maximum_fusion.5), channel_id=1, source_target_pairs={{0,16},{1,17},{2,18},{3,19},{4,20},{5,21},{6,22},{7,23},{8,24},{9,... | collective-permute-start | bytes 1179656 | tf_op jit(solution)/shard_map/back/ppermute | solution.py:57
  82.5 11.9 %collective-permute-start.15 = (bf16[2,96,1024]{2,1,0:T(8,128)(2,1)S(1)}, bf16[2,96,1024]{2,1,0:T(8,128)(2,1)S(1)}, u32[]{:S(2)}, u32[]{:S(2)}) collective-permute-start(bf16[2,96,1024]{2,1,0:T(8,128)(2,1)S(1)} %bitcast.134), channel_id=1, source_target_pairs={{0,4},{1,5},{2,6},{3,7},{4,8},{5,9},{6,10},{7,11},{8,12},{9,13},{1... | collective-permute-start | bytes 1179656 | tf_op jit(solution)/shard_map/reduce_draft/ppermute | solution.py:57
  84.6 11.1 %collective-permute-start.18 = (bf16[2,96,1024]{2,1,0:T(8,128)(2,1)S(1)}, bf16[2,96,1024]{2,1,0:T(8,128)(2,1)S(1)}, u32[]{:S(2)}, u32[]{:S(2)}) collective-permute-start(bf16[2,96,1024]{2,1,0:T(8,128)(2,1)S(1)} %bitcast.131), channel_id=1, source_target_pairs={{0,12},{1,13},{2,14},{3,15},{4,0},{5,1},{6,2},{7,3},{8,4},{9,5},{1... | collective-permute-start | bytes 1179656 | tf_op jit(solution)/shard_map/reduce_draft/ppermute | solution.py:57
  90.6 9.1 %collective-permute-start.17 = (bf16[2,96,1024]{2,1,0:T(8,128)(2,1)S(1)}, bf16[2,96,1024]{2,1,0:T(8,128)(2,1)S(1)}, u32[]{:S(2)}, u32[]{:S(2)}) collective-permute-start(bf16[2,96,1024]{2,1,0:T(8,128)(2,1)S(1)} %bitcast.133), channel_id=1, source_target_pairs={{0,12},{1,13},{2,14},{3,15},{4,0},{5,1},{6,2},{7,3},{8,4},{9,5},{1... | collective-permute-start | bytes 1179656 | tf_op jit(solution)/shard_map/reduce_draft/ppermute | solution.py:57
  92.8 13.4 %collective-permute-start.20 = (bf16[2,96,1024]{2,1,0:T(8,128)(2,1)S(1)}, bf16[2,96,1024]{2,1,0:T(8,128)(2,1)S(1)}, u32[]{:S(2)}, u32[]{:S(2)}) collective-permute-start(bf16[2,96,1024]{2,1,0:T(8,128)(2,1)S(1)} %bitcast.132), channel_id=1, source_target_pairs={{0,4},{1,5},{2,6},{3,7},{4,8},{5,9},{6,10},{7,11},{8,12},{9,13},{1... | collective-permute-start | bytes 1179656 | tf_op jit(solution)/shard_map/reduce_draft/ppermute | solution.py:57
  94.6 11.4 %collective-permute-start.16 = (bf16[2,96,1024]{2,1,0:T(8,128)(2,1)S(1)}, bf16[2,96,1024]{2,1,0:T(8,128)(2,1)S(1)}, u32[]{:S(2)}, u32[]{:S(2)}) collective-permute-start(bf16[2,96,1024]{2,1,0:T(8,128)(2,1)S(1)} %add.467), channel_id=1, source_target_pairs={{0,4},{1,5},{2,6},{3,7},{4,8},{5,9},{6,10},{7,11},{8,12},{9,13},{1... | collective-permute-start | bytes 1179656 | tf_op jit(solution)/shard_map/reduce_draft/ppermute | solution.py:57
  95.8 10.4 %collective-permute-start.19 = (bf16[2,96,1024]{2,1,0:T(8,128)(2,1)S(1)}, bf16[2,96,1024]{2,1,0:T(8,128)(2,1)S(1)}, u32[]{:S(2)}, u32[]{:S(2)}) collective-permute-start(bf16[2,96,1024]{2,1,0:T(8,128)(2,1)S(1)} %add.472), channel_id=1, source_target_pairs={{0,12},{1,13},{2,14},{3,15},{4,0},{5,1},{6,2},{7,3},{8,4},{9,5},{1... | collective-permute-start | bytes 1179656 | tf_op jit(solution)/shard_map/reduce_draft/ppermute | solution.py:57
  106.5 6.9 %collective-permute-start.21 = (bf16[96,1024]{1,0:T(8,128)(2,1)S(1)}, bf16[96,1024]{1,0:T(8,128)(2,1)S(1)}, u32[]{:S(2)}, u32[]{:S(2)}) collective-permute-start(bf16[96,1024]{1,0:T(8,128)(2,1)S(1)} %get-tuple-element.91), channel_id=1, source_target_pairs={{0,1},{1,2},{2,3},{3,0},{4,5},{5,6},{6,7},{7,4},{8,9},{9,10},{10,1... | collective-permute-start | bytes 589832 | tf_op jit(solution)/shard_map/reduce_draft/ppermute | solution.py:57
  109.9 7.2 %collective-permute-start.23 = (bf16[96,1024]{1,0:T(8,128)(2,1)S(1)}, bf16[96,1024]{1,0:T(8,128)(2,1)S(1)}, u32[]{:S(2)}, u32[]{:S(2)}) collective-permute-start(bf16[96,1024]{1,0:T(8,128)(2,1)S(1)} %get-tuple-element.92), channel_id=1, source_target_pairs={{0,2},{1,3},{2,0},{3,1},{4,6},{5,7},{6,4},{7,5},{8,10},{9,11},{10,... | collective-permute-start | bytes 589832 | tf_op jit(solution)/shard_map/reduce_draft/ppermute | solution.py:57
  124.9 12.5 %collective-permute-start.28 = (bf16[96,1024]{1,0:T(8,128)(2,1)S(1)}, bf16[96,1024]{1,0:T(8,128)(2,1)S(1)}, u32[]{:S(2)}, u32[]{:S(2)}) collective-permute-start(bf16[96,1024]{1,0:T(8,128)(2,1)S(1)} %fusion.57), channel_id=1, source_target_pairs={{0,3},{1,0},{2,1},{3,2},{4,7},{5,4},{6,5},{7,6},{8,11},{9,8},{10,9... | collective-permute-start | bytes 589832 | tf_op jit(solution)/shard_map/gather_slope/ppermute | solution.py:57
  132.0 7.4 %collective-permute-start.29 = (bf16[96,1024]{1,0:T(8,128)(2,1)S(1)}, bf16[96,1024]{1,0:T(8,128)(2,1)}, u32[]{:S(2)}, u32[]{:S(2)}) collective-permute-start(bf16[96,1024]{1,0:T(8,128)(2,1)S(1)} %fusion.57), channel_id=1, source_target_pairs={{0,2},{1,3},{2,0},{3,1},{4,6},{5,7},{6,4},{7,5},{8,10},{9,11},{10,... | collective-permute-start | bytes 589832 | tf_op jit(solution)/shard_map/gather_slope/ppermute | solution.py:57
  132.2 9.1 %collective-permute-start.30 = (bf16[96,1024]{1,0:T(8,128)(2,1)S(1)}, bf16[96,1024]{1,0:T(8,128)(2,1)}, u32[]{:S(2)}, u32[]{:S(2)}) collective-permute-start(bf16[96,1024]{1,0:T(8,128)(2,1)S(1)} %fusion.57), channel_id=1, source_target_pairs={{0,1},{1,2},{2,3},{3,0},{4,5},{5,6},{6,7},{7,4},{8,9},{9,10},{10,1... | collective-permute-start | bytes 589832 | tf_op jit(solution)/shard_map/gather_slope/ppermute | solution.py:57
  143.4 11.2 %collective-permute-start.31 = (bf16[192,1024]{1,0:T(8,128)(2,1)}, bf16[192,1024]{1,0:T(8,128)(2,1)}, u32[]{:S(2)}, u32[]{:S(2)}) collective-permute-start(bf16[192,1024]{1,0:T(8,128)(2,1)} %pad_maximum_fusion.6.first_ref), channel_id=1, source_target_pairs={{0,4},{1,5},{2,6},{3,7},{4,8},{5,9},{6,10},{7,11},{8,12},{9,13},{1... | collective-permute-start | bytes 1179656 | tf_op jit(solution)/shard_map/gather_slope/ppermute | solution.py:57
  146.3 8.8 %collective-permute-start.34 = (bf16[192,1024]{1,0:T(8,128)(2,1)}, bf16[192,1024]{1,0:T(8,128)(2,1)S(1)}, u32[]{:S(2)}, u32[]{:S(2)}) collective-permute-start(bf16[192,1024]{1,0:T(8,128)(2,1)} %pad_maximum_fusion.7.second_ref), channel_id=1, source_target_pairs={{0,12},{1,13},{2,14},{3,15},{4,0},{5,1},{6,2},{7,3},{8,4},{9,5},{1... | collective-permute-start | bytes 1179656 | tf_op jit(solution)/shard_map/gather_slope/ppermute | solution.py:57
  149.5 9.2 %collective-permute-start.32 = (bf16[192,1024]{1,0:T(8,128)(2,1)}, bf16[192,1024]{1,0:T(8,128)(2,1)S(1)}, u32[]{:S(2)}, u32[]{:S(2)}) collective-permute-start(bf16[192,1024]{1,0:T(8,128)(2,1)} %get-tuple-element.66), channel_id=1, source_target_pairs={{0,4},{1,5},{2,6},{3,7},{4,8},{5,9},{6,10},{7,11},{8,12},{9,13},{1... | collective-permute-start | bytes 1179656 | tf_op jit(solution)/shard_map/gather_slope/ppermute | solution.py:57
  149.5 9.8 %collective-permute-start.33 = (bf16[192,1024]{1,0:T(8,128)(2,1)}, bf16[192,1024]{1,0:T(8,128)(2,1)S(1)}, u32[]{:S(2)}, u32[]{:S(2)}) collective-permute-start(bf16[192,1024]{1,0:T(8,128)(2,1)} %get-tuple-element.67), channel_id=1, source_target_pairs={{0,12},{1,13},{2,14},{3,15},{4,0},{5,1},{6,2},{7,3},{8,4},{9,5},{1... | collective-permute-start | bytes 1179656 | tf_op jit(solution)/shard_map/gather_slope/ppermute | solution.py:57
  154.6 10.4 %collective-permute-start.35 = (bf16[192,1024]{1,0:T(8,128)(2,1)}, bf16[192,1024]{1,0:T(8,128)(2,1)S(1)}, u32[]{:S(2)}, u32[]{:S(2)}) collective-permute-start(bf16[192,1024]{1,0:T(8,128)(2,1)} %collective-permute-done.31), channel_id=1, source_target_pairs={{0,4},{1,5},{2,6},{3,7},{4,8},{5,9},{6,10},{7,11},{8,12},{9,13},{1... | collective-permute-start | bytes 1179656 | tf_op jit(solution)/shard_map/gather_slope/ppermute | solution.py:57
  155.1 9.9 %collective-permute-start.36 = (bf16[192,1024]{1,0:T(8,128)(2,1)S(1)}, bf16[192,1024]{1,0:T(8,128)(2,1)S(1)}, u32[]{:S(2)}, u32[]{:S(2)}) collective-permute-start(bf16[192,1024]{1,0:T(8,128)(2,1)S(1)} %collective-permute-done.34), channel_id=1, source_target_pairs={{0,12},{1,13},{2,14},{3,15},{4,0},{5,1},{6,2},{7,3},{8,4},{9,5},{1... | collective-permute-start | bytes 1179656 | tf_op jit(solution)/shard_map/gather_slope/ppermute | solution.py:57
  (32 other events, 149.4 us)
Sparse Core Ops, SparseCore 0:
  15.3 33.5 all-gather.1

commit v3 on v2

--- a/solution.py
+++ b/solution.py
@@ -146,12 +146,13 @@
     out_ref[half:] = lower_ref[...].astype(bf16)
 
 
-def rounded_layers(wide, layers, start, after):
+def rounded(wide, after):
     rows, columns = wide.shape
-    step = rows // 3
+    layers = 3
+    step = rows // layers
 
     def half_layer(half):
-        return pl.BlockSpec((step // 2, columns), lambda i: (2 * (start + i) + half, 0))
+        return pl.BlockSpec((step // 2, columns), lambda i: (2 * i + half, 0))
 
     return pl.pallas_call(
         round_kernel,
@@ -169,6 +170,20 @@
     )(after, wide, wide)
 
 
+def held_kernel(after_ref, value_ref, out_ref):
+    out_ref[...] = value_ref[...]
+
+
+def held(value, after):
+    return pl.pallas_call(
+        held_kernel,
+        in_specs=[pl.BlockSpec(memory_space=pl.ANY), pl.BlockSpec(memory_space=pltpu.VMEM)],
+        out_specs=pl.BlockSpec(memory_space=pltpu.VMEM),
+        out_shape=jax.ShapeDtypeStruct((8, 128), jnp.int32),
+        name="held",
+    )(after, jnp.full((8, 128), value, jnp.int32))[0, 0]
+
+
 def together_kernel(first_ref, second_ref, first_out_ref, second_out_ref):
     first_out_ref[...] = first_ref[...]
     second_out_ref[...] = second_ref[...]
@@ -184,7 +199,7 @@
     )(first, second)
 
 
-def reduce_blocks(near, direct, own, q):
+def reduce_blocks(near, direct, own, q, after=None):
     low_right = send(near[0], along_first(1))
     high_left = send(near[1], along_first(-1))
     high_right = send(direct[1], along_first(1))
@@ -197,11 +212,11 @@
     )
     halved = summed.astype(bf16)
 
-    def at(array, shift):
-        return lax.dynamic_index_in_dim(array, (q + shift) % side, 0, keepdims=False)
-
-    parts = [send(at(halved, shift), along_second(shift)) for shift in (1, 3, 2)]
-    return plus(at(summed, 0), *parts), summed[0, :8, :128]
+    def at(array, index):
+        return lax.dynamic_index_in_dim(array, index % side, 0, keepdims=False)
+
+    parts = [send(at(halved, q + shift), along_second(shift)) for shift in (1, 3, 2)]
+    return plus(at(summed, q if after is None else held(q, after)), *parts)
 
 
 def body(
@@ -276,12 +291,15 @@
         direct = down_pieces(others, tokens, coded_weight, block_exponent, bf16)
         direct, mine = lax.optimization_barrier((direct, columns(0)))
         own = down_pieces(mine, tokens, coded_weight, block_exponent, f32)
+    flat_weight = draft_input_weight.reshape(3 * feature_slice, out_slice)
+    narrow_weight = rounded(flat_weight, own[0])
+    third_weight = narrow_weight[2 * feature_slice :]
+    with jax.named_scope("early"):
+        early = jnp.dot(
+            gathered, narrow_weight[: 2 * feature_slice], preferred_element_type=f32
+        )
     with jax.named_scope("reduce_down"):
-        mixed, first_sum = reduce_blocks(near, direct, own, q)
-
-    flat_weight = draft_input_weight.reshape(3 * feature_slice, out_slice)
-    pair_weight = rounded_layers(flat_weight, 2, 0, first_sum)
-    third_weight = rounded_layers(flat_weight, 1, 2, first_sum)
+        mixed = reduce_blocks(near, direct, own, q, early[:8, :128])
     upper_layer = (
         stream_input.astype(f32) + mixed.reshape(steps, rows, feature_slice)
     ).astype(bf16)
@@ -318,11 +336,10 @@
         def replica_of(shift, half):
             return 2 * ((p + shift) % side) + half
 
-        def pair_product(weight, shift, half):
-            rows_of = lax.dynamic_slice_in_dim(
-                gathered, replica_of(shift, half) * stride, 2 * slots, axis=0
+        def pair_product(shift, half):
+            return lax.dynamic_slice_in_dim(
+                early, replica_of(shift, half) * stride, 2 * slots, axis=0
             )
-            return jnp.dot(rows_of, weight, preferred_element_type=f32)
 
         def third_product(weight, shift, half):
             rows_of = lax.dynamic_slice_in_dim(
@@ -333,39 +350,29 @@
         def piece(total, kind):
             return total.astype(kind).reshape(2, slots, out_slice)
 
-        far_pairs = [
-            pair_product(pair_weight, shift, half) for shift in (2, 1, 3) for half in range(2)
-        ]
-        others, fronts, far_pairs, _ = lax.optimization_barrier(
-            (others, fronts, far_pairs, posted)
-        )
+        others, fronts, _ = lax.optimization_barrier((others, fronts, posted))
         backs = jnp.stack(
             [jnp.where(c == 0, chips, others), jnp.where(c == 0, others, chips)], axis=1
         ).reshape(replicas, slots, feature_slice)
         thirds = jnp.concatenate([fronts, backs], axis=1).reshape(-1, feature_slice)
         near = [
-            piece(far_pairs[half] + third_product(third_weight, 2, half), bf16)
+            piece(pair_product(2, half) + third_product(third_weight, 2, half), bf16)
             for half in range(2)
         ]
-        _, got, pair_weight, third_weight = lax.optimization_barrier(
-            (near, got, pair_weight, third_weight)
-        )
+        _, got, third_weight = lax.optimization_barrier((near, got, third_weight))
         direct = [
-            piece(far_pairs[2 + k] + third_product(third_weight, (1, 3)[k // 2], k % 2), bf16)
-            for k in range(4)
-        ]
-        _, pair_weight, third_weight = lax.optimization_barrier(
-            (direct, pair_weight, third_weight)
-        )
-        own = [
-            piece(
-                pair_product(pair_weight, 0, half) + third_product(third_weight, 0, half), f32
-            )
+            piece(pair_product(shift, half) + third_product(third_weight, shift, half), bf16)
+            for shift in (1, 3)
             for half in range(2)
         ]
+        _, third_weight = lax.optimization_barrier((direct, third_weight))
+        own = [
+            piece(pair_product(0, half) + third_product(third_weight, 0, half), f32)
+            for half in range(2)
+        ]
 
     with jax.named_scope("reduce_draft"):
-        drafted, _ = reduce_blocks(near, direct, own, q)
+        drafted = reduce_blocks(near, direct, own, q)
 
     with jax.named_scope("norm"):
         front_rows = q % 2 == 0
@@ -420,17 +427,19 @@
                 preferred_element_type=f32,
             )
 
-        total = product([(0, 0), (0, 1)], [upper_half, lower_half])
-        total = lax.optimization_barrier(
-            total
-            + product(
+        updated = lax.optimization_barrier(
+            flat_weight - step_rate * product([(0, 0), (0, 1)], [upper_half, lower_half])
+        )
+        updated = lax.optimization_barrier(
+            updated
+            - step_rate
+            * product(
                 [(3, 0), (3, 1), (1, 0), (1, 1)],
                 [previous_upper, previous_lower, following_upper, following_lower],
             )
         )
-        total = total + product([(2, 0), (2, 1)], [low, high])
-        new_weight = (flat_weight - step_rate * total).astype(bf16)
-        new_weight = new_weight.reshape(draft_input_weight.shape)
+        updated = updated - step_rate * product([(2, 0), (2, 1)], [low, high])
+        new_weight = updated.astype(bf16).reshape(draft_input_weight.shape)
     return (upper_layer, new_weight)
 
 

time: 178 us -> 189 us (1.062)
  local copies, waits for them, and re-layouts: 9.69 us -> 14.3 us
  matrix products: 19.1 us -> 23.2 us
  between operations: 14.9 us -> 16.9 us
    slice x0 -> x3, local copies, waits for them, and re-layouts: none -> 3.21 us  [the longest x1 1.38 us: body(): third_weight = narrow_weight[2 * feature_slice:]]
    dot_general x3, matrix products: 9.59 us -> 12.3 us  [product(): lax.dot_general(jnp.concatenate(inputs), jnp.concatenate(slopes), (((0,),...]
    unnamed x52 -> x50, local copies, waits for them, and re-layouts: 4.48 us -> 5.84 us
    dot_general x8 -> x1, matrix products: 5.72 us -> 7.04 us  [body(): jnp.dot(gathered, narrow_weight[:2 * feature_slice], preferred_element_ty...]
  transfers between devices with their start and end apart: 38 -> 38, of which waited for: 17 -> 12; matrix products, arithmetic and copies ran while one was open for 18% -> 21% of each run, Pallas kernels for 12% -> 12%
where the time goes in v3:
time: 189 us; the launch traced here: 188 us
  starting transfers between devices  64 us (34%)
  Pallas kernels  27.6 us (15%)
  waiting for transfers between devices  26.7 us (14%)
  matrix products  23.2 us (12%)
  between operations  16.9 us (9%)
  other arithmetic  15.7 us (8%)
  local copies, waits for them, and re-layouts  14.3 us (8%)
    ppermute x37, starting transfers between devices, send(): return lax.ppermute(array, mesh_axes, pairs)  63.9 us
    ppermute x37, waiting for transfers between devices, send(): return lax.ppermute(array, mesh_axes, pairs)  26.7 us
    pallas_call x3, Pallas kernels, down_pieces(): pl.pallas_call(down_kernel, grid_spec=pltpu.PrefetchScalarGridSpec(num_sc...  19.1 us
    dot_general x3, matrix products, product(): lax.dot_general(jnp.concatenate(inputs), jnp.concatenate(slopes), (((0,),...  12.3 us
    dot_general x1, matrix products, body(): jnp.dot(gathered, narrow_weight[:2 * feature_slice], preferred_element_ty...  7.04 us
    unnamed x50, local copies, waits for them, and re-layouts  5.84 us
    pallas_call x1, Pallas kernels, rounded(): pl.pallas_call(round_kernel, grid=(layers,), in_specs=[pl.BlockSpec(memor...  5.19 us
    add x5, other arithmetic, plus(): return functools.reduce(jnp.add, [term.astype(f32) for term in terms])  4.84 us
  transfers between devices with their start and end apart: 38, of which 12 were waited for; matrix products, arithmetic and copies ran while one was open for 21% of the time, Pallas kernels for 12%

profile of v3, /device:TPU:0, one launch (start us, length us, event | category | flops | bytes accessed | tf_op | source)
XLA Modules:
  0.0 188.4 jit_solution(12156269432909383279)
XLA Ops:
  7.8 5.4 %down_projection.3 = (bf16[2,256,512]{2,1,0:T(8,128)(2,1)}, bf16[2,256,512]{2,1,0:T(8,128)(2,1)}) custom-call(s32[4]{0:T(128)} %broadcast_select_fusion.17.blocks_ref, bf16[256,896]{1,0:T(8,128)(2,1)} %bitcast.107, bf16[896,8192]{1,0:T(8,128)(2,1)} %refs_1_.5, bf16[896,8192]{1,0:T(8,128)(2,1)} %refs_1_.5, s32[28,8192]{1,0:T(8,128)} %refs_3_.5, ...), custom_call_target="tpu_custom_call" | custom-call | flops 939524096 | bytes 5505024 | tf_op jit(solution)/shard_map/down/down_projection/pallas_call | solution.py:115
  14.8 2.1 %collective-permute-start = (bf16[2,256,512]{2,1,0:T(8,128)(2,1)S(1)}, bf16[2,256,512]{2,1,0:T(8,128)(2,1)S(1)}, u32[]{:S(2)}, u32[]{:S(2)}) collective-permute-start(bf16[2,256,512]{2,1,0:T(8,128)(2,1)S(1)} %copy-done.18), channel_id=1, source_target_pairs={{0,4},{1,5},{2,6},{3,7},{4,8},{5,9},{6,10},{7,11},{8,12},{9,13},{1... | collective-permute-start | bytes 1572872 | tf_op jit(solution)/shard_map/reduce_down/ppermute | solution.py:57
  16.9 2.2 %collective-permute-start.3 = (bf16[2,256,512]{2,1,0:T(8,128)(2,1)S(1)}, bf16[2,256,512]{2,1,0:T(8,128)(2,1)S(1)}, u32[]{:S(2)}, u32[]{:S(2)}) collective-permute-start(bf16[2,256,512]{2,1,0:T(8,128)(2,1)S(1)} %copy-done.17), channel_id=1, source_target_pairs={{0,12},{1,13},{2,14},{3,15},{4,0},{5,1},{6,2},{7,3},{8,4},{9,5},{1... | collective-permute-start | bytes 1572872 | tf_op jit(solution)/shard_map/reduce_down/ppermute | solution.py:57
  20.2 8.0 %down_projection.4 = (bf16[2,256,512]{2,1,0:T(8,128)(2,1)}, bf16[2,256,512]{2,1,0:T(8,128)(2,1)}, bf16[2,256,512]{2,1,0:T(8,128)(2,1)}, bf16[2,256,512]{2,1,0:T(8,128)(2,1)}) custom-call(s32[8]{0:T(128)} %pad_add_fusion.1.blocks_ref, bf16[256,896]{1,0:T(8,128)(2,1)} %bitcast.108, bf16[896,8192]{1,0:T(8,128)(2,1)} %refs_1_.5, bf16[896,8192]{1,0:T(8,128)(2,1)} %refs_1_.5, ...), custom_call_target="tpu_custom_call" | custom-call | flops 1879048192 | bytes 11010048 | tf_op jit(solution)/shard_map/down/down_projection/pallas_call | solution.py:115
  33.6 3.2 %collective-permute-start.4 = (bf16[2,256,512]{2,1,0:T(8,128)(2,1)}, bf16[2,256,512]{2,1,0:T(8,128)(2,1)}, u32[]{:S(2)}, u32[]{:S(2)}) collective-permute-start(bf16[2,256,512]{2,1,0:T(8,128)(2,1)} %add.413), channel_id=1, source_target_pairs={{0,12},{1,13},{2,14},{3,15},{4,0},{5,1},{6,2},{7,3},{8,4},{9,5},{1... | collective-permute-start | bytes 1572872 | tf_op jit(solution)/shard_map/reduce_down/ppermute | solution.py:57
  36.7 5.7 %down_projection.5 = (f32[2,256,512]{2,1,0:T(8,128)}, f32[2,256,512]{2,1,0:T(8,128)}) custom-call(s32[4]{0:T(128)} %get-tuple-element.35.blocks_ref, bf16[256,896]{1,0:T(8,128)(2,1)} %bitcast.109, bf16[896,8192]{1,0:T(8,128)(2,1)} %refs_1_.5, bf16[896,8192]{1,0:T(8,128)(2,1)} %refs_1_.5, s32[28,8192]{1,0:T(8,128)} %refs_3_.5, s32[28,8192]{1,0:T(8,128)} %refs_3_.5), custom_call_target="tpu_custom_call" | custom-call | flops 939524096 | bytes 5505024 | tf_op jit(solution)/shard_map/down/down_projection/pallas_call | solution.py:115
  42.4 5.2 %round_weight.1 = bf16[1536,1024]{1,0:T(8,128)(2,1)} custom-call(f32[2,256,512]{2,1,0:T(8,128)} %get-tuple-element.36.after_ref, f32[1536,1024]{1,0:T(8,128)} %bitcast.90, f32[1536,1024]{1,0:T(8,128)} %bitcast.91), custom_call_target="tpu_custom_call" | custom-call | flops 1572864 | bytes 9437184 | tf_op jit(solution)/shard_map/round_weight/pallas_call | solution.py:157
  57.4 2.0 %collective-permute-start.8 = (bf16[256,512]{1,0:T(8,128)(2,1)}, bf16[256,512]{1,0:T(8,128)(2,1)}, u32[]{:S(2)}, u32[]{:S(2)}) collective-permute-start(bf16[256,512]{1,0:T(8,128)(2,1)} %get-tuple-element.69), channel_id=1, source_target_pairs={{0,2},{1,3},{2,0},{3,1},{4,6},{5,7},{6,4},{7,5},{8,10},{9,11},{10,... | collective-permute-start | bytes 786440 | tf_op jit(solution)/shard_map/reduce_down/ppermute | solution.py:57
  59.5 7.0 %fusion.8 = f32[1920,1024]{1,0:T(8,128)S(1)} fusion(bf16[1920,1024]{1,0:T(8,128)(2,1)} %all-gather.2.cloned.1.call-done, bf16[1536,1024]{1,0:T(8,128)(2,1)} %round_weight.1), kind=kOutput, calls=%fused_computation.30 | convolution fusion | flops 4026531840 | bytes 13893632 | tf_op jit(solution)/shard_map/early/dot_general | solution.py:298
  66.5 3.1 %copy-done.1 = f32[1920,1024]{1,0:T(8,128)} copy-done((f32[1920,1024]{1,0:T(8,128)}, f32[1920,1024]{1,0:T(8,128)S(1)}, u32[]{:S(2)}) %copy-start.1) | copy-done | bytes 7864344
  77.0 3.1 %collective-permute-start.10 = (bf16[96,512]{1,0:T(8,128)(2,1)S(1)}, bf16[96,512]{1,0:T(8,128)(2,1)S(1)}, u32[]{:S(2)}, u32[]{:S(2)}) collective-permute-start(bf16[96,512]{1,0:T(8,128)(2,1)S(1)} %convolution_convert_fusion.2), channel_id=1, source_target_pairs={{0,64},{1,65},{2,66},{3,67},{4,68},{5,69},{6,70},{7,71},{8,72},{9,... | collective-permute-start | bytes 294920 | tf_op jit(solution)/shard_map/back/ppermute | solution.py:57
  80.7 2.6 %collective-permute-start.9 = (bf16[96,512]{1,0:T(8,128)(2,1)S(1)}, bf16[96,512]{1,0:T(8,128)(2,1)S(1)}, u32[]{:S(2)}, u32[]{:S(2)}) collective-permute-start(bf16[96,512]{1,0:T(8,128)(2,1)S(1)} %convolution_convert_fusion.2), channel_id=1, source_target_pairs={{0,96},{1,97},{2,98},{3,99},{4,100},{5,101},{6,102},{7,103},{8,104... | collective-permute-start | bytes 294920 | tf_op jit(solution)/shard_map/back/ppermute | solution.py:57
  83.5 2.4 %collective-permute-done.11 = bf16[96,512]{1,0:T(8,128)(2,1)S(1)} collective-permute-done((bf16[96,512]{1,0:T(8,128)(2,1)S(1)}, bf16[96,512]{1,0:T(8,128)(2,1)S(1)}, u32[]{:S(2)}, u32[]{:S(2)}) %collective-permute-start.11) | collective-permute-done | bytes 98336 | tf_op jit(solution)/shard_map/back/ppermute | solution.py:57
  91.6 2.6 %collective-permute-start.15 = (bf16[2,96,1024]{2,1,0:T(8,128)(2,1)S(1)}, bf16[2,96,1024]{2,1,0:T(8,128)(2,1)S(1)}, u32[]{:S(2)}, u32[]{:S(2)}) collective-permute-start(bf16[2,96,1024]{2,1,0:T(8,128)(2,1)S(1)} %bitcast.122), channel_id=1, source_target_pairs={{0,4},{1,5},{2,6},{3,7},{4,8},{5,9},{6,10},{7,11},{8,12},{9,13},{1... | collective-permute-start | bytes 1179656 | tf_op jit(solution)/shard_map/reduce_draft/ppermute | solution.py:57
  94.5 5.5 %collective-permute-start.18 = (bf16[2,96,1024]{2,1,0:T(8,128)(2,1)S(1)}, bf16[2,96,1024]{2,1,0:T(8,128)(2,1)S(1)}, u32[]{:S(2)}, u32[]{:S(2)}) collective-permute-start(bf16[2,96,1024]{2,1,0:T(8,128)(2,1)S(1)} %bitcast.120), channel_id=1, source_target_pairs={{0,12},{1,13},{2,14},{3,15},{4,0},{5,1},{6,2},{7,3},{8,4},{9,5},{1... | collective-permute-start | bytes 1179656 | tf_op jit(solution)/shard_map/reduce_draft/ppermute | solution.py:57
  100.5 5.1 %collective-permute-start.17 = (bf16[2,96,1024]{2,1,0:T(8,128)(2,1)S(1)}, bf16[2,96,1024]{2,1,0:T(8,128)(2,1)S(1)}, u32[]{:S(2)}, u32[]{:S(2)}) collective-permute-start(bf16[2,96,1024]{2,1,0:T(8,128)(2,1)S(1)} %bitcast.121), channel_id=1, source_target_pairs={{0,12},{1,13},{2,14},{3,15},{4,0},{5,1},{6,2},{7,3},{8,4},{9,5},{1... | collective-permute-start | bytes 1179656 | tf_op jit(solution)/shard_map/reduce_draft/ppermute | solution.py:57
  107.6 3.5 %collective-permute-start.19 = (bf16[2,96,1024]{2,1,0:T(8,128)(2,1)S(1)}, bf16[2,96,1024]{2,1,0:T(8,128)(2,1)S(1)}, u32[]{:S(2)}, u32[]{:S(2)}) collective-permute-start(bf16[2,96,1024]{2,1,0:T(8,128)(2,1)S(1)} %add.470), channel_id=1, source_target_pairs={{0,12},{1,13},{2,14},{3,15},{4,0},{5,1},{6,2},{7,3},{8,4},{9,5},{1... | collective-permute-start | bytes 1179656 | tf_op jit(solution)/shard_map/reduce_draft/ppermute | solution.py:57
  111.5 7.7 %collective-permute-done.16 = bf16[2,96,1024]{2,1,0:T(8,128)(2,1)S(1)} collective-permute-done((bf16[2,96,1024]{2,1,0:T(8,128)(2,1)S(1)}, bf16[2,96,1024]{2,1,0:T(8,128)(2,1)S(1)}, u32[]{:S(2)}, u32[]{:S(2)}) %collective-permute-start.16) | collective-permute-done | bytes 393248 | tf_op jit(solution)/shard_map/reduce_draft/ppermute | solution.py:57
  124.1 2.6 %collective-permute-done.21 = bf16[96,1024]{1,0:T(8,128)(2,1)S(1)} collective-permute-done((bf16[96,1024]{1,0:T(8,128)(2,1)S(1)}, bf16[96,1024]{1,0:T(8,128)(2,1)S(1)}, u32[]{:S(2)}, u32[]{:S(2)}) %collective-permute-start.21) | collective-permute-done | bytes 196640 | tf_op jit(solution)/shard_map/reduce_draft/ppermute | solution.py:57
  126.8 3.4 %collective-permute-done.23 = bf16[96,1024]{1,0:T(8,128)(2,1)S(1)} collective-permute-done((bf16[96,1024]{1,0:T(8,128)(2,1)S(1)}, bf16[96,1024]{1,0:T(8,128)(2,1)S(1)}, u32[]{:S(2)}, u32[]{:S(2)}) %collective-permute-start.23) | collective-permute-done | bytes 196640 | tf_op jit(solution)/shard_map/reduce_draft/ppermute | solution.py:57
  130.7 2.3 %slice.81 = bf16[8,192,1024]{2,1,0:T(8,128)(2,1)S(1)} slice(bf16[8,240,1024]{2,1,0:T(8,128)(2,1)} %bitcast.111), slice={[0:8], [0:192], [0:1024]} | slice | bytes 6291456 | tf_op jit(solution)/shard_map/forward/slice | solution.py:331
  133.1 2.5 %collective-permute-start.26 = (f32[3,96]{1,0:T(4,128)S(1)}, f32[3,96]{1,0:T(4,128)S(1)}, u32[]{:S(2)}, u32[]{:S(2)}) collective-permute-start(f32[3,96]{1,0:T(4,128)S(1)} %fusion.105), channel_id=1, source_target_pairs={{0,64},{1,65},{2,66},{3,67},{4,68},{5,69},{6,70},{7,71},{8,72},{9,... | collective-permute-start | bytes 3464 | tf_op jit(solution)/shard_map/norm/ppermute | solution.py:57
  139.4 5.9 %collective-permute-start.28 = (bf16[96,1024]{1,0:T(8,128)(2,1)S(1)}, bf16[96,1024]{1,0:T(8,128)(2,1)S(1)}, u32[]{:S(2)}, u32[]{:S(2)}) collective-permute-start(bf16[96,1024]{1,0:T(8,128)(2,1)S(1)} %fusion.64), channel_id=1, source_target_pairs={{0,3},{1,0},{2,1},{3,2},{4,7},{5,4},{6,5},{7,6},{8,11},{9,8},{10,9... | collective-permute-start | bytes 589832 | tf_op jit(solution)/shard_map/gather_slope/ppermute | solution.py:57
  147.3 3.2 %collective-permute-done.28 = bf16[96,1024]{1,0:T(8,128)(2,1)S(1)} collective-permute-done((bf16[96,1024]{1,0:T(8,128)(2,1)S(1)}, bf16[96,1024]{1,0:T(8,128)(2,1)S(1)}, u32[]{:S(2)}, u32[]{:S(2)}) %collective-permute-start.28) | collective-permute-done | bytes 196640 | tf_op jit(solution)/shard_map/gather_slope/ppermute | solution.py:57
  150.5 2.0 %collective-permute-done.29 = bf16[96,1024]{1,0:T(8,128)(2,1)S(1)} collective-permute-done((bf16[96,1024]{1,0:T(8,128)(2,1)S(1)}, bf16[96,1024]{1,0:T(8,128)(2,1)S(1)}, u32[]{:S(2)}, u32[]{:S(2)}) %collective-permute-start.29) | collective-permute-done | bytes 196640 | tf_op jit(solution)/shard_map/gather_slope/ppermute | solution.py:57
  156.8 2.1 %together.1 = (bf16[192,1024]{1,0:T(8,128)(2,1)}, bf16[192,1024]{1,0:T(8,128)(2,1)}) custom-call(bf16[192,1024]{1,0:T(8,128)(2,1)} %copy-done.5, bf16[192,1024]{1,0:T(8,128)(2,1)} %pad_maximum_fusion.7.second_ref), custom_call_target="tpu_custom_call" | custom-call | tf_op jit(solution)/shard_map/gather_slope/together/pallas_call | solution.py:193
  160.8 2.9 %collective-permute-start.33 = (bf16[192,1024]{1,0:T(8,128)(2,1)}, bf16[192,1024]{1,0:T(8,128)(2,1)S(1)}, u32[]{:S(2)}, u32[]{:S(2)}) collective-permute-start(bf16[192,1024]{1,0:T(8,128)(2,1)} %get-tuple-element.51), channel_id=1, source_target_pairs={{0,12},{1,13},{2,14},{3,15},{4,0},{5,1},{6,2},{7,3},{8,4},{9,5},{1... | collective-permute-start | bytes 1179656 | tf_op jit(solution)/shard_map/gather_slope/ppermute | solution.py:57
  163.8 4.9 %multiply_subtract_fusion.1 = f32[1536,1024]{1,0:T(8,128)S(1)} fusion(f32[1536,1024]{1,0:T(8,128)} %bitcast.92, bf16[192,1536]{1,0:T(8,128)(2,1)S(1)} %copy-done.3, bf16[192,1536]{1,0:T(8,128)(2,1)S(1)} %get-tuple-element.59, bf16[96,1024]{1,0:T(8,128)(2,1)S(1)} %get-tuple-element.74, bf16[96,1024]{1,0:T(8,128)(2,1)S(1)} %get-tuple-element.73, ...), kind=kOutput, calls=%fused_computation.18 | convolution fusion | flops 1216610304 | bytes 14548992 | tf_op jit(solution)/shard_map/step/dot_general | solution.py:423
  168.7 3.2 %collective-permute-start.36 = (bf16[192,1024]{1,0:T(8,128)(2,1)S(1)}, bf16[192,1024]{1,0:T(8,128)(2,1)S(1)}, u32[]{:S(2)}, u32[]{:S(2)}) collective-permute-start(bf16[192,1024]{1,0:T(8,128)(2,1)S(1)} %collective-permute-done.34), channel_id=1, source_target_pairs={{0,12},{1,13},{2,14},{3,15},{4,0},{5,1},{6,2},{7,3},{8,4},{9,5},{1... | collective-permute-start | bytes 1179656 | tf_op jit(solution)/shard_map/gather_slope/ppermute | solution.py:57
  172.0 3.7 %multiply_subtract_fusion = f32[1536,1024]{1,0:T(8,128)S(1)} fusion(f32[1536,1024]{1,0:T(8,128)S(1)} %multiply_subtract_fusion.1, bf16[192,1536]{1,0:T(8,128)(2,1)S(1)} %copy-done.10, bf16[192,1536]{1,0:T(8,128)(2,1)S(1)} %copy-done.9, bf16[192,1536]{1,0:T(8,128)(2,1)S(1)} %copy-done.8, bf16[192,1536]{1,0:T(8,128)(2,1)S(1)} %copy-done.7, ...), kind=kOutput, calls=%fused_computation.17 | convolution fusion | flops 2434793472 | bytes 16515072 | tf_op jit(solution)/shard_map/step/dot_general | solution.py:423
  175.8 2.1 %collective-permute-done.35 = bf16[192,1024]{1,0:T(8,128)(2,1)S(1)} collective-permute-done((bf16[192,1024]{1,0:T(8,128)(2,1)}, bf16[192,1024]{1,0:T(8,128)(2,1)S(1)}, u32[]{:S(2)}, u32[]{:S(2)}) %collective-permute-start.35) | collective-permute-done | bytes 393248 | tf_op jit(solution)/shard_map/gather_slope/ppermute | solution.py:57
  177.9 3.6 %subtract_convert_fusion = bf16[1536,1024]{1,0:T(8,128)(2,1)} fusion(f32[1536,1024]{1,0:T(8,128)S(1)} %multiply_subtract_fusion, bf16[192,1536]{1,0:T(8,128)(2,1)S(1)} %copy-done.4, bf16[192,1536]{1,0:T(8,128)(2,1)S(1)} %get-tuple-element.58, bf16[192,1024]{1,0:T(8,128)(2,1)S(1)} %collective-permute-done.36, bf16[192,1024]{1,0:T(8,128)(2,1)S(1)} %collective-permute-done.35), kind=kOutput, calls=%fused_computation.16 | convolution fusion | flops 1216610304 | bytes 11403264 | tf_op jit(solution)/shard_map/step/dot_general | solution.py:423
  (171 shorter events, 50.6 us)
Async XLA Ops:
  7.2 52.3 %all-gather.2.cloned.1.call-start = ((), (), s32[]{:S(2)}) async-start(), calls=%async_computation | async-start | bytes 4423680 | tf_op jit(solution)/shard_map/all_gather | solution.py:285
  14.8 15.4 %collective-permute-start = (bf16[2,256,512]{2,1,0:T(8,128)(2,1)S(1)}, bf16[2,256,512]{2,1,0:T(8,128)(2,1)S(1)}, u32[]{:S(2)}, u32[]{:S(2)}) collective-permute-start(bf16[2,256,512]{2,1,0:T(8,128)(2,1)S(1)} %copy-done.18), channel_id=1, source_target_pairs={{0,4},{1,5},{2,6},{3,7},{4,8},{5,9},{6,10},{7,11},{8,12},{9,13},{1... | collective-permute-start | bytes 1572872 | tf_op jit(solution)/shard_map/reduce_down/ppermute | solution.py:57
  16.9 14.7 %collective-permute-start.3 = (bf16[2,256,512]{2,1,0:T(8,128)(2,1)S(1)}, bf16[2,256,512]{2,1,0:T(8,128)(2,1)S(1)}, u32[]{:S(2)}, u32[]{:S(2)}) collective-permute-start(bf16[2,256,512]{2,1,0:T(8,128)(2,1)S(1)} %copy-done.17), channel_id=1, source_target_pairs={{0,12},{1,13},{2,14},{3,15},{4,0},{5,1},{6,2},{7,3},{8,4},{9,5},{1... | collective-permute-start | bytes 1572872 | tf_op jit(solution)/shard_map/reduce_down/ppermute | solution.py:57
  28.2 20.9 %collective-permute-start.2 = (bf16[2,256,512]{2,1,0:T(8,128)(2,1)}, bf16[2,256,512]{2,1,0:T(8,128)(2,1)S(1)}, u32[]{:S(2)}, u32[]{:S(2)}) collective-permute-start(bf16[2,256,512]{2,1,0:T(8,128)(2,1)} %get-tuple-element.39), channel_id=1, source_target_pairs={{0,12},{1,13},{2,14},{3,15},{4,0},{5,1},{6,2},{7,3},{8,4},{9,5},{1... | collective-permute-start | bytes 1572872 | tf_op jit(solution)/shard_map/reduce_down/ppermute | solution.py:57
  31.3 18.6 %collective-permute-start.1 = (bf16[2,256,512]{2,1,0:T(8,128)(2,1)S(1)}, bf16[2,256,512]{2,1,0:T(8,128)(2,1)}, u32[]{:S(2)}, u32[]{:S(2)}) collective-permute-start(bf16[2,256,512]{2,1,0:T(8,128)(2,1)S(1)} %add.410), channel_id=1, source_target_pairs={{0,4},{1,5},{2,6},{3,7},{4,8},{5,9},{6,10},{7,11},{8,12},{9,13},{1... | collective-permute-start | bytes 1572872 | tf_op jit(solution)/shard_map/reduce_down/ppermute | solution.py:57
  31.5 19.9 %collective-permute-start.5 = (bf16[2,256,512]{2,1,0:T(8,128)(2,1)}, bf16[2,256,512]{2,1,0:T(8,128)(2,1)}, u32[]{:S(2)}, u32[]{:S(2)}) collective-permute-start(bf16[2,256,512]{2,1,0:T(8,128)(2,1)} %get-tuple-element.43), channel_id=1, source_target_pairs={{0,4},{1,5},{2,6},{3,7},{4,8},{5,9},{6,10},{7,11},{8,12},{9,13},{1... | collective-permute-start | bytes 1572872 | tf_op jit(solution)/shard_map/reduce_down/ppermute | solution.py:57
  33.6 17.8 %collective-permute-start.4 = (bf16[2,256,512]{2,1,0:T(8,128)(2,1)}, bf16[2,256,512]{2,1,0:T(8,128)(2,1)}, u32[]{:S(2)}, u32[]{:S(2)}) collective-permute-start(bf16[2,256,512]{2,1,0:T(8,128)(2,1)} %add.413), channel_id=1, source_target_pairs={{0,12},{1,13},{2,14},{3,15},{4,0},{5,1},{6,2},{7,3},{8,4},{9,5},{1... | collective-permute-start | bytes 1572872 | tf_op jit(solution)/shard_map/reduce_down/ppermute | solution.py:57
  54.2 21.0 %collective-permute-start.6 = (bf16[256,512]{1,0:T(8,128)(2,1)}, bf16[256,512]{1,0:T(8,128)(2,1)S(1)}, u32[]{:S(2)}, u32[]{:S(2)}) collective-permute-start(bf16[256,512]{1,0:T(8,128)(2,1)} %get-tuple-element.68), channel_id=1, source_target_pairs={{0,1},{1,2},{2,3},{3,0},{4,5},{5,6},{6,7},{7,4},{8,9},{9,10},{10,1... | collective-permute-start | bytes 786440 | tf_op jit(solution)/shard_map/reduce_down/ppermute | solution.py:57
  55.8 19.5 %collective-permute-start.7 = (bf16[256,512]{1,0:T(8,128)(2,1)}, bf16[256,512]{1,0:T(8,128)(2,1)}, u32[]{:S(2)}, u32[]{:S(2)}) collective-permute-start(bf16[256,512]{1,0:T(8,128)(2,1)} %get-tuple-element.70), channel_id=1, source_target_pairs={{0,3},{1,0},{2,1},{3,2},{4,7},{5,4},{6,5},{7,6},{8,11},{9,8},{10,9... | collective-permute-start | bytes 786440 | tf_op jit(solution)/shard_map/reduce_down/ppermute | solution.py:57
  57.4 17.8 %collective-permute-start.8 = (bf16[256,512]{1,0:T(8,128)(2,1)}, bf16[256,512]{1,0:T(8,128)(2,1)}, u32[]{:S(2)}, u32[]{:S(2)}) collective-permute-start(bf16[256,512]{1,0:T(8,128)(2,1)} %get-tuple-element.69), channel_id=1, source_target_pairs={{0,2},{1,3},{2,0},{3,1},{4,6},{5,7},{6,4},{7,5},{8,10},{9,11},{10,... | collective-permute-start | bytes 786440 | tf_op jit(solution)/shard_map/reduce_down/ppermute | solution.py:57
  77.0 6.6 %collective-permute-start.10 = (bf16[96,512]{1,0:T(8,128)(2,1)S(1)}, bf16[96,512]{1,0:T(8,128)(2,1)S(1)}, u32[]{:S(2)}, u32[]{:S(2)}) collective-permute-start(bf16[96,512]{1,0:T(8,128)(2,1)S(1)} %convolution_convert_fusion.2), channel_id=1, source_target_pairs={{0,64},{1,65},{2,66},{3,67},{4,68},{5,69},{6,70},{7,71},{8,72},{9,... | collective-permute-start | bytes 294920 | tf_op jit(solution)/shard_map/back/ppermute | solution.py:57
  80.1 5.8 %collective-permute-start.11 = (bf16[96,512]{1,0:T(8,128)(2,1)S(1)}, bf16[96,512]{1,0:T(8,128)(2,1)S(1)}, u32[]{:S(2)}, u32[]{:S(2)}) collective-permute-start(bf16[96,512]{1,0:T(8,128)(2,1)S(1)} %convolution_convert_fusion.2), channel_id=1, source_target_pairs={{0,32},{1,33},{2,34},{3,35},{4,36},{5,37},{6,38},{7,39},{8,40},{9,... | collective-permute-start | bytes 294920 | tf_op jit(solution)/shard_map/back/ppermute | solution.py:57
  86.1 13.9 %collective-permute-start.13 = (bf16[96,512]{1,0:T(8,128)(2,1)S(1)}, bf16[96,512]{1,0:T(8,128)(2,1)S(1)}, u32[]{:S(2)}, u32[]{:S(2)}) collective-permute-start(bf16[96,512]{1,0:T(8,128)(2,1)S(1)} %get-tuple-element.89), channel_id=1, source_target_pairs={{0,0},{1,1},{2,16},{3,20},{4,32},{5,33},{6,48},{7,52},{8,64},{9,65... | collective-permute-start | bytes 294920 | tf_op jit(solution)/shard_map/targets/ppermute | solution.py:57
  86.8 13.3 %collective-permute-start.14 = (bf16[96,512]{1,0:T(8,128)(2,1)S(1)}, bf16[96,512]{1,0:T(8,128)(2,1)S(1)}, u32[]{:S(2)}, u32[]{:S(2)}) collective-permute-start(bf16[96,512]{1,0:T(8,128)(2,1)S(1)} %get-tuple-element.88), channel_id=1, source_target_pairs={{0,1},{1,0},{2,20},{3,16},{4,33},{5,32},{6,52},{7,48},{8,65},{9,64... | collective-permute-start | bytes 294920 | tf_op jit(solution)/shard_map/targets/ppermute | solution.py:57
  91.6 15.2 %collective-permute-start.15 = (bf16[2,96,1024]{2,1,0:T(8,128)(2,1)S(1)}, bf16[2,96,1024]{2,1,0:T(8,128)(2,1)S(1)}, u32[]{:S(2)}, u32[]{:S(2)}) collective-permute-start(bf16[2,96,1024]{2,1,0:T(8,128)(2,1)S(1)} %bitcast.122), channel_id=1, source_target_pairs={{0,4},{1,5},{2,6},{3,7},{4,8},{5,9},{6,10},{7,11},{8,12},{9,13},{1... | collective-permute-start | bytes 1179656 | tf_op jit(solution)/shard_map/reduce_draft/ppermute | solution.py:57
  94.5 12.9 %collective-permute-start.18 = (bf16[2,96,1024]{2,1,0:T(8,128)(2,1)S(1)}, bf16[2,96,1024]{2,1,0:T(8,128)(2,1)S(1)}, u32[]{:S(2)}, u32[]{:S(2)}) collective-permute-start(bf16[2,96,1024]{2,1,0:T(8,128)(2,1)S(1)} %bitcast.120), channel_id=1, source_target_pairs={{0,12},{1,13},{2,14},{3,15},{4,0},{5,1},{6,2},{7,3},{8,4},{9,5},{1... | collective-permute-start | bytes 1179656 | tf_op jit(solution)/shard_map/reduce_draft/ppermute | solution.py:57
  100.5 11.0 %collective-permute-start.17 = (bf16[2,96,1024]{2,1,0:T(8,128)(2,1)S(1)}, bf16[2,96,1024]{2,1,0:T(8,128)(2,1)S(1)}, u32[]{:S(2)}, u32[]{:S(2)}) collective-permute-start(bf16[2,96,1024]{2,1,0:T(8,128)(2,1)S(1)} %bitcast.121), channel_id=1, source_target_pairs={{0,12},{1,13},{2,14},{3,15},{4,0},{5,1},{6,2},{7,3},{8,4},{9,5},{1... | collective-permute-start | bytes 1179656 | tf_op jit(solution)/shard_map/reduce_draft/ppermute | solution.py:57
  106.0 13.4 %collective-permute-start.20 = (bf16[2,96,1024]{2,1,0:T(8,128)(2,1)S(1)}, bf16[2,96,1024]{2,1,0:T(8,128)(2,1)S(1)}, u32[]{:S(2)}, u32[]{:S(2)}) collective-permute-start(bf16[2,96,1024]{2,1,0:T(8,128)(2,1)S(1)} %bitcast.119), channel_id=1, source_target_pairs={{0,4},{1,5},{2,6},{3,7},{4,8},{5,9},{6,10},{7,11},{8,12},{9,13},{1... | collective-permute-start | bytes 1179656 | tf_op jit(solution)/shard_map/reduce_draft/ppermute | solution.py:57
  107.0 12.3 %collective-permute-start.16 = (bf16[2,96,1024]{2,1,0:T(8,128)(2,1)S(1)}, bf16[2,96,1024]{2,1,0:T(8,128)(2,1)S(1)}, u32[]{:S(2)}, u32[]{:S(2)}) collective-permute-start(bf16[2,96,1024]{2,1,0:T(8,128)(2,1)S(1)} %add.465), channel_id=1, source_target_pairs={{0,4},{1,5},{2,6},{3,7},{4,8},{5,9},{6,10},{7,11},{8,12},{9,13},{1... | collective-permute-start | bytes 1179656 | tf_op jit(solution)/shard_map/reduce_draft/ppermute | solution.py:57
  107.6 11.8 %collective-permute-start.19 = (bf16[2,96,1024]{2,1,0:T(8,128)(2,1)S(1)}, bf16[2,96,1024]{2,1,0:T(8,128)(2,1)S(1)}, u32[]{:S(2)}, u32[]{:S(2)}) collective-permute-start(bf16[2,96,1024]{2,1,0:T(8,128)(2,1)S(1)} %add.470), channel_id=1, source_target_pairs={{0,12},{1,13},{2,14},{3,15},{4,0},{5,1},{6,2},{7,3},{8,4},{9,5},{1... | collective-permute-start | bytes 1179656 | tf_op jit(solution)/shard_map/reduce_draft/ppermute | solution.py:57
  119.8 6.9 %collective-permute-start.21 = (bf16[96,1024]{1,0:T(8,128)(2,1)S(1)}, bf16[96,1024]{1,0:T(8,128)(2,1)S(1)}, u32[]{:S(2)}, u32[]{:S(2)}) collective-permute-start(bf16[96,1024]{1,0:T(8,128)(2,1)S(1)} %get-tuple-element.75), channel_id=1, source_target_pairs={{0,1},{1,2},{2,3},{3,0},{4,5},{5,6},{6,7},{7,4},{8,9},{9,10},{10,1... | collective-permute-start | bytes 589832 | tf_op jit(solution)/shard_map/reduce_draft/ppermute | solution.py:57
  121.1 5.7 %collective-permute-start.22 = (bf16[96,1024]{1,0:T(8,128)(2,1)S(1)}, bf16[96,1024]{1,0:T(8,128)(2,1)S(1)}, u32[]{:S(2)}, u32[]{:S(2)}) collective-permute-start(bf16[96,1024]{1,0:T(8,128)(2,1)S(1)} %get-tuple-element.77), channel_id=1, source_target_pairs={{0,3},{1,0},{2,1},{3,2},{4,7},{5,4},{6,5},{7,6},{8,11},{9,8},{10,9... | collective-permute-start | bytes 589832 | tf_op jit(solution)/shard_map/reduce_draft/ppermute | solution.py:57
  123.1 7.2 %collective-permute-start.23 = (bf16[96,1024]{1,0:T(8,128)(2,1)S(1)}, bf16[96,1024]{1,0:T(8,128)(2,1)S(1)}, u32[]{:S(2)}, u32[]{:S(2)}) collective-permute-start(bf16[96,1024]{1,0:T(8,128)(2,1)S(1)} %get-tuple-element.76), channel_id=1, source_target_pairs={{0,2},{1,3},{2,0},{3,1},{4,6},{5,7},{6,4},{7,5},{8,10},{9,11},{10,... | collective-permute-start | bytes 589832 | tf_op jit(solution)/shard_map/reduce_draft/ppermute | solution.py:57
  139.4 11.2 %collective-permute-start.28 = (bf16[96,1024]{1,0:T(8,128)(2,1)S(1)}, bf16[96,1024]{1,0:T(8,128)(2,1)S(1)}, u32[]{:S(2)}, u32[]{:S(2)}) collective-permute-start(bf16[96,1024]{1,0:T(8,128)(2,1)S(1)} %fusion.64), channel_id=1, source_target_pairs={{0,3},{1,0},{2,1},{3,2},{4,7},{5,4},{6,5},{7,6},{8,11},{9,8},{10,9... | collective-permute-start | bytes 589832 | tf_op jit(solution)/shard_map/gather_slope/ppermute | solution.py:57
  145.2 7.3 %collective-permute-start.29 = (bf16[96,1024]{1,0:T(8,128)(2,1)S(1)}, bf16[96,1024]{1,0:T(8,128)(2,1)S(1)}, u32[]{:S(2)}, u32[]{:S(2)}) collective-permute-start(bf16[96,1024]{1,0:T(8,128)(2,1)S(1)} %fusion.64), channel_id=1, source_target_pairs={{0,2},{1,3},{2,0},{3,1},{4,6},{5,7},{6,4},{7,5},{8,10},{9,11},{10,... | collective-permute-start | bytes 589832 | tf_op jit(solution)/shard_map/gather_slope/ppermute | solution.py:57
  145.3 9.0 %collective-permute-start.30 = (bf16[96,1024]{1,0:T(8,128)(2,1)S(1)}, bf16[96,1024]{1,0:T(8,128)(2,1)S(1)}, u32[]{:S(2)}, u32[]{:S(2)}) collective-permute-start(bf16[96,1024]{1,0:T(8,128)(2,1)S(1)} %fusion.64), channel_id=1, source_target_pairs={{0,1},{1,2},{2,3},{3,0},{4,5},{5,6},{6,7},{7,4},{8,9},{9,10},{10,1... | collective-permute-start | bytes 589832 | tf_op jit(solution)/shard_map/gather_slope/ppermute | solution.py:57
  154.4 14.3 %collective-permute-start.31 = (bf16[192,1024]{1,0:T(8,128)(2,1)S(1)}, bf16[192,1024]{1,0:T(8,128)(2,1)}, u32[]{:S(2)}, u32[]{:S(2)}) collective-permute-start(bf16[192,1024]{1,0:T(8,128)(2,1)S(1)} %pad_maximum_fusion.6.first_ref), channel_id=1, source_target_pairs={{0,4},{1,5},{2,6},{3,7},{4,8},{5,9},{6,10},{7,11},{8,12},{9,13},{1... | collective-permute-start | bytes 1179656 | tf_op jit(solution)/shard_map/gather_slope/ppermute | solution.py:57
  158.8 9.9 %collective-permute-start.34 = (bf16[192,1024]{1,0:T(8,128)(2,1)}, bf16[192,1024]{1,0:T(8,128)(2,1)S(1)}, u32[]{:S(2)}, u32[]{:S(2)}) collective-permute-start(bf16[192,1024]{1,0:T(8,128)(2,1)} %pad_maximum_fusion.7.second_ref), channel_id=1, source_target_pairs={{0,12},{1,13},{2,14},{3,15},{4,0},{5,1},{6,2},{7,3},{8,4},{9,5},{1... | collective-permute-start | bytes 1179656 | tf_op jit(solution)/shard_map/gather_slope/ppermute | solution.py:57
  160.5 11.5 %collective-permute-start.32 = (bf16[192,1024]{1,0:T(8,128)(2,1)}, bf16[192,1024]{1,0:T(8,128)(2,1)S(1)}, u32[]{:S(2)}, u32[]{:S(2)}) collective-permute-start(bf16[192,1024]{1,0:T(8,128)(2,1)} %get-tuple-element.50), channel_id=1, source_target_pairs={{0,4},{1,5},{2,6},{3,7},{4,8},{5,9},{6,10},{7,11},{8,12},{9,13},{1... | collective-permute-start | bytes 1179656 | tf_op jit(solution)/shard_map/gather_slope/ppermute | solution.py:57
  160.8 11.1 %collective-permute-start.33 = (bf16[192,1024]{1,0:T(8,128)(2,1)}, bf16[192,1024]{1,0:T(8,128)(2,1)S(1)}, u32[]{:S(2)}, u32[]{:S(2)}) collective-permute-start(bf16[192,1024]{1,0:T(8,128)(2,1)} %get-tuple-element.51), channel_id=1, source_target_pairs={{0,12},{1,13},{2,14},{3,15},{4,0},{5,1},{6,2},{7,3},{8,4},{9,5},{1... | collective-permute-start | bytes 1179656 | tf_op jit(solution)/shard_map/gather_slope/ppermute | solution.py:57
  168.7 9.3 %collective-permute-start.35 = (bf16[192,1024]{1,0:T(8,128)(2,1)}, bf16[192,1024]{1,0:T(8,128)(2,1)S(1)}, u32[]{:S(2)}, u32[]{:S(2)}) collective-permute-start(bf16[192,1024]{1,0:T(8,128)(2,1)} %collective-permute-done.31), channel_id=1, source_target_pairs={{0,4},{1,5},{2,6},{3,7},{4,8},{5,9},{6,10},{7,11},{8,12},{9,13},{1... | collective-permute-start | bytes 1179656 | tf_op jit(solution)/shard_map/gather_slope/ppermute | solution.py:57
  168.7 9.2 %collective-permute-start.36 = (bf16[192,1024]{1,0:T(8,128)(2,1)S(1)}, bf16[192,1024]{1,0:T(8,128)(2,1)S(1)}, u32[]{:S(2)}, u32[]{:S(2)}) collective-permute-start(bf16[192,1024]{1,0:T(8,128)(2,1)S(1)} %collective-permute-done.34), channel_id=1, source_target_pairs={{0,12},{1,13},{2,14},{3,15},{4,0},{5,1},{6,2},{7,3},{8,4},{9,5},{1... | collective-permute-start | bytes 1179656 | tf_op jit(solution)/shard_map/gather_slope/ppermute | solution.py:57
  (31 other events, 172.2 us)
Sparse Core Ops, SparseCore 0:
  14.9 33.5 all-gather.1

commit v4 on v2

--- a/solution.py
+++ b/solution.py
@@ -146,12 +146,12 @@
     out_ref[half:] = lower_ref[...].astype(bf16)
 
 
-def rounded_layers(wide, layers, start, after):
+def rounded_pair(wide, after):
     rows, columns = wide.shape
-    step = rows // 3
+    layers, step = 2, rows // 3
 
     def half_layer(half):
-        return pl.BlockSpec((step // 2, columns), lambda i: (2 * (start + i) + half, 0))
+        return pl.BlockSpec((step // 2, columns), lambda i: (2 * i + half, 0))
 
     return pl.pallas_call(
         round_kernel,
@@ -167,21 +167,6 @@
         ),
         name="round_weight",
     )(after, wide, wide)
-
-
-def together_kernel(first_ref, second_ref, first_out_ref, second_out_ref):
-    first_out_ref[...] = first_ref[...]
-    second_out_ref[...] = second_ref[...]
-
-
-def together(first, second):
-    return pl.pallas_call(
-        together_kernel,
-        in_specs=[pl.BlockSpec(memory_space=pltpu.VMEM)] * 2,
-        out_specs=[pl.BlockSpec(memory_space=pltpu.VMEM)] * 2,
-        out_shape=[jax.ShapeDtypeStruct(a.shape, a.dtype) for a in (first, second)],
-        name="together",
-    )(first, second)
 
 
 def reduce_blocks(near, direct, own, q):
@@ -280,8 +265,8 @@
         mixed, first_sum = reduce_blocks(near, direct, own, q)
 
     flat_weight = draft_input_weight.reshape(3 * feature_slice, out_slice)
-    pair_weight = rounded_layers(flat_weight, 2, 0, first_sum)
-    third_weight = rounded_layers(flat_weight, 1, 2, first_sum)
+    pair_weight = rounded_pair(flat_weight, first_sum)
+    third_weight = draft_input_weight[2].astype(bf16)
     upper_layer = (
         stream_input.astype(f32) + mixed.reshape(steps, rows, feature_slice)
     ).astype(bf16)
@@ -333,9 +318,7 @@
         def piece(total, kind):
             return total.astype(kind).reshape(2, slots, out_slice)
 
-        far_pairs = [
-            pair_product(pair_weight, shift, half) for shift in (2, 1, 3) for half in range(2)
-        ]
+        far_pairs = [pair_product(pair_weight, 2, half) for half in range(2)]
         others, fronts, far_pairs, _ = lax.optimization_barrier(
             (others, fronts, far_pairs, posted)
         )
@@ -351,8 +334,12 @@
             (near, got, pair_weight, third_weight)
         )
         direct = [
-            piece(far_pairs[2 + k] + third_product(third_weight, (1, 3)[k // 2], k % 2), bf16)
-            for k in range(4)
+            piece(
+                pair_product(pair_weight, shift, half) + third_product(third_weight, shift, half),
+                bf16,
+            )
+            for shift in (1, 3)
+            for half in range(2)
         ]
         _, pair_weight, third_weight = lax.optimization_barrier(
             (direct, pair_weight, third_weight)
@@ -396,12 +383,23 @@
         ring = turned(ring, q)
         upper_half, lower_half = jnp.concatenate(ring[:2]), jnp.concatenate(ring[2:])
         previous_upper = send(upper_half, along_first(1))
+        following_upper = send(upper_half, along_first(-1))
+        previous_lower = send(lower_half, along_first(1))
         following_lower = send(lower_half, along_first(-1))
-        upper_again, lower_again = together(upper_half, lower_half)
-        previous_lower = send(lower_again, along_first(1))
-        following_upper = send(upper_again, along_first(-1))
-        low = send(previous_upper, along_first(1))
-        high = send(following_lower, along_first(-1))
+        upper, lower = [
+            lax.optimization_barrier(
+                jnp.concatenate(
+                    [
+                        send(previous[:slots], along_first(1)),
+                        send(following[slots:], along_first(-1)),
+                    ]
+                )
+            )
+            for previous, following in (
+                (previous_upper, following_upper),
+                (previous_lower, following_lower),
+            )
+        ]
 
     with jax.named_scope("step"):
         features = jnp.concatenate([pairs.reshape(-1, 2 * feature_slice), thirds], axis=1)
@@ -428,7 +426,7 @@
                 [previous_upper, previous_lower, following_upper, following_lower],
             )
         )
-        total = total + product([(2, 0), (2, 1)], [low, high])
+        total = total + product([(2, 0), (2, 1)], [upper, lower])
         new_weight = (flat_weight - step_rate * total).astype(bf16)
         new_weight = new_weight.reshape(draft_input_weight.shape)
     return (upper_layer, new_weight)

time: 178 us -> 183 us (1.028)
  waiting for transfers between devices: 26.3 us -> 32.1 us
  starting transfers between devices: 64.1 us -> 69.6 us
  Pallas kernels: 27 us -> 22.3 us
    ppermute x37 -> x39, waiting for transfers between devices: 26.3 us -> 32.1 us  [send(): return lax.ppermute(array, mesh_axes, pairs)]
    ppermute x37 -> x39, starting transfers between devices: 64.1 us -> 69.5 us  [send(): return lax.ppermute(array, mesh_axes, pairs)]
    pallas_call x3 -> x1, Pallas kernels: 7.92 us -> 3.25 us  [rounded_pair(): pl.pallas_call(round_kernel, grid=(layers,), in_specs=[pl.BlockSpec(memor...]
    unnamed x52 -> x54, local copies, waits for them, and re-layouts: 4.48 us -> 2.35 us
  transfers between devices with their start and end apart: 38 -> 40, of which waited for: 17 -> 14; matrix products, arithmetic and copies ran while one was open for 18% -> 18% of each run, Pallas kernels for 12% -> 9%
where the time goes in v4:
time: 183 us; the launch traced here: 182 us
  starting transfers between devices  69.6 us (38%)
  waiting for transfers between devices  32.1 us (18%)
  Pallas kernels  22.3 us (12%)
  matrix products  18.2 us (10%)
  other arithmetic  15.2 us (8%)
  between operations  15.2 us (8%)
  local copies, waits for them, and re-layouts  9.23 us (5%)
    ppermute x39, starting transfers between devices, send(): return lax.ppermute(array, mesh_axes, pairs)  69.5 us
    ppermute x39, waiting for transfers between devices, send(): return lax.ppermute(array, mesh_axes, pairs)  32.1 us
    pallas_call x3, Pallas kernels, down_pieces(): pl.pallas_call(down_kernel, grid_spec=pltpu.PrefetchScalarGridSpec(num_sc...  19.1 us
    dot_general x3, matrix products, product(): lax.dot_general(jnp.concatenate(inputs), jnp.concatenate(slopes), (((0,),...  8.51 us
    dot_general x8, matrix products, pair_product(): return jnp.dot(rows_of, weight, preferred_element_type=f32)  5.82 us
    add x5, other arithmetic, plus(): return functools.reduce(jnp.add, [term.astype(f32) for term in terms])  4.51 us
  transfers between devices with their start and end apart: 40, of which 14 were waited for; matrix products, arithmetic and copies ran while one was open for 18% of the time, Pallas kernels for 9%

profile of v4, /device:TPU:0, one launch (start us, length us, event | category | flops | bytes accessed | tf_op | source)
XLA Modules:
  0.0 181.8 jit_solution(11459152711731360165)
XLA Ops:
  7.8 5.4 %down_projection.3 = (bf16[2,256,512]{2,1,0:T(8,128)(2,1)}, bf16[2,256,512]{2,1,0:T(8,128)(2,1)}) custom-call(s32[4]{0:T(128)} %broadcast_select_fusion.17.blocks_ref, bf16[256,896]{1,0:T(8,128)(2,1)} %bitcast.121, bf16[896,8192]{1,0:T(8,128)(2,1)} %refs_1_.5, bf16[896,8192]{1,0:T(8,128)(2,1)} %refs_1_.5, s32[28,8192]{1,0:T(8,128)} %refs_3_.5, ...), custom_call_target="tpu_custom_call" | custom-call | flops 939524096 | bytes 5505024 | tf_op jit(solution)/shard_map/down/down_projection/pallas_call | solution.py:115
  15.2 2.1 %collective-permute-start = (bf16[2,256,512]{2,1,0:T(8,128)(2,1)S(1)}, bf16[2,256,512]{2,1,0:T(8,128)(2,1)S(1)}, u32[]{:S(2)}, u32[]{:S(2)}) collective-permute-start(bf16[2,256,512]{2,1,0:T(8,128)(2,1)S(1)} %copy-done.20), channel_id=1, source_target_pairs={{0,4},{1,5},{2,6},{3,7},{4,8},{5,9},{6,10},{7,11},{8,12},{9,13},{1... | collective-permute-start | bytes 1572872 | tf_op jit(solution)/shard_map/reduce_down/ppermute | solution.py:57
  17.3 2.2 %collective-permute-start.3 = (bf16[2,256,512]{2,1,0:T(8,128)(2,1)S(1)}, bf16[2,256,512]{2,1,0:T(8,128)(2,1)S(1)}, u32[]{:S(2)}, u32[]{:S(2)}) collective-permute-start(bf16[2,256,512]{2,1,0:T(8,128)(2,1)S(1)} %copy-done.19), channel_id=1, source_target_pairs={{0,12},{1,13},{2,14},{3,15},{4,0},{5,1},{6,2},{7,3},{8,4},{9,5},{1... | collective-permute-start | bytes 1572872 | tf_op jit(solution)/shard_map/reduce_down/ppermute | solution.py:57
  20.6 8.0 %down_projection.4 = (bf16[2,256,512]{2,1,0:T(8,128)(2,1)}, bf16[2,256,512]{2,1,0:T(8,128)(2,1)}, bf16[2,256,512]{2,1,0:T(8,128)(2,1)}, bf16[2,256,512]{2,1,0:T(8,128)(2,1)}) custom-call(s32[8]{0:T(128)} %pad_add_fusion.1.blocks_ref, bf16[256,896]{1,0:T(8,128)(2,1)} %bitcast.122, bf16[896,8192]{1,0:T(8,128)(2,1)} %refs_1_.5, bf16[896,8192]{1,0:T(8,128)(2,1)} %refs_1_.5, ...), custom_call_target="tpu_custom_call" | custom-call | flops 1879048192 | bytes 11010048 | tf_op jit(solution)/shard_map/down/down_projection/pallas_call | solution.py:115
  28.6 1.9 %collective-permute-start.2 = (bf16[2,256,512]{2,1,0:T(8,128)(2,1)}, bf16[2,256,512]{2,1,0:T(8,128)(2,1)S(1)}, u32[]{:S(2)}, u32[]{:S(2)}) collective-permute-start(bf16[2,256,512]{2,1,0:T(8,128)(2,1)} %get-tuple-element.41), channel_id=1, source_target_pairs={{0,12},{1,13},{2,14},{3,15},{4,0},{5,1},{6,2},{7,3},{8,4},{9,5},{1... | collective-permute-start | bytes 1572872 | tf_op jit(solution)/shard_map/reduce_down/ppermute | solution.py:57
  33.2 3.2 %collective-permute-start.4 = (bf16[2,256,512]{2,1,0:T(8,128)(2,1)S(1)}, bf16[2,256,512]{2,1,0:T(8,128)(2,1)}, u32[]{:S(2)}, u32[]{:S(2)}) collective-permute-start(bf16[2,256,512]{2,1,0:T(8,128)(2,1)S(1)} %add.415), channel_id=1, source_target_pairs={{0,12},{1,13},{2,14},{3,15},{4,0},{5,1},{6,2},{7,3},{8,4},{9,5},{1... | collective-permute-start | bytes 1572872 | tf_op jit(solution)/shard_map/reduce_down/ppermute | solution.py:57
  36.4 5.7 %down_projection.5 = (f32[2,256,512]{2,1,0:T(8,128)}, f32[2,256,512]{2,1,0:T(8,128)}) custom-call(s32[4]{0:T(128)} %get-tuple-element.37.blocks_ref, bf16[256,896]{1,0:T(8,128)(2,1)} %bitcast.123, bf16[896,8192]{1,0:T(8,128)(2,1)} %refs_1_.5, bf16[896,8192]{1,0:T(8,128)(2,1)} %refs_1_.5, s32[28,8192]{1,0:T(8,128)} %refs_3_.5, s32[28,8192]{1,0:T(8,128)} %refs_3_.5), custom_call_target="tpu_custom_call" | custom-call | flops 939524096 | bytes 5505024 | tf_op jit(solution)/shard_map/down/down_projection/pallas_call | solution.py:115
  43.8 4.0 %collective-permute-done.5 = bf16[2,256,512]{2,1,0:T(8,128)(2,1)S(1)} collective-permute-done((bf16[2,256,512]{2,1,0:T(8,128)(2,1)}, bf16[2,256,512]{2,1,0:T(8,128)(2,1)S(1)}, u32[]{:S(2)}, u32[]{:S(2)}) %collective-permute-start.5) | collective-permute-done | bytes 524320 | tf_op jit(solution)/shard_map/reduce_down/ppermute | solution.py:57
  52.6 2.9 %collective-permute-start.8 = (bf16[256,512]{1,0:T(8,128)(2,1)}, bf16[256,512]{1,0:T(8,128)(2,1)}, u32[]{:S(2)}, u32[]{:S(2)}) collective-permute-start(bf16[256,512]{1,0:T(8,128)(2,1)} %get-tuple-element.73), channel_id=1, source_target_pairs={{0,2},{1,3},{2,0},{3,1},{4,6},{5,7},{6,4},{7,5},{8,10},{9,11},{10,... | collective-permute-start | bytes 786440 | tf_op jit(solution)/shard_map/reduce_down/ppermute | solution.py:57
  59.5 3.2 %round_weight.1 = bf16[1024,1024]{1,0:T(8,128)(2,1)} custom-call(f32[8,128]{1,0:T(8,128)} %slice_bitcast_fusion.2.after_ref, f32[1536,1024]{1,0:T(8,128)} %bitcast.102, f32[1536,1024]{1,0:T(8,128)} %bitcast.103), custom_call_target="tpu_custom_call" | custom-call | flops 1048576 | bytes 6291456 | tf_op jit(solution)/shard_map/round_weight/pallas_call | solution.py:156
  66.1 2.7 %collective-permute-start.10 = (bf16[96,512]{1,0:T(8,128)(2,1)S(1)}, bf16[96,512]{1,0:T(8,128)(2,1)S(1)}, u32[]{:S(2)}, u32[]{:S(2)}) collective-permute-start(bf16[96,512]{1,0:T(8,128)(2,1)S(1)} %convolution_convert_fusion.2), channel_id=1, source_target_pairs={{0,64},{1,65},{2,66},{3,67},{4,68},{5,69},{6,70},{7,71},{8,72},{9,... | collective-permute-start | bytes 294920 | tf_op jit(solution)/shard_map/back/ppermute | solution.py:57
  72.9 2.1 %collective-permute-start.13 = (bf16[96,512]{1,0:T(8,128)(2,1)}, bf16[96,512]{1,0:T(8,128)(2,1)}, u32[]{:S(2)}, u32[]{:S(2)}) collective-permute-start(bf16[96,512]{1,0:T(8,128)(2,1)} %get-tuple-element.93), channel_id=1, source_target_pairs={{0,0},{1,1},{2,16},{3,20},{4,32},{5,33},{6,48},{7,52},{8,64},{9,65... | collective-permute-start | bytes 294920 | tf_op jit(solution)/shard_map/targets/ppermute | solution.py:57
  83.5 3.2 %collective-permute-start.18 = (bf16[2,96,1024]{2,1,0:T(8,128)(2,1)S(1)}, bf16[2,96,1024]{2,1,0:T(8,128)(2,1)S(1)}, u32[]{:S(2)}, u32[]{:S(2)}) collective-permute-start(bf16[2,96,1024]{2,1,0:T(8,128)(2,1)S(1)} %bitcast.133), channel_id=1, source_target_pairs={{0,12},{1,13},{2,14},{3,15},{4,0},{5,1},{6,2},{7,3},{8,4},{9,5},{1... | collective-permute-start | bytes 1179656 | tf_op jit(solution)/shard_map/reduce_draft/ppermute | solution.py:57
  88.7 3.3 %collective-permute-start.17 = (bf16[2,96,1024]{2,1,0:T(8,128)(2,1)S(1)}, bf16[2,96,1024]{2,1,0:T(8,128)(2,1)S(1)}, u32[]{:S(2)}, u32[]{:S(2)}) collective-permute-start(bf16[2,96,1024]{2,1,0:T(8,128)(2,1)S(1)} %bitcast.131), channel_id=1, source_target_pairs={{0,12},{1,13},{2,14},{3,15},{4,0},{5,1},{6,2},{7,3},{8,4},{9,5},{1... | collective-permute-start | bytes 1179656 | tf_op jit(solution)/shard_map/reduce_draft/ppermute | solution.py:57
  96.0 3.3 %collective-permute-start.19 = (bf16[2,96,1024]{2,1,0:T(8,128)(2,1)S(1)}, bf16[2,96,1024]{2,1,0:T(8,128)(2,1)S(1)}, u32[]{:S(2)}, u32[]{:S(2)}) collective-permute-start(bf16[2,96,1024]{2,1,0:T(8,128)(2,1)S(1)} %add.472), channel_id=1, source_target_pairs={{0,12},{1,13},{2,14},{3,15},{4,0},{5,1},{6,2},{7,3},{8,4},{9,5},{1... | collective-permute-start | bytes 1179656 | tf_op jit(solution)/shard_map/reduce_draft/ppermute | solution.py:57
  102.0 2.5 %collective-permute-done.19 = bf16[2,96,1024]{2,1,0:T(8,128)(2,1)S(1)} collective-permute-done((bf16[2,96,1024]{2,1,0:T(8,128)(2,1)S(1)}, bf16[2,96,1024]{2,1,0:T(8,128)(2,1)S(1)}, u32[]{:S(2)}, u32[]{:S(2)}) %collective-permute-start.19) | collective-permute-done | bytes 393248 | tf_op jit(solution)/shard_map/reduce_draft/ppermute | solution.py:57
  104.7 4.1 %collective-permute-done.16 = bf16[2,96,1024]{2,1,0:T(8,128)(2,1)S(1)} collective-permute-done((bf16[2,96,1024]{2,1,0:T(8,128)(2,1)S(1)}, bf16[2,96,1024]{2,1,0:T(8,128)(2,1)S(1)}, u32[]{:S(2)}, u32[]{:S(2)}) %collective-permute-start.16) | collective-permute-done | bytes 393248 | tf_op jit(solution)/shard_map/reduce_draft/ppermute | solution.py:57
  109.6 7.2 %collective-permute-start.23 = (bf16[96,1024]{1,0:T(8,128)(2,1)S(1)}, bf16[96,1024]{1,0:T(8,128)(2,1)S(1)}, u32[]{:S(2)}, u32[]{:S(2)}) collective-permute-start(bf16[96,1024]{1,0:T(8,128)(2,1)S(1)} %get-tuple-element.80), channel_id=1, source_target_pairs={{0,2},{1,3},{2,0},{3,1},{4,6},{5,7},{6,4},{7,5},{8,10},{9,11},{10,... | collective-permute-start | bytes 589832 | tf_op jit(solution)/shard_map/reduce_draft/ppermute | solution.py:57
  116.9 2.5 %collective-permute-start.22 = (bf16[96,1024]{1,0:T(8,128)(2,1)S(1)}, bf16[96,1024]{1,0:T(8,128)(2,1)S(1)}, u32[]{:S(2)}, u32[]{:S(2)}) collective-permute-start(bf16[96,1024]{1,0:T(8,128)(2,1)S(1)} %get-tuple-element.81), channel_id=1, source_target_pairs={{0,3},{1,0},{2,1},{3,2},{4,7},{5,4},{6,5},{7,6},{8,11},{9,8},{10,9... | collective-permute-start | bytes 589832 | tf_op jit(solution)/shard_map/reduce_draft/ppermute | solution.py:57
  120.4 2.2 %collective-permute-done.23 = bf16[96,1024]{1,0:T(8,128)(2,1)S(1)} collective-permute-done((bf16[96,1024]{1,0:T(8,128)(2,1)S(1)}, bf16[96,1024]{1,0:T(8,128)(2,1)S(1)}, u32[]{:S(2)}, u32[]{:S(2)}) %collective-permute-start.23) | collective-permute-done | bytes 196640 | tf_op jit(solution)/shard_map/reduce_draft/ppermute | solution.py:57
  126.4 3.0 %collective-permute-done.26 = f32[3,96]{1,0:T(4,128)S(1)} collective-permute-done((f32[3,96]{1,0:T(4,128)S(1)}, f32[3,96]{1,0:T(4,128)S(1)}, u32[]{:S(2)}, u32[]{:S(2)}) %collective-permute-start.26) | collective-permute-done | bytes 1184 | tf_op jit(solution)/shard_map/norm/ppermute | solution.py:57
  130.4 4.5 %collective-permute-start.30 = (bf16[96,1024]{1,0:T(8,128)(2,1)S(1)}, bf16[96,1024]{1,0:T(8,128)(2,1)S(1)}, u32[]{:S(2)}, u32[]{:S(2)}) collective-permute-start(bf16[96,1024]{1,0:T(8,128)(2,1)S(1)} %fusion.62), channel_id=1, source_target_pairs={{0,1},{1,2},{2,3},{3,0},{4,5},{5,6},{6,7},{7,4},{8,9},{9,10},{10,1... | collective-permute-start | bytes 589832 | tf_op jit(solution)/shard_map/gather_slope/ppermute | solution.py:57
  134.9 5.7 %collective-permute-start.29 = (bf16[96,1024]{1,0:T(8,128)(2,1)S(1)}, bf16[96,1024]{1,0:T(8,128)(2,1)S(1)}, u32[]{:S(2)}, u32[]{:S(2)}) collective-permute-start(bf16[96,1024]{1,0:T(8,128)(2,1)S(1)} %fusion.62), channel_id=1, source_target_pairs={{0,2},{1,3},{2,0},{3,1},{4,6},{5,7},{6,4},{7,5},{8,10},{9,11},{10,... | collective-permute-start | bytes 589832 | tf_op jit(solution)/shard_map/gather_slope/ppermute | solution.py:57
  140.5 2.2 %collective-permute-start.28 = (bf16[96,1024]{1,0:T(8,128)(2,1)S(1)}, bf16[96,1024]{1,0:T(8,128)(2,1)S(1)}, u32[]{:S(2)}, u32[]{:S(2)}) collective-permute-start(bf16[96,1024]{1,0:T(8,128)(2,1)S(1)} %fusion.62), channel_id=1, source_target_pairs={{0,3},{1,0},{2,1},{3,2},{4,7},{5,4},{6,5},{7,6},{8,11},{9,8},{10,9... | collective-permute-start | bytes 589832 | tf_op jit(solution)/shard_map/gather_slope/ppermute | solution.py:57
  142.8 2.3 %slice.88 = bf16[8,192,1024]{2,1,0:T(8,128)(2,1)S(1)} slice(bf16[8,240,1024]{2,1,0:T(8,128)(2,1)} %bitcast.120), slice={[0:8], [0:192], [0:1024]} | slice | bytes 6291456 | tf_op jit(solution)/shard_map/forward/slice | solution.py:298
  145.1 5.4 %collective-permute-done.29 = bf16[96,1024]{1,0:T(8,128)(2,1)S(1)} collective-permute-done((bf16[96,1024]{1,0:T(8,128)(2,1)S(1)}, bf16[96,1024]{1,0:T(8,128)(2,1)S(1)}, u32[]{:S(2)}, u32[]{:S(2)}) %collective-permute-start.29) | collective-permute-done | bytes 196640 | tf_op jit(solution)/shard_map/gather_slope/ppermute | solution.py:57
  150.7 2.0 %collective-permute-start.32 = (bf16[192,1024]{1,0:T(8,128)(2,1)S(1)}, bf16[192,1024]{1,0:T(8,128)(2,1)S(1)}, u32[]{:S(2)}, u32[]{:S(2)}) collective-permute-start(bf16[192,1024]{1,0:T(8,128)(2,1)S(1)} %pad_maximum_fusion.7), channel_id=1, source_target_pairs={{0,4},{1,5},{2,6},{3,7},{4,8},{5,9},{6,10},{7,11},{8,12},{9,13},{1... | collective-permute-start | bytes 1179656 | tf_op jit(solution)/shard_map/gather_slope/ppermute | solution.py:57
  155.2 3.2 %collective-permute-done.34 = bf16[192,1024]{1,0:T(8,128)(2,1)S(1)} collective-permute-done((bf16[192,1024]{1,0:T(8,128)(2,1)S(1)}, bf16[192,1024]{1,0:T(8,128)(2,1)S(1)}, u32[]{:S(2)}, u32[]{:S(2)}) %collective-permute-start.34) | collective-permute-done | bytes 393248 | tf_op jit(solution)/shard_map/gather_slope/ppermute | solution.py:57
  160.7 2.0 %collective-permute-done.33 = bf16[192,1024]{1,0:T(8,128)(2,1)S(1)} collective-permute-done((bf16[192,1024]{1,0:T(8,128)(2,1)S(1)}, bf16[192,1024]{1,0:T(8,128)(2,1)S(1)}, u32[]{:S(2)}, u32[]{:S(2)}) %collective-permute-start.33) | collective-permute-done | bytes 393248 | tf_op jit(solution)/shard_map/gather_slope/ppermute | solution.py:57
  164.9 2.7 %fusion = f32[1536,1024]{1,0:T(8,128)S(1)} fusion(bf16[192,1536]{1,0:T(8,128)(2,1)S(1)} %get-tuple-element.69, bf16[192,1536]{1,0:T(8,128)(2,1)S(1)} %get-tuple-element.67, bf16[192,1536]{1,0:T(8,128)(2,1)S(1)} %get-tuple-element.66, bf16[192,1536]{1,0:T(8,128)(2,1)S(1)} %get-tuple-element.65, bf16[192,1024]{1,0:T(8,128)(2,1)S(1)} %collective-permute-done.34, ...), kind=kOutput, calls=%fused_computation.21 | convolution fusion | flops 2431647744 | bytes 10223616 | tf_op jit(solution)/shard_map/step/dot_general | solution.py:414
  167.6 1.9 %convolution_add_fusion = f32[1536,1024]{1,0:T(8,128)S(1)} fusion(f32[1536,1024]{1,0:T(8,128)S(1)} %fusion, bf16[192,1536]{1,0:T(8,128)(2,1)S(1)} %get-tuple-element.64, bf16[192,1536]{1,0:T(8,128)(2,1)S(1)} %get-tuple-element.63, bf16[96,1024]{1,0:T(8,128)(2,1)S(1)} %get-tuple-element.78, bf16[96,1024]{1,0:T(8,128)(2,1)S(1)} %get-tuple-element.77, ...), kind=kOutput, calls=%fused_computation.17 | convolution fusion | flops 1215037440 | bytes 14548992 | tf_op jit(solution)/shard_map/step/dot_general | solution.py:414
  171.0 4.0 %subtract_convert_fusion = bf16[1536,1024]{1,0:T(8,128)(2,1)} fusion(f32[1536,1024]{1,0:T(8,128)S(1)} %bitcast.106, f32[1536,1024]{1,0:T(8,128)S(1)} %convolution_add_fusion, bf16[192,1536]{1,0:T(8,128)(2,1)S(1)} %get-tuple-element.68, bf16[192,1536]{1,0:T(8,128)(2,1)S(1)} %get-tuple-element.62, bf16[192,1024]{1,0:T(8,128)(2,1)S(1)} %pad_maximum_fusion.9, ...), kind=kOutput, calls=%fused_computation.16 | convolution fusion | flops 1218183168 | bytes 17694720 | tf_op jit(solution)/shard_map/step/dot_general | solution.py:414
  (190 shorter events, 55.9 us)
Async XLA Ops:
  7.2 70.5 %all-gather.2.cloned.1.call-start = ((), (), s32[]{:S(2)}) async-start(), calls=%async_computation | async-start | bytes 4423680 | tf_op jit(solution)/shard_map/all_gather | solution.py:255
  15.2 15.4 %collective-permute-start = (bf16[2,256,512]{2,1,0:T(8,128)(2,1)S(1)}, bf16[2,256,512]{2,1,0:T(8,128)(2,1)S(1)}, u32[]{:S(2)}, u32[]{:S(2)}) collective-permute-start(bf16[2,256,512]{2,1,0:T(8,128)(2,1)S(1)} %copy-done.20), channel_id=1, source_target_pairs={{0,4},{1,5},{2,6},{3,7},{4,8},{5,9},{6,10},{7,11},{8,12},{9,13},{1... | collective-permute-start | bytes 1572872 | tf_op jit(solution)/shard_map/reduce_down/ppermute | solution.py:57
  17.3 14.7 %collective-permute-start.3 = (bf16[2,256,512]{2,1,0:T(8,128)(2,1)S(1)}, bf16[2,256,512]{2,1,0:T(8,128)(2,1)S(1)}, u32[]{:S(2)}, u32[]{:S(2)}) collective-permute-start(bf16[2,256,512]{2,1,0:T(8,128)(2,1)S(1)} %copy-done.19), channel_id=1, source_target_pairs={{0,12},{1,13},{2,14},{3,15},{4,0},{5,1},{6,2},{7,3},{8,4},{9,5},{1... | collective-permute-start | bytes 1572872 | tf_op jit(solution)/shard_map/reduce_down/ppermute | solution.py:57
  28.6 13.4 %collective-permute-start.2 = (bf16[2,256,512]{2,1,0:T(8,128)(2,1)}, bf16[2,256,512]{2,1,0:T(8,128)(2,1)S(1)}, u32[]{:S(2)}, u32[]{:S(2)}) collective-permute-start(bf16[2,256,512]{2,1,0:T(8,128)(2,1)} %get-tuple-element.41), channel_id=1, source_target_pairs={{0,12},{1,13},{2,14},{3,15},{4,0},{5,1},{6,2},{7,3},{8,4},{9,5},{1... | collective-permute-start | bytes 1572872 | tf_op jit(solution)/shard_map/reduce_down/ppermute | solution.py:57
  31.7 10.5 %collective-permute-start.1 = (bf16[2,256,512]{2,1,0:T(8,128)(2,1)S(1)}, bf16[2,256,512]{2,1,0:T(8,128)(2,1)S(1)}, u32[]{:S(2)}, u32[]{:S(2)}) collective-permute-start(bf16[2,256,512]{2,1,0:T(8,128)(2,1)S(1)} %add.412), channel_id=1, source_target_pairs={{0,4},{1,5},{2,6},{3,7},{4,8},{5,9},{6,10},{7,11},{8,12},{9,13},{1... | collective-permute-start | bytes 1572872 | tf_op jit(solution)/shard_map/reduce_down/ppermute | solution.py:57
  31.9 15.9 %collective-permute-start.5 = (bf16[2,256,512]{2,1,0:T(8,128)(2,1)}, bf16[2,256,512]{2,1,0:T(8,128)(2,1)S(1)}, u32[]{:S(2)}, u32[]{:S(2)}) collective-permute-start(bf16[2,256,512]{2,1,0:T(8,128)(2,1)} %get-tuple-element.45), channel_id=1, source_target_pairs={{0,4},{1,5},{2,6},{3,7},{4,8},{5,9},{6,10},{7,11},{8,12},{9,13},{1... | collective-permute-start | bytes 1572872 | tf_op jit(solution)/shard_map/reduce_down/ppermute | solution.py:57
  33.2 14.7 %collective-permute-start.4 = (bf16[2,256,512]{2,1,0:T(8,128)(2,1)S(1)}, bf16[2,256,512]{2,1,0:T(8,128)(2,1)}, u32[]{:S(2)}, u32[]{:S(2)}) collective-permute-start(bf16[2,256,512]{2,1,0:T(8,128)(2,1)S(1)} %add.415), channel_id=1, source_target_pairs={{0,12},{1,13},{2,14},{3,15},{4,0},{5,1},{6,2},{7,3},{8,4},{9,5},{1... | collective-permute-start | bytes 1572872 | tf_op jit(solution)/shard_map/reduce_down/ppermute | solution.py:57
  51.1 11.7 %collective-permute-start.6 = (bf16[256,512]{1,0:T(8,128)(2,1)}, bf16[256,512]{1,0:T(8,128)(2,1)S(1)}, u32[]{:S(2)}, u32[]{:S(2)}) collective-permute-start(bf16[256,512]{1,0:T(8,128)(2,1)} %get-tuple-element.72), channel_id=1, source_target_pairs={{0,1},{1,2},{2,3},{3,0},{4,5},{5,6},{6,7},{7,4},{8,9},{9,10},{10,1... | collective-permute-start | bytes 786440 | tf_op jit(solution)/shard_map/reduce_down/ppermute | solution.py:57
  52.6 10.4 %collective-permute-start.8 = (bf16[256,512]{1,0:T(8,128)(2,1)}, bf16[256,512]{1,0:T(8,128)(2,1)}, u32[]{:S(2)}, u32[]{:S(2)}) collective-permute-start(bf16[256,512]{1,0:T(8,128)(2,1)} %get-tuple-element.73), channel_id=1, source_target_pairs={{0,2},{1,3},{2,0},{3,1},{4,6},{5,7},{6,4},{7,5},{8,10},{9,11},{10,... | collective-permute-start | bytes 786440 | tf_op jit(solution)/shard_map/reduce_down/ppermute | solution.py:57
  55.5 7.5 %collective-permute-start.7 = (bf16[256,512]{1,0:T(8,128)(2,1)}, bf16[256,512]{1,0:T(8,128)(2,1)}, u32[]{:S(2)}, u32[]{:S(2)}) collective-permute-start(bf16[256,512]{1,0:T(8,128)(2,1)} %get-tuple-element.74), channel_id=1, source_target_pairs={{0,3},{1,0},{2,1},{3,2},{4,7},{5,4},{6,5},{7,6},{8,11},{9,8},{10,9... | collective-permute-start | bytes 786440 | tf_op jit(solution)/shard_map/reduce_down/ppermute | solution.py:57
  64.6 10.4 %collective-permute-start.11 = (bf16[96,512]{1,0:T(8,128)(2,1)S(1)}, bf16[96,512]{1,0:T(8,128)(2,1)S(1)}, u32[]{:S(2)}, u32[]{:S(2)}) collective-permute-start(bf16[96,512]{1,0:T(8,128)(2,1)S(1)} %convolution_convert_fusion.2), channel_id=1, source_target_pairs={{0,32},{1,33},{2,34},{3,35},{4,36},{5,37},{6,38},{7,39},{8,40},{9,... | collective-permute-start | bytes 294920 | tf_op jit(solution)/shard_map/back/ppermute | solution.py:57
  66.1 8.9 %collective-permute-start.10 = (bf16[96,512]{1,0:T(8,128)(2,1)S(1)}, bf16[96,512]{1,0:T(8,128)(2,1)S(1)}, u32[]{:S(2)}, u32[]{:S(2)}) collective-permute-start(bf16[96,512]{1,0:T(8,128)(2,1)S(1)} %convolution_convert_fusion.2), channel_id=1, source_target_pairs={{0,64},{1,65},{2,66},{3,67},{4,68},{5,69},{6,70},{7,71},{8,72},{9,... | collective-permute-start | bytes 294920 | tf_op jit(solution)/shard_map/back/ppermute | solution.py:57
  71.2 16.1 %collective-permute-start.14 = (bf16[96,512]{1,0:T(8,128)(2,1)}, bf16[96,512]{1,0:T(8,128)(2,1)}, u32[]{:S(2)}, u32[]{:S(2)}) collective-permute-start(bf16[96,512]{1,0:T(8,128)(2,1)} %get-tuple-element.92), channel_id=1, source_target_pairs={{0,1},{1,0},{2,20},{3,16},{4,33},{5,32},{6,52},{7,48},{8,65},{9,64... | collective-permute-start | bytes 294920 | tf_op jit(solution)/shard_map/targets/ppermute | solution.py:57
  72.9 14.5 %collective-permute-start.13 = (bf16[96,512]{1,0:T(8,128)(2,1)}, bf16[96,512]{1,0:T(8,128)(2,1)}, u32[]{:S(2)}, u32[]{:S(2)}) collective-permute-start(bf16[96,512]{1,0:T(8,128)(2,1)} %get-tuple-element.93), channel_id=1, source_target_pairs={{0,0},{1,1},{2,16},{3,20},{4,32},{5,33},{6,48},{7,52},{8,64},{9,65... | collective-permute-start | bytes 294920 | tf_op jit(solution)/shard_map/targets/ppermute | solution.py:57
  83.5 12.3 %collective-permute-start.18 = (bf16[2,96,1024]{2,1,0:T(8,128)(2,1)S(1)}, bf16[2,96,1024]{2,1,0:T(8,128)(2,1)S(1)}, u32[]{:S(2)}, u32[]{:S(2)}) collective-permute-start(bf16[2,96,1024]{2,1,0:T(8,128)(2,1)S(1)} %bitcast.133), channel_id=1, source_target_pairs={{0,12},{1,13},{2,14},{3,15},{4,0},{5,1},{6,2},{7,3},{8,4},{9,5},{1... | collective-permute-start | bytes 1179656 | tf_op jit(solution)/shard_map/reduce_draft/ppermute | solution.py:57
  87.3 12.4 %collective-permute-start.15 = (bf16[2,96,1024]{2,1,0:T(8,128)(2,1)S(1)}, bf16[2,96,1024]{2,1,0:T(8,128)(2,1)S(1)}, u32[]{:S(2)}, u32[]{:S(2)}) collective-permute-start(bf16[2,96,1024]{2,1,0:T(8,128)(2,1)S(1)} %bitcast.132), channel_id=1, source_target_pairs={{0,4},{1,5},{2,6},{3,7},{4,8},{5,9},{6,10},{7,11},{8,12},{9,13},{1... | collective-permute-start | bytes 1179656 | tf_op jit(solution)/shard_map/reduce_draft/ppermute | solution.py:57
  88.7 16.0 %collective-permute-start.17 = (bf16[2,96,1024]{2,1,0:T(8,128)(2,1)S(1)}, bf16[2,96,1024]{2,1,0:T(8,128)(2,1)S(1)}, u32[]{:S(2)}, u32[]{:S(2)}) collective-permute-start(bf16[2,96,1024]{2,1,0:T(8,128)(2,1)S(1)} %bitcast.131), channel_id=1, source_target_pairs={{0,12},{1,13},{2,14},{3,15},{4,0},{5,1},{6,2},{7,3},{8,4},{9,5},{1... | collective-permute-start | bytes 1179656 | tf_op jit(solution)/shard_map/reduce_draft/ppermute | solution.py:57
  93.0 9.1 %collective-permute-start.20 = (bf16[2,96,1024]{2,1,0:T(8,128)(2,1)S(1)}, bf16[2,96,1024]{2,1,0:T(8,128)(2,1)S(1)}, u32[]{:S(2)}, u32[]{:S(2)}) collective-permute-start(bf16[2,96,1024]{2,1,0:T(8,128)(2,1)S(1)} %bitcast.134), channel_id=1, source_target_pairs={{0,4},{1,5},{2,6},{3,7},{4,8},{5,9},{6,10},{7,11},{8,12},{9,13},{1... | collective-permute-start | bytes 1179656 | tf_op jit(solution)/shard_map/reduce_draft/ppermute | solution.py:57
  96.0 8.6 %collective-permute-start.19 = (bf16[2,96,1024]{2,1,0:T(8,128)(2,1)S(1)}, bf16[2,96,1024]{2,1,0:T(8,128)(2,1)S(1)}, u32[]{:S(2)}, u32[]{:S(2)}) collective-permute-start(bf16[2,96,1024]{2,1,0:T(8,128)(2,1)S(1)} %add.472), channel_id=1, source_target_pairs={{0,12},{1,13},{2,14},{3,15},{4,0},{5,1},{6,2},{7,3},{8,4},{9,5},{1... | collective-permute-start | bytes 1179656 | tf_op jit(solution)/shard_map/reduce_draft/ppermute | solution.py:57
  99.8 9.1 %collective-permute-start.16 = (bf16[2,96,1024]{2,1,0:T(8,128)(2,1)S(1)}, bf16[2,96,1024]{2,1,0:T(8,128)(2,1)S(1)}, u32[]{:S(2)}, u32[]{:S(2)}) collective-permute-start(bf16[2,96,1024]{2,1,0:T(8,128)(2,1)S(1)} %add.467), channel_id=1, source_target_pairs={{0,4},{1,5},{2,6},{3,7},{4,8},{5,9},{6,10},{7,11},{8,12},{9,13},{1... | collective-permute-start | bytes 1179656 | tf_op jit(solution)/shard_map/reduce_draft/ppermute | solution.py:57
  109.2 11.2 %collective-permute-start.21 = (bf16[96,1024]{1,0:T(8,128)(2,1)S(1)}, bf16[96,1024]{1,0:T(8,128)(2,1)S(1)}, u32[]{:S(2)}, u32[]{:S(2)}) collective-permute-start(bf16[96,1024]{1,0:T(8,128)(2,1)S(1)} %get-tuple-element.79), channel_id=1, source_target_pairs={{0,1},{1,2},{2,3},{3,0},{4,5},{5,6},{6,7},{7,4},{8,9},{9,10},{10,1... | collective-permute-start | bytes 589832 | tf_op jit(solution)/shard_map/reduce_draft/ppermute | solution.py:57
  109.6 12.9 %collective-permute-start.23 = (bf16[96,1024]{1,0:T(8,128)(2,1)S(1)}, bf16[96,1024]{1,0:T(8,128)(2,1)S(1)}, u32[]{:S(2)}, u32[]{:S(2)}) collective-permute-start(bf16[96,1024]{1,0:T(8,128)(2,1)S(1)} %get-tuple-element.80), channel_id=1, source_target_pairs={{0,2},{1,3},{2,0},{3,1},{4,6},{5,7},{6,4},{7,5},{8,10},{9,11},{10,... | collective-permute-start | bytes 589832 | tf_op jit(solution)/shard_map/reduce_draft/ppermute | solution.py:57
  130.4 14.7 %collective-permute-start.30 = (bf16[96,1024]{1,0:T(8,128)(2,1)S(1)}, bf16[96,1024]{1,0:T(8,128)(2,1)S(1)}, u32[]{:S(2)}, u32[]{:S(2)}) collective-permute-start(bf16[96,1024]{1,0:T(8,128)(2,1)S(1)} %fusion.62), channel_id=1, source_target_pairs={{0,1},{1,2},{2,3},{3,0},{4,5},{5,6},{6,7},{7,4},{8,9},{9,10},{10,1... | collective-permute-start | bytes 589832 | tf_op jit(solution)/shard_map/gather_slope/ppermute | solution.py:57
  134.9 15.6 %collective-permute-start.29 = (bf16[96,1024]{1,0:T(8,128)(2,1)S(1)}, bf16[96,1024]{1,0:T(8,128)(2,1)S(1)}, u32[]{:S(2)}, u32[]{:S(2)}) collective-permute-start(bf16[96,1024]{1,0:T(8,128)(2,1)S(1)} %fusion.62), channel_id=1, source_target_pairs={{0,2},{1,3},{2,0},{3,1},{4,6},{5,7},{6,4},{7,5},{8,10},{9,11},{10,... | collective-permute-start | bytes 589832 | tf_op jit(solution)/shard_map/gather_slope/ppermute | solution.py:57
  140.5 10.0 %collective-permute-start.28 = (bf16[96,1024]{1,0:T(8,128)(2,1)S(1)}, bf16[96,1024]{1,0:T(8,128)(2,1)S(1)}, u32[]{:S(2)}, u32[]{:S(2)}) collective-permute-start(bf16[96,1024]{1,0:T(8,128)(2,1)S(1)} %fusion.62), channel_id=1, source_target_pairs={{0,3},{1,0},{2,1},{3,2},{4,7},{5,4},{6,5},{7,6},{8,11},{9,8},{10,9... | collective-permute-start | bytes 589832 | tf_op jit(solution)/shard_map/gather_slope/ppermute | solution.py:57
  150.6 7.8 %collective-permute-start.34 = (bf16[192,1024]{1,0:T(8,128)(2,1)S(1)}, bf16[192,1024]{1,0:T(8,128)(2,1)S(1)}, u32[]{:S(2)}, u32[]{:S(2)}) collective-permute-start(bf16[192,1024]{1,0:T(8,128)(2,1)S(1)} %pad_maximum_fusion.7), channel_id=1, source_target_pairs={{0,12},{1,13},{2,14},{3,15},{4,0},{5,1},{6,2},{7,3},{8,4},{9,5},{1... | collective-permute-start | bytes 1179656 | tf_op jit(solution)/shard_map/gather_slope/ppermute | solution.py:57
  150.7 9.1 %collective-permute-start.32 = (bf16[192,1024]{1,0:T(8,128)(2,1)S(1)}, bf16[192,1024]{1,0:T(8,128)(2,1)S(1)}, u32[]{:S(2)}, u32[]{:S(2)}) collective-permute-start(bf16[192,1024]{1,0:T(8,128)(2,1)S(1)} %pad_maximum_fusion.7), channel_id=1, source_target_pairs={{0,4},{1,5},{2,6},{3,7},{4,8},{5,9},{6,10},{7,11},{8,12},{9,13},{1... | collective-permute-start | bytes 1179656 | tf_op jit(solution)/shard_map/gather_slope/ppermute | solution.py:57
  152.7 9.9 %collective-permute-start.33 = (bf16[192,1024]{1,0:T(8,128)(2,1)S(1)}, bf16[192,1024]{1,0:T(8,128)(2,1)S(1)}, u32[]{:S(2)}, u32[]{:S(2)}) collective-permute-start(bf16[192,1024]{1,0:T(8,128)(2,1)S(1)} %pad_maximum_fusion.6), channel_id=1, source_target_pairs={{0,12},{1,13},{2,14},{3,15},{4,0},{5,1},{6,2},{7,3},{8,4},{9,5},{1... | collective-permute-start | bytes 1179656 | tf_op jit(solution)/shard_map/gather_slope/ppermute | solution.py:57
  154.1 9.9 %collective-permute-start.31 = (bf16[192,1024]{1,0:T(8,128)(2,1)S(1)}, bf16[192,1024]{1,0:T(8,128)(2,1)S(1)}, u32[]{:S(2)}, u32[]{:S(2)}) collective-permute-start(bf16[192,1024]{1,0:T(8,128)(2,1)S(1)} %pad_maximum_fusion.6), channel_id=1, source_target_pairs={{0,4},{1,5},{2,6},{3,7},{4,8},{5,9},{6,10},{7,11},{8,12},{9,13},{1... | collective-permute-start | bytes 1179656 | tf_op jit(solution)/shard_map/gather_slope/ppermute | solution.py:57
  158.5 11.0 %collective-permute-start.38 = (bf16[96,1024]{1,0:T(8,128)(2,1)S(1)}, bf16[96,1024]{1,0:T(8,128)(2,1)S(1)}, u32[]{:S(2)}, u32[]{:S(2)}) collective-permute-start(bf16[96,1024]{1,0:T(8,128)(2,1)S(1)} %slice.101), channel_id=1, source_target_pairs={{0,12},{1,13},{2,14},{3,15},{4,0},{5,1},{6,2},{7,3},{8,4},{9,5},{1... | collective-permute-start | bytes 589832 | tf_op jit(solution)/shard_map/gather_slope/ppermute | solution.py:57
  159.8 9.7 %collective-permute-start.37 = (bf16[96,1024]{1,0:T(8,128)(2,1)S(1)}, bf16[96,1024]{1,0:T(8,128)(2,1)S(1)}, u32[]{:S(2)}, u32[]{:S(2)}) collective-permute-start(bf16[96,1024]{1,0:T(8,128)(2,1)S(1)} %slice.100), channel_id=1, source_target_pairs={{0,4},{1,5},{2,6},{3,7},{4,8},{5,9},{6,10},{7,11},{8,12},{9,13},{1... | collective-permute-start | bytes 589832 | tf_op jit(solution)/shard_map/gather_slope/ppermute | solution.py:57
  164.0 7.0 %collective-permute-start.35 = (bf16[96,1024]{1,0:T(8,128)(2,1)S(1)}, bf16[96,1024]{1,0:T(8,128)(2,1)S(1)}, u32[]{:S(2)}, u32[]{:S(2)}) collective-permute-start(bf16[96,1024]{1,0:T(8,128)(2,1)S(1)} %slice.98), channel_id=1, source_target_pairs={{0,4},{1,5},{2,6},{3,7},{4,8},{5,9},{6,10},{7,11},{8,12},{9,13},{1... | collective-permute-start | bytes 589832 | tf_op jit(solution)/shard_map/gather_slope/ppermute | solution.py:57
  (35 other events, 178.1 us)
Sparse Core Ops, SparseCore 0:
  15.3 33.5 all-gather.1

commit v5 on v2

--- a/solution.py
+++ b/solution.py
@@ -146,12 +146,12 @@
     out_ref[half:] = lower_ref[...].astype(bf16)
 
 
-def rounded_layers(wide, layers, start, after):
+def rounded_pair(wide, after):
     rows, columns = wide.shape
-    step = rows // 3
+    layers, step = 2, rows // 3
 
     def half_layer(half):
-        return pl.BlockSpec((step // 2, columns), lambda i: (2 * (start + i) + half, 0))
+        return pl.BlockSpec((step // 2, columns), lambda i: (2 * i + half, 0))
 
     return pl.pallas_call(
         round_kernel,
@@ -280,8 +280,8 @@
         mixed, first_sum = reduce_blocks(near, direct, own, q)
 
     flat_weight = draft_input_weight.reshape(3 * feature_slice, out_slice)
-    pair_weight = rounded_layers(flat_weight, 2, 0, first_sum)
-    third_weight = rounded_layers(flat_weight, 1, 2, first_sum)
+    pair_weight = rounded_pair(flat_weight, first_sum)
+    third_weight = draft_input_weight[2].astype(bf16)
     upper_layer = (
         stream_input.astype(f32) + mixed.reshape(steps, rows, feature_slice)
     ).astype(bf16)
@@ -333,9 +333,7 @@
         def piece(total, kind):
             return total.astype(kind).reshape(2, slots, out_slice)
 
-        far_pairs = [
-            pair_product(pair_weight, shift, half) for shift in (2, 1, 3) for half in range(2)
-        ]
+        far_pairs = [pair_product(pair_weight, 2, half) for half in range(2)]
         others, fronts, far_pairs, _ = lax.optimization_barrier(
             (others, fronts, far_pairs, posted)
         )
@@ -343,16 +341,28 @@
             [jnp.where(c == 0, chips, others), jnp.where(c == 0, others, chips)], axis=1
         ).reshape(replicas, slots, feature_slice)
         thirds = jnp.concatenate([fronts, backs], axis=1).reshape(-1, feature_slice)
-        near = [
-            piece(far_pairs[half] + third_product(third_weight, 2, half), bf16)
-            for half in range(2)
-        ]
+
+        def far_third(half):
+            chip = (p + 2) % side
+            rows_of = [
+                fronts[replica_of(2, half)],
+                jnp.where(c == half, chips[chip], others[chip]),
+            ]
+            return jnp.dot(
+                jnp.concatenate(rows_of), third_weight, preferred_element_type=f32
+            )
+
+        near = [piece(far_pairs[half] + far_third(half), bf16) for half in range(2)]
         _, got, pair_weight, third_weight = lax.optimization_barrier(
             (near, got, pair_weight, third_weight)
         )
         direct = [
-            piece(far_pairs[2 + k] + third_product(third_weight, (1, 3)[k // 2], k % 2), bf16)
-            for k in range(4)
+            piece(
+                pair_product(pair_weight, shift, half) + third_product(third_weight, shift, half),
+                bf16,
+            )
+            for shift in (1, 3)
+            for half in range(2)
         ]
         _, pair_weight, third_weight = lax.optimization_barrier(
             (direct, pair_weight, third_weight)
@@ -420,13 +430,12 @@
                 preferred_element_type=f32,
             )
 
-        total = product([(0, 0), (0, 1)], [upper_half, lower_half])
+        total = lax.optimization_barrier(product([(0, 0), (0, 1)], [upper_half, lower_half]))
         total = lax.optimization_barrier(
-            total
-            + product(
-                [(3, 0), (3, 1), (1, 0), (1, 1)],
-                [previous_upper, previous_lower, following_upper, following_lower],
-            )
+            total + product([(3, 0), (1, 1)], [previous_upper, following_lower])
+        )
+        total = lax.optimization_barrier(
+            total + product([(3, 1), (1, 0)], [previous_lower, following_upper])
         )
         total = total + product([(2, 0), (2, 1)], [low, high])
         new_weight = (flat_weight - step_rate * total).astype(bf16)

time: 178 us -> 185 us (1.039)
  other arithmetic: 15.7 us -> 23 us
  starting transfers between devices: 64.1 us -> 57.5 us
  matrix products: 19.1 us -> 23.6 us
  waiting for transfers between devices: 26.3 us -> 30.3 us
  Pallas kernels: 27 us -> 24.3 us
    ppermute x37, starting transfers between devices: 64.1 us -> 57.5 us  [send(): return lax.ppermute(array, mesh_axes, pairs)]
    dot_general x3 -> x4, matrix products: 9.59 us -> 13.9 us  [product(): lax.dot_general(jnp.concatenate(inputs), jnp.concatenate(slopes), (((0,),...]
    add x0 -> x1, other arithmetic: none -> 4.13 us  [body(): total + product([(3, 1), (1, 0)], [previous_lower, following_upper])]
    ppermute x37, waiting for transfers between devices: 26.3 us -> 30.2 us  [send(): return lax.ppermute(array, mesh_axes, pairs)]
    pallas_call x2 -> x1, Pallas kernels: 5.89 us -> 3.25 us  [rounded_pair(): pl.pallas_call(round_kernel, grid=(layers,), in_specs=[pl.BlockSpec(memor...]
  transfers between devices with their start and end apart: 38 -> 38, of which waited for: 17 -> 18; matrix products, arithmetic and copies ran while one was open for 18% -> 23% of each run, Pallas kernels for 12% -> 10%
where the time goes in v5:
time: 185 us; the launch traced here: 184 us
  starting transfers between devices  57.5 us (31%)
  waiting for transfers between devices  30.3 us (16%)
  Pallas kernels  24.3 us (13%)
  matrix products  23.6 us (13%)
  other arithmetic  23 us (12%)
  between operations  15.1 us (8%)
  local copies, waits for them, and re-layouts  10.2 us (6%)
    ppermute x37, starting transfers between devices, send(): return lax.ppermute(array, mesh_axes, pairs)  57.5 us
    ppermute x37, waiting for transfers between devices, send(): return lax.ppermute(array, mesh_axes, pairs)  30.2 us
    pallas_call x3, Pallas kernels, down_pieces(): pl.pallas_call(down_kernel, grid_spec=pltpu.PrefetchScalarGridSpec(num_sc...  19.1 us
    dot_general x4, matrix products, product(): lax.dot_general(jnp.concatenate(inputs), jnp.concatenate(slopes), (((0,),...  13.9 us
    dot_general x8, matrix products, pair_product(): return jnp.dot(rows_of, weight, preferred_element_type=f32)  5.81 us
    add x5, other arithmetic, plus(): return functools.reduce(jnp.add, [term.astype(f32) for term in terms])  4.52 us
    add x1, other arithmetic, body(): total + product([(3, 1), (1, 0)], [previous_lower, following_upper])  4.13 us
  transfers between devices with their start and end apart: 38, of which 18 were waited for; matrix products, arithmetic and copies ran while one was open for 23% of the time, Pallas kernels for 10%

profile of v5, /device:TPU:0, one launch (start us, length us, event | category | flops | bytes accessed | tf_op | source)
XLA Modules:
  0.0 184.0 jit_solution(6741348423782653083)
XLA Ops:
  7.8 5.4 %down_projection.3 = (bf16[2,256,512]{2,1,0:T(8,128)(2,1)}, bf16[2,256,512]{2,1,0:T(8,128)(2,1)}) custom-call(s32[4]{0:T(128)} %broadcast_select_fusion.17.blocks_ref, bf16[256,896]{1,0:T(8,128)(2,1)} %bitcast.127, bf16[896,8192]{1,0:T(8,128)(2,1)} %refs_1_.5, bf16[896,8192]{1,0:T(8,128)(2,1)} %refs_1_.5, s32[28,8192]{1,0:T(8,128)} %refs_3_.5, ...), custom_call_target="tpu_custom_call" | custom-call | flops 939524096 | bytes 5505024 | tf_op jit(solution)/shard_map/down/down_projection/pallas_call | solution.py:115
  15.2 2.1 %collective-permute-start = (bf16[2,256,512]{2,1,0:T(8,128)(2,1)S(1)}, bf16[2,256,512]{2,1,0:T(8,128)(2,1)S(1)}, u32[]{:S(2)}, u32[]{:S(2)}) collective-permute-start(bf16[2,256,512]{2,1,0:T(8,128)(2,1)S(1)} %copy-done.17), channel_id=1, source_target_pairs={{0,4},{1,5},{2,6},{3,7},{4,8},{5,9},{6,10},{7,11},{8,12},{9,13},{1... | collective-permute-start | bytes 1572872 | tf_op jit(solution)/shard_map/reduce_down/ppermute | solution.py:57
  17.3 2.2 %collective-permute-start.3 = (bf16[2,256,512]{2,1,0:T(8,128)(2,1)}, bf16[2,256,512]{2,1,0:T(8,128)(2,1)S(1)}, u32[]{:S(2)}, u32[]{:S(2)}) collective-permute-start(bf16[2,256,512]{2,1,0:T(8,128)(2,1)} %get-tuple-element.46), channel_id=1, source_target_pairs={{0,12},{1,13},{2,14},{3,15},{4,0},{5,1},{6,2},{7,3},{8,4},{9,5},{1... | collective-permute-start | bytes 1572872 | tf_op jit(solution)/shard_map/reduce_down/ppermute | solution.py:57
  20.6 8.0 %down_projection.4 = (bf16[2,256,512]{2,1,0:T(8,128)(2,1)}, bf16[2,256,512]{2,1,0:T(8,128)(2,1)}, bf16[2,256,512]{2,1,0:T(8,128)(2,1)}, bf16[2,256,512]{2,1,0:T(8,128)(2,1)}) custom-call(s32[8]{0:T(128)} %pad_add_fusion.1.blocks_ref, bf16[256,896]{1,0:T(8,128)(2,1)} %bitcast.128, bf16[896,8192]{1,0:T(8,128)(2,1)} %refs_1_.5, bf16[896,8192]{1,0:T(8,128)(2,1)} %refs_1_.5, ...), custom_call_target="tpu_custom_call" | custom-call | flops 1879048192 | bytes 11010048 | tf_op jit(solution)/shard_map/down/down_projection/pallas_call | solution.py:115
  28.6 1.9 %collective-permute-start.2 = (bf16[2,256,512]{2,1,0:T(8,128)(2,1)}, bf16[2,256,512]{2,1,0:T(8,128)(2,1)S(1)}, u32[]{:S(2)}, u32[]{:S(2)}) collective-permute-start(bf16[2,256,512]{2,1,0:T(8,128)(2,1)} %get-tuple-element.43), channel_id=1, source_target_pairs={{0,12},{1,13},{2,14},{3,15},{4,0},{5,1},{6,2},{7,3},{8,4},{9,5},{1... | collective-permute-start | bytes 1572872 | tf_op jit(solution)/shard_map/reduce_down/ppermute | solution.py:57
  33.1 3.2 %collective-permute-start.4 = (bf16[2,256,512]{2,1,0:T(8,128)(2,1)S(1)}, bf16[2,256,512]{2,1,0:T(8,128)(2,1)}, u32[]{:S(2)}, u32[]{:S(2)}) collective-permute-start(bf16[2,256,512]{2,1,0:T(8,128)(2,1)S(1)} %add.434), channel_id=1, source_target_pairs={{0,12},{1,13},{2,14},{3,15},{4,0},{5,1},{6,2},{7,3},{8,4},{9,5},{1... | collective-permute-start | bytes 1572872 | tf_op jit(solution)/shard_map/reduce_down/ppermute | solution.py:57
  36.4 5.7 %down_projection.5 = (f32[2,256,512]{2,1,0:T(8,128)}, f32[2,256,512]{2,1,0:T(8,128)}) custom-call(s32[4]{0:T(128)} %get-tuple-element.39.blocks_ref, bf16[256,896]{1,0:T(8,128)(2,1)} %bitcast.129, bf16[896,8192]{1,0:T(8,128)(2,1)} %refs_1_.5, bf16[896,8192]{1,0:T(8,128)(2,1)} %refs_1_.5, s32[28,8192]{1,0:T(8,128)} %refs_3_.5, s32[28,8192]{1,0:T(8,128)} %refs_3_.5), custom_call_target="tpu_custom_call" | custom-call | flops 939524096 | bytes 5505024 | tf_op jit(solution)/shard_map/down/down_projection/pallas_call | solution.py:115
  44.6 3.2 %collective-permute-done.5 = bf16[2,256,512]{2,1,0:T(8,128)(2,1)S(1)} collective-permute-done((bf16[2,256,512]{2,1,0:T(8,128)(2,1)}, bf16[2,256,512]{2,1,0:T(8,128)(2,1)S(1)}, u32[]{:S(2)}, u32[]{:S(2)}) %collective-permute-start.5) | collective-permute-done | bytes 524320 | tf_op jit(solution)/shard_map/reduce_down/ppermute | solution.py:57
  51.1 3.2 %collective-permute-start.8 = (bf16[256,512]{1,0:T(8,128)(2,1)}, bf16[256,512]{1,0:T(8,128)(2,1)S(1)}, u32[]{:S(2)}, u32[]{:S(2)}) collective-permute-start(bf16[256,512]{1,0:T(8,128)(2,1)} %get-tuple-element.77), channel_id=1, source_target_pairs={{0,2},{1,3},{2,0},{3,1},{4,6},{5,7},{6,4},{7,5},{8,10},{9,11},{10,... | collective-permute-start | bytes 786440 | tf_op jit(solution)/shard_map/reduce_down/ppermute | solution.py:57
  58.9 3.2 %round_weight.1 = bf16[1024,1024]{1,0:T(8,128)(2,1)} custom-call(f32[8,128]{1,0:T(8,128)} %slice_bitcast_fusion.2.after_ref, f32[1536,1024]{1,0:T(8,128)} %bitcast.110, f32[1536,1024]{1,0:T(8,128)} %bitcast.111), custom_call_target="tpu_custom_call" | custom-call | flops 1048576 | bytes 6291456 | tf_op jit(solution)/shard_map/round_weight/pallas_call | solution.py:156
  65.4 2.8 %collective-permute-start.9 = (bf16[96,512]{1,0:T(8,128)(2,1)S(1)}, bf16[96,512]{1,0:T(8,128)(2,1)S(1)}, u32[]{:S(2)}, u32[]{:S(2)}) collective-permute-start(bf16[96,512]{1,0:T(8,128)(2,1)S(1)} %convolution_convert_fusion.2), channel_id=1, source_target_pairs={{0,96},{1,97},{2,98},{3,99},{4,100},{5,101},{6,102},{7,103},{8,104... | collective-permute-start | bytes 294920 | tf_op jit(solution)/shard_map/back/ppermute | solution.py:57
  70.8 2.1 %collective-permute-start.13 = (bf16[96,512]{1,0:T(8,128)(2,1)}, bf16[96,512]{1,0:T(8,128)(2,1)}, u32[]{:S(2)}, u32[]{:S(2)}) collective-permute-start(bf16[96,512]{1,0:T(8,128)(2,1)} %get-tuple-element.101), channel_id=1, source_target_pairs={{0,0},{1,1},{2,16},{3,20},{4,32},{5,33},{6,48},{7,52},{8,64},{9,65... | collective-permute-start | bytes 294920 | tf_op jit(solution)/shard_map/targets/ppermute | solution.py:57
  83.0 4.2 %collective-permute-start.18 = (bf16[2,96,1024]{2,1,0:T(8,128)(2,1)S(1)}, bf16[2,96,1024]{2,1,0:T(8,128)(2,1)S(1)}, u32[]{:S(2)}, u32[]{:S(2)}) collective-permute-start(bf16[2,96,1024]{2,1,0:T(8,128)(2,1)S(1)} %bitcast.138), channel_id=1, source_target_pairs={{0,12},{1,13},{2,14},{3,15},{4,0},{5,1},{6,2},{7,3},{8,4},{9,5},{1... | collective-permute-start | bytes 1179656 | tf_op jit(solution)/shard_map/reduce_draft/ppermute | solution.py:57
  90.9 3.1 %collective-permute-start.17 = (bf16[2,96,1024]{2,1,0:T(8,128)(2,1)S(1)}, bf16[2,96,1024]{2,1,0:T(8,128)(2,1)S(1)}, u32[]{:S(2)}, u32[]{:S(2)}) collective-permute-start(bf16[2,96,1024]{2,1,0:T(8,128)(2,1)S(1)} %bitcast.139), channel_id=1, source_target_pairs={{0,12},{1,13},{2,14},{3,15},{4,0},{5,1},{6,2},{7,3},{8,4},{9,5},{1... | collective-permute-start | bytes 1179656 | tf_op jit(solution)/shard_map/reduce_draft/ppermute | solution.py:57
  96.5 2.1 %collective-permute-start.19 = (bf16[2,96,1024]{2,1,0:T(8,128)(2,1)S(1)}, bf16[2,96,1024]{2,1,0:T(8,128)(2,1)S(1)}, u32[]{:S(2)}, u32[]{:S(2)}) collective-permute-start(bf16[2,96,1024]{2,1,0:T(8,128)(2,1)S(1)} %add.492), channel_id=1, source_target_pairs={{0,12},{1,13},{2,14},{3,15},{4,0},{5,1},{6,2},{7,3},{8,4},{9,5},{1... | collective-permute-start | bytes 1179656 | tf_op jit(solution)/shard_map/reduce_draft/ppermute | solution.py:57
  100.9 3.4 %collective-permute-done.19 = bf16[2,96,1024]{2,1,0:T(8,128)(2,1)S(1)} collective-permute-done((bf16[2,96,1024]{2,1,0:T(8,128)(2,1)S(1)}, bf16[2,96,1024]{2,1,0:T(8,128)(2,1)S(1)}, u32[]{:S(2)}, u32[]{:S(2)}) %collective-permute-start.19) | collective-permute-done | bytes 393248 | tf_op jit(solution)/shard_map/reduce_draft/ppermute | solution.py:57
  104.5 3.6 %collective-permute-done.16 = bf16[2,96,1024]{2,1,0:T(8,128)(2,1)S(1)} collective-permute-done((bf16[2,96,1024]{2,1,0:T(8,128)(2,1)S(1)}, bf16[2,96,1024]{2,1,0:T(8,128)(2,1)S(1)}, u32[]{:S(2)}, u32[]{:S(2)}) %collective-permute-start.16) | collective-permute-done | bytes 393248 | tf_op jit(solution)/shard_map/reduce_draft/ppermute | solution.py:57
  108.5 4.1 %collective-permute-start.23 = (bf16[96,1024]{1,0:T(8,128)(2,1)S(1)}, bf16[96,1024]{1,0:T(8,128)(2,1)S(1)}, u32[]{:S(2)}, u32[]{:S(2)}) collective-permute-start(bf16[96,1024]{1,0:T(8,128)(2,1)S(1)} %get-tuple-element.84), channel_id=1, source_target_pairs={{0,2},{1,3},{2,0},{3,1},{4,6},{5,7},{6,4},{7,5},{8,10},{9,11},{10,... | collective-permute-start | bytes 589832 | tf_op jit(solution)/shard_map/reduce_draft/ppermute | solution.py:57
  112.6 2.0 %collective-permute-start.21 = (bf16[96,1024]{1,0:T(8,128)(2,1)S(1)}, bf16[96,1024]{1,0:T(8,128)(2,1)S(1)}, u32[]{:S(2)}, u32[]{:S(2)}) collective-permute-start(bf16[96,1024]{1,0:T(8,128)(2,1)S(1)} %get-tuple-element.83), channel_id=1, source_target_pairs={{0,1},{1,2},{2,3},{3,0},{4,5},{5,6},{6,7},{7,4},{8,9},{9,10},{10,1... | collective-permute-start | bytes 589832 | tf_op jit(solution)/shard_map/reduce_draft/ppermute | solution.py:57
  116.3 2.0 %collective-permute-done.22 = bf16[96,1024]{1,0:T(8,128)(2,1)S(1)} collective-permute-done((bf16[96,1024]{1,0:T(8,128)(2,1)S(1)}, bf16[96,1024]{1,0:T(8,128)(2,1)S(1)}, u32[]{:S(2)}, u32[]{:S(2)}) %collective-permute-start.22) | collective-permute-done | bytes 196640 | tf_op jit(solution)/shard_map/reduce_draft/ppermute | solution.py:57
  124.1 2.4 %slice.72 = bf16[8,192,1024]{2,1,0:T(8,128)(2,1)S(1)} slice(bf16[8,240,1024]{2,1,0:T(8,128)(2,1)} %bitcast.126), slice={[0:8], [0:192], [0:1024]} | slice | bytes 6291456 | tf_op jit(solution)/shard_map/forward/slice | solution.py:313
  129.1 6.5 %collective-permute-start.28 = (bf16[96,1024]{1,0:T(8,128)(2,1)S(1)}, bf16[96,1024]{1,0:T(8,128)(2,1)S(1)}, u32[]{:S(2)}, u32[]{:S(2)}) collective-permute-start(bf16[96,1024]{1,0:T(8,128)(2,1)S(1)} %fusion.61), channel_id=1, source_target_pairs={{0,3},{1,0},{2,1},{3,2},{4,7},{5,4},{6,5},{7,6},{8,11},{9,8},{10,9... | collective-permute-start | bytes 589832 | tf_op jit(solution)/shard_map/gather_slope/ppermute | solution.py:57
  139.3 3.6 %collective-permute-done.29 = bf16[96,1024]{1,0:T(8,128)(2,1)S(1)} collective-permute-done((bf16[96,1024]{1,0:T(8,128)(2,1)S(1)}, bf16[96,1024]{1,0:T(8,128)(2,1)S(1)}, u32[]{:S(2)}, u32[]{:S(2)}) %collective-permute-start.29) | collective-permute-done | bytes 196640 | tf_op jit(solution)/shard_map/gather_slope/ppermute | solution.py:57
  142.9 2.0 %collective-permute-done.30 = bf16[96,1024]{1,0:T(8,128)(2,1)S(1)} collective-permute-done((bf16[96,1024]{1,0:T(8,128)(2,1)S(1)}, bf16[96,1024]{1,0:T(8,128)(2,1)S(1)}, u32[]{:S(2)}, u32[]{:S(2)}) %collective-permute-start.30) | collective-permute-done | bytes 196640 | tf_op jit(solution)/shard_map/gather_slope/ppermute | solution.py:57
  149.0 2.0 %together.1 = (bf16[192,1024]{1,0:T(8,128)(2,1)}, bf16[192,1024]{1,0:T(8,128)(2,1)}) custom-call(bf16[192,1024]{1,0:T(8,128)(2,1)} %copy-done.6, bf16[192,1024]{1,0:T(8,128)(2,1)} %pad_maximum_fusion.7.second_ref), custom_call_target="tpu_custom_call" | custom-call | tf_op jit(solution)/shard_map/gather_slope/together/pallas_call | solution.py:178
  152.9 2.2 %collective-permute-start.34 = (bf16[192,1024]{1,0:T(8,128)(2,1)S(1)}, bf16[192,1024]{1,0:T(8,128)(2,1)S(1)}, u32[]{:S(2)}, u32[]{:S(2)}) collective-permute-start(bf16[192,1024]{1,0:T(8,128)(2,1)S(1)} %copy-done.19), channel_id=1, source_target_pairs={{0,12},{1,13},{2,14},{3,15},{4,0},{5,1},{6,2},{7,3},{8,4},{9,5},{1... | collective-permute-start | bytes 1179656 | tf_op jit(solution)/shard_map/gather_slope/ppermute | solution.py:57
  155.1 3.2 %collective-permute-start.36 = (bf16[192,1024]{1,0:T(8,128)(2,1)}, bf16[192,1024]{1,0:T(8,128)(2,1)}, u32[]{:S(2)}, u32[]{:S(2)}) collective-permute-start(bf16[192,1024]{1,0:T(8,128)(2,1)} %collective-permute-done.32), channel_id=1, source_target_pairs={{0,12},{1,13},{2,14},{3,15},{4,0},{5,1},{6,2},{7,3},{8,4},{9,5},{1... | collective-permute-start | bytes 1179656 | tf_op jit(solution)/shard_map/gather_slope/ppermute | solution.py:57
  158.3 3.1 %convolution_add_fusion = f32[1536,1024]{1,0:T(8,128)S(1)} fusion(f32[1536,1024]{1,0:T(8,128)S(1)} %fusion.6, bf16[192,1536]{1,0:T(8,128)(2,1)S(1)} %get-tuple-element.70, bf16[192,1536]{1,0:T(8,128)(2,1)S(1)} %get-tuple-element.69, bf16[192,1024]{1,0:T(8,128)(2,1)} %collective-permute-done.32, bf16[192,1024]{1,0:T(8,128)(2,1)} %collective-permute-done.31), kind=kOutput, calls=%fused_computation.17 | convolution fusion | flops 1213464576 | bytes 14548992 | tf_op jit(solution)/shard_map/step/dot_general | solution.py:426
  161.5 2.6 %collective-permute-done.33 = bf16[192,1024]{1,0:T(8,128)(2,1)S(1)} collective-permute-done((bf16[192,1024]{1,0:T(8,128)(2,1)S(1)}, bf16[192,1024]{1,0:T(8,128)(2,1)S(1)}, u32[]{:S(2)}, u32[]{:S(2)}) %collective-permute-start.33) | collective-permute-done | bytes 393248 | tf_op jit(solution)/shard_map/gather_slope/ppermute | solution.py:57
  164.0 1.8 fusion.13
  165.9 4.1 %add.505 = f32[1536,1024]{1,0:T(8,128)} add(f32[1536,1024]{1,0:T(8,128)S(1)} %convolution_add_fusion, f32[1536,1024]{1,0:T(8,128)S(1)} %fusion.13) | non-fusion elementwise | flops 1572864 | bytes 18874368 | tf_op jit(solution)/shard_map/step/add | solution.py:438
  170.1 7.1 %subtract_convert_fusion = bf16[1536,1024]{1,0:T(8,128)(2,1)} fusion(f32[1536,1024]{1,0:T(8,128)S(1)} %bitcast.114, f32[1536,1024]{1,0:T(8,128)} %add.505, bf16[192,1536]{1,0:T(8,128)(2,1)} %get-tuple-element.72, bf16[192,1536]{1,0:T(8,128)(2,1)} %get-tuple-element.66, bf16[192,1024]{1,0:T(8,128)(2,1)} %collective-permute-done.36, ...), kind=kOutput, calls=%fused_computation.16 | convolution fusion | flops 1218183168 | bytes 17694720 | tf_op jit(solution)/shard_map/step/dot_general | solution.py:426
  (183 shorter events, 60.6 us)
Async XLA Ops:
  7.2 69.1 %all-gather.2.cloned.1.call-start = ((), (), s32[]{:S(2)}) async-start(), calls=%async_computation | async-start | bytes 4423680 | tf_op jit(solution)/shard_map/all_gather | solution.py:270
  15.2 15.4 %collective-permute-start = (bf16[2,256,512]{2,1,0:T(8,128)(2,1)S(1)}, bf16[2,256,512]{2,1,0:T(8,128)(2,1)S(1)}, u32[]{:S(2)}, u32[]{:S(2)}) collective-permute-start(bf16[2,256,512]{2,1,0:T(8,128)(2,1)S(1)} %copy-done.17), channel_id=1, source_target_pairs={{0,4},{1,5},{2,6},{3,7},{4,8},{5,9},{6,10},{7,11},{8,12},{9,13},{1... | collective-permute-start | bytes 1572872 | tf_op jit(solution)/shard_map/reduce_down/ppermute | solution.py:57
  17.3 14.7 %collective-permute-start.3 = (bf16[2,256,512]{2,1,0:T(8,128)(2,1)}, bf16[2,256,512]{2,1,0:T(8,128)(2,1)S(1)}, u32[]{:S(2)}, u32[]{:S(2)}) collective-permute-start(bf16[2,256,512]{2,1,0:T(8,128)(2,1)} %get-tuple-element.46), channel_id=1, source_target_pairs={{0,12},{1,13},{2,14},{3,15},{4,0},{5,1},{6,2},{7,3},{8,4},{9,5},{1... | collective-permute-start | bytes 1572872 | tf_op jit(solution)/shard_map/reduce_down/ppermute | solution.py:57
  28.6 13.4 %collective-permute-start.2 = (bf16[2,256,512]{2,1,0:T(8,128)(2,1)}, bf16[2,256,512]{2,1,0:T(8,128)(2,1)S(1)}, u32[]{:S(2)}, u32[]{:S(2)}) collective-permute-start(bf16[2,256,512]{2,1,0:T(8,128)(2,1)} %get-tuple-element.43), channel_id=1, source_target_pairs={{0,12},{1,13},{2,14},{3,15},{4,0},{5,1},{6,2},{7,3},{8,4},{9,5},{1... | collective-permute-start | bytes 1572872 | tf_op jit(solution)/shard_map/reduce_down/ppermute | solution.py:57
  31.7 10.5 %collective-permute-start.1 = (bf16[2,256,512]{2,1,0:T(8,128)(2,1)S(1)}, bf16[2,256,512]{2,1,0:T(8,128)(2,1)S(1)}, u32[]{:S(2)}, u32[]{:S(2)}) collective-permute-start(bf16[2,256,512]{2,1,0:T(8,128)(2,1)S(1)} %add.431), channel_id=1, source_target_pairs={{0,4},{1,5},{2,6},{3,7},{4,8},{5,9},{6,10},{7,11},{8,12},{9,13},{1... | collective-permute-start | bytes 1572872 | tf_op jit(solution)/shard_map/reduce_down/ppermute | solution.py:57
  31.9 15.9 %collective-permute-start.5 = (bf16[2,256,512]{2,1,0:T(8,128)(2,1)}, bf16[2,256,512]{2,1,0:T(8,128)(2,1)S(1)}, u32[]{:S(2)}, u32[]{:S(2)}) collective-permute-start(bf16[2,256,512]{2,1,0:T(8,128)(2,1)} %get-tuple-element.47), channel_id=1, source_target_pairs={{0,4},{1,5},{2,6},{3,7},{4,8},{5,9},{6,10},{7,11},{8,12},{9,13},{1... | collective-permute-start | bytes 1572872 | tf_op jit(solution)/shard_map/reduce_down/ppermute | solution.py:57
  33.1 14.7 %collective-permute-start.4 = (bf16[2,256,512]{2,1,0:T(8,128)(2,1)S(1)}, bf16[2,256,512]{2,1,0:T(8,128)(2,1)}, u32[]{:S(2)}, u32[]{:S(2)}) collective-permute-start(bf16[2,256,512]{2,1,0:T(8,128)(2,1)S(1)} %add.434), channel_id=1, source_target_pairs={{0,12},{1,13},{2,14},{3,15},{4,0},{5,1},{6,2},{7,3},{8,4},{9,5},{1... | collective-permute-start | bytes 1572872 | tf_op jit(solution)/shard_map/reduce_down/ppermute | solution.py:57
  51.1 11.1 %collective-permute-start.8 = (bf16[256,512]{1,0:T(8,128)(2,1)}, bf16[256,512]{1,0:T(8,128)(2,1)S(1)}, u32[]{:S(2)}, u32[]{:S(2)}) collective-permute-start(bf16[256,512]{1,0:T(8,128)(2,1)} %get-tuple-element.77), channel_id=1, source_target_pairs={{0,2},{1,3},{2,0},{3,1},{4,6},{5,7},{6,4},{7,5},{8,10},{9,11},{10,... | collective-permute-start | bytes 786440 | tf_op jit(solution)/shard_map/reduce_down/ppermute | solution.py:57
  54.2 8.2 %collective-permute-start.7 = (bf16[256,512]{1,0:T(8,128)(2,1)}, bf16[256,512]{1,0:T(8,128)(2,1)}, u32[]{:S(2)}, u32[]{:S(2)}) collective-permute-start(bf16[256,512]{1,0:T(8,128)(2,1)} %get-tuple-element.78), channel_id=1, source_target_pairs={{0,3},{1,0},{2,1},{3,2},{4,7},{5,4},{6,5},{7,6},{8,11},{9,8},{10,9... | collective-permute-start | bytes 786440 | tf_op jit(solution)/shard_map/reduce_down/ppermute | solution.py:57
  55.3 7.9 %collective-permute-start.6 = (bf16[256,512]{1,0:T(8,128)(2,1)}, bf16[256,512]{1,0:T(8,128)(2,1)}, u32[]{:S(2)}, u32[]{:S(2)}) collective-permute-start(bf16[256,512]{1,0:T(8,128)(2,1)} %get-tuple-element.76), channel_id=1, source_target_pairs={{0,1},{1,2},{2,3},{3,0},{4,5},{5,6},{6,7},{7,4},{8,9},{9,10},{10,1... | collective-permute-start | bytes 786440 | tf_op jit(solution)/shard_map/reduce_down/ppermute | solution.py:57
  65.4 8.1 %collective-permute-start.9 = (bf16[96,512]{1,0:T(8,128)(2,1)S(1)}, bf16[96,512]{1,0:T(8,128)(2,1)S(1)}, u32[]{:S(2)}, u32[]{:S(2)}) collective-permute-start(bf16[96,512]{1,0:T(8,128)(2,1)S(1)} %convolution_convert_fusion.2), channel_id=1, source_target_pairs={{0,96},{1,97},{2,98},{3,99},{4,100},{5,101},{6,102},{7,103},{8,104... | collective-permute-start | bytes 294920 | tf_op jit(solution)/shard_map/back/ppermute | solution.py:57
  68.2 6.2 %collective-permute-start.10 = (bf16[96,512]{1,0:T(8,128)(2,1)S(1)}, bf16[96,512]{1,0:T(8,128)(2,1)S(1)}, u32[]{:S(2)}, u32[]{:S(2)}) collective-permute-start(bf16[96,512]{1,0:T(8,128)(2,1)S(1)} %convolution_convert_fusion.2), channel_id=1, source_target_pairs={{0,64},{1,65},{2,66},{3,67},{4,68},{5,69},{6,70},{7,71},{8,72},{9,... | collective-permute-start | bytes 294920 | tf_op jit(solution)/shard_map/back/ppermute | solution.py:57
  69.0 6.4 %collective-permute-start.11 = (bf16[96,512]{1,0:T(8,128)(2,1)S(1)}, bf16[96,512]{1,0:T(8,128)(2,1)S(1)}, u32[]{:S(2)}, u32[]{:S(2)}) collective-permute-start(bf16[96,512]{1,0:T(8,128)(2,1)S(1)} %convolution_convert_fusion.2), channel_id=1, source_target_pairs={{0,32},{1,33},{2,34},{3,35},{4,36},{5,37},{6,38},{7,39},{8,40},{9,... | collective-permute-start | bytes 294920 | tf_op jit(solution)/shard_map/back/ppermute | solution.py:57
  70.8 17.0 %collective-permute-start.13 = (bf16[96,512]{1,0:T(8,128)(2,1)}, bf16[96,512]{1,0:T(8,128)(2,1)}, u32[]{:S(2)}, u32[]{:S(2)}) collective-permute-start(bf16[96,512]{1,0:T(8,128)(2,1)} %get-tuple-element.101), channel_id=1, source_target_pairs={{0,0},{1,1},{2,16},{3,20},{4,32},{5,33},{6,48},{7,52},{8,64},{9,65... | collective-permute-start | bytes 294920 | tf_op jit(solution)/shard_map/targets/ppermute | solution.py:57
  73.0 14.9 %collective-permute-start.14 = (bf16[96,512]{1,0:T(8,128)(2,1)}, bf16[96,512]{1,0:T(8,128)(2,1)}, u32[]{:S(2)}, u32[]{:S(2)}) collective-permute-start(bf16[96,512]{1,0:T(8,128)(2,1)} %get-tuple-element.100), channel_id=1, source_target_pairs={{0,1},{1,0},{2,20},{3,16},{4,33},{5,32},{6,52},{7,48},{8,65},{9,64... | collective-permute-start | bytes 294920 | tf_op jit(solution)/shard_map/targets/ppermute | solution.py:57
  83.0 13.3 %collective-permute-start.18 = (bf16[2,96,1024]{2,1,0:T(8,128)(2,1)S(1)}, bf16[2,96,1024]{2,1,0:T(8,128)(2,1)S(1)}, u32[]{:S(2)}, u32[]{:S(2)}) collective-permute-start(bf16[2,96,1024]{2,1,0:T(8,128)(2,1)S(1)} %bitcast.138), channel_id=1, source_target_pairs={{0,12},{1,13},{2,14},{3,15},{4,0},{5,1},{6,2},{7,3},{8,4},{9,5},{1... | collective-permute-start | bytes 1179656 | tf_op jit(solution)/shard_map/reduce_draft/ppermute | solution.py:57
  87.7 11.3 %collective-permute-start.15 = (bf16[2,96,1024]{2,1,0:T(8,128)(2,1)S(1)}, bf16[2,96,1024]{2,1,0:T(8,128)(2,1)S(1)}, u32[]{:S(2)}, u32[]{:S(2)}) collective-permute-start(bf16[2,96,1024]{2,1,0:T(8,128)(2,1)S(1)} %bitcast.137), channel_id=1, source_target_pairs={{0,4},{1,5},{2,6},{3,7},{4,8},{5,9},{6,10},{7,11},{8,12},{9,13},{1... | collective-permute-start | bytes 1179656 | tf_op jit(solution)/shard_map/reduce_draft/ppermute | solution.py:57
  88.9 12.1 %collective-permute-start.20 = (bf16[2,96,1024]{2,1,0:T(8,128)(2,1)S(1)}, bf16[2,96,1024]{2,1,0:T(8,128)(2,1)S(1)}, u32[]{:S(2)}, u32[]{:S(2)}) collective-permute-start(bf16[2,96,1024]{2,1,0:T(8,128)(2,1)S(1)} %bitcast.140), channel_id=1, source_target_pairs={{0,4},{1,5},{2,6},{3,7},{4,8},{5,9},{6,10},{7,11},{8,12},{9,13},{1... | collective-permute-start | bytes 1179656 | tf_op jit(solution)/shard_map/reduce_draft/ppermute | solution.py:57
  90.9 13.6 %collective-permute-start.17 = (bf16[2,96,1024]{2,1,0:T(8,128)(2,1)S(1)}, bf16[2,96,1024]{2,1,0:T(8,128)(2,1)S(1)}, u32[]{:S(2)}, u32[]{:S(2)}) collective-permute-start(bf16[2,96,1024]{2,1,0:T(8,128)(2,1)S(1)} %bitcast.139), channel_id=1, source_target_pairs={{0,12},{1,13},{2,14},{3,15},{4,0},{5,1},{6,2},{7,3},{8,4},{9,5},{1... | collective-permute-start | bytes 1179656 | tf_op jit(solution)/shard_map/reduce_draft/ppermute | solution.py:57
  96.5 7.8 %collective-permute-start.19 = (bf16[2,96,1024]{2,1,0:T(8,128)(2,1)S(1)}, bf16[2,96,1024]{2,1,0:T(8,128)(2,1)S(1)}, u32[]{:S(2)}, u32[]{:S(2)}) collective-permute-start(bf16[2,96,1024]{2,1,0:T(8,128)(2,1)S(1)} %add.492), channel_id=1, source_target_pairs={{0,12},{1,13},{2,14},{3,15},{4,0},{5,1},{6,2},{7,3},{8,4},{9,5},{1... | collective-permute-start | bytes 1179656 | tf_op jit(solution)/shard_map/reduce_draft/ppermute | solution.py:57
  99.1 9.1 %collective-permute-start.16 = (bf16[2,96,1024]{2,1,0:T(8,128)(2,1)S(1)}, bf16[2,96,1024]{2,1,0:T(8,128)(2,1)S(1)}, u32[]{:S(2)}, u32[]{:S(2)}) collective-permute-start(bf16[2,96,1024]{2,1,0:T(8,128)(2,1)S(1)} %add.487), channel_id=1, source_target_pairs={{0,4},{1,5},{2,6},{3,7},{4,8},{5,9},{6,10},{7,11},{8,12},{9,13},{1... | collective-permute-start | bytes 1179656 | tf_op jit(solution)/shard_map/reduce_draft/ppermute | solution.py:57
  108.5 7.8 %collective-permute-start.23 = (bf16[96,1024]{1,0:T(8,128)(2,1)S(1)}, bf16[96,1024]{1,0:T(8,128)(2,1)S(1)}, u32[]{:S(2)}, u32[]{:S(2)}) collective-permute-start(bf16[96,1024]{1,0:T(8,128)(2,1)S(1)} %get-tuple-element.84), channel_id=1, source_target_pairs={{0,2},{1,3},{2,0},{3,1},{4,6},{5,7},{6,4},{7,5},{8,10},{9,11},{10,... | collective-permute-start | bytes 589832 | tf_op jit(solution)/shard_map/reduce_draft/ppermute | solution.py:57
  112.6 6.9 %collective-permute-start.21 = (bf16[96,1024]{1,0:T(8,128)(2,1)S(1)}, bf16[96,1024]{1,0:T(8,128)(2,1)S(1)}, u32[]{:S(2)}, u32[]{:S(2)}) collective-permute-start(bf16[96,1024]{1,0:T(8,128)(2,1)S(1)} %get-tuple-element.83), channel_id=1, source_target_pairs={{0,1},{1,2},{2,3},{3,0},{4,5},{5,6},{6,7},{7,4},{8,9},{9,10},{10,1... | collective-permute-start | bytes 589832 | tf_op jit(solution)/shard_map/reduce_draft/ppermute | solution.py:57
  129.1 10.2 %collective-permute-start.28 = (bf16[96,1024]{1,0:T(8,128)(2,1)S(1)}, bf16[96,1024]{1,0:T(8,128)(2,1)S(1)}, u32[]{:S(2)}, u32[]{:S(2)}) collective-permute-start(bf16[96,1024]{1,0:T(8,128)(2,1)S(1)} %fusion.61), channel_id=1, source_target_pairs={{0,3},{1,0},{2,1},{3,2},{4,7},{5,4},{6,5},{7,6},{8,11},{9,8},{10,9... | collective-permute-start | bytes 589832 | tf_op jit(solution)/shard_map/gather_slope/ppermute | solution.py:57
  135.6 7.3 %collective-permute-start.29 = (bf16[96,1024]{1,0:T(8,128)(2,1)S(1)}, bf16[96,1024]{1,0:T(8,128)(2,1)S(1)}, u32[]{:S(2)}, u32[]{:S(2)}) collective-permute-start(bf16[96,1024]{1,0:T(8,128)(2,1)S(1)} %fusion.61), channel_id=1, source_target_pairs={{0,2},{1,3},{2,0},{3,1},{4,6},{5,7},{6,4},{7,5},{8,10},{9,11},{10,... | collective-permute-start | bytes 589832 | tf_op jit(solution)/shard_map/gather_slope/ppermute | solution.py:57
  136.7 8.2 %collective-permute-start.30 = (bf16[96,1024]{1,0:T(8,128)(2,1)S(1)}, bf16[96,1024]{1,0:T(8,128)(2,1)S(1)}, u32[]{:S(2)}, u32[]{:S(2)}) collective-permute-start(bf16[96,1024]{1,0:T(8,128)(2,1)S(1)} %fusion.61), channel_id=1, source_target_pairs={{0,1},{1,2},{2,3},{3,0},{4,5},{5,6},{6,7},{7,4},{8,9},{9,10},{10,1... | collective-permute-start | bytes 589832 | tf_op jit(solution)/shard_map/gather_slope/ppermute | solution.py:57
  145.7 9.3 %collective-permute-start.32 = (bf16[192,1024]{1,0:T(8,128)(2,1)}, bf16[192,1024]{1,0:T(8,128)(2,1)}, u32[]{:S(2)}, u32[]{:S(2)}) collective-permute-start(bf16[192,1024]{1,0:T(8,128)(2,1)} %pad_maximum_fusion.7.second_ref), channel_id=1, source_target_pairs={{0,12},{1,13},{2,14},{3,15},{4,0},{5,1},{6,2},{7,3},{8,4},{9,5},{1... | collective-permute-start | bytes 1179656 | tf_op jit(solution)/shard_map/gather_slope/ppermute | solution.py:57
  146.7 11.6 %collective-permute-start.31 = (bf16[192,1024]{1,0:T(8,128)(2,1)S(1)}, bf16[192,1024]{1,0:T(8,128)(2,1)}, u32[]{:S(2)}, u32[]{:S(2)}) collective-permute-start(bf16[192,1024]{1,0:T(8,128)(2,1)S(1)} %pad_maximum_fusion.6.first_ref), channel_id=1, source_target_pairs={{0,4},{1,5},{2,6},{3,7},{4,8},{5,9},{6,10},{7,11},{8,12},{9,13},{1... | collective-permute-start | bytes 1179656 | tf_op jit(solution)/shard_map/gather_slope/ppermute | solution.py:57
  152.9 8.6 %collective-permute-start.34 = (bf16[192,1024]{1,0:T(8,128)(2,1)S(1)}, bf16[192,1024]{1,0:T(8,128)(2,1)S(1)}, u32[]{:S(2)}, u32[]{:S(2)}) collective-permute-start(bf16[192,1024]{1,0:T(8,128)(2,1)S(1)} %copy-done.19), channel_id=1, source_target_pairs={{0,12},{1,13},{2,14},{3,15},{4,0},{5,1},{6,2},{7,3},{8,4},{9,5},{1... | collective-permute-start | bytes 1179656 | tf_op jit(solution)/shard_map/gather_slope/ppermute | solution.py:57
  155.0 9.0 %collective-permute-start.33 = (bf16[192,1024]{1,0:T(8,128)(2,1)S(1)}, bf16[192,1024]{1,0:T(8,128)(2,1)S(1)}, u32[]{:S(2)}, u32[]{:S(2)}) collective-permute-start(bf16[192,1024]{1,0:T(8,128)(2,1)S(1)} %copy-done.18), channel_id=1, source_target_pairs={{0,4},{1,5},{2,6},{3,7},{4,8},{5,9},{6,10},{7,11},{8,12},{9,13},{1... | collective-permute-start | bytes 1179656 | tf_op jit(solution)/shard_map/gather_slope/ppermute | solution.py:57
  155.1 15.0 %collective-permute-start.36 = (bf16[192,1024]{1,0:T(8,128)(2,1)}, bf16[192,1024]{1,0:T(8,128)(2,1)}, u32[]{:S(2)}, u32[]{:S(2)}) collective-permute-start(bf16[192,1024]{1,0:T(8,128)(2,1)} %collective-permute-done.32), channel_id=1, source_target_pairs={{0,12},{1,13},{2,14},{3,15},{4,0},{5,1},{6,2},{7,3},{8,4},{9,5},{1... | collective-permute-start | bytes 1179656 | tf_op jit(solution)/shard_map/gather_slope/ppermute | solution.py:57
  158.3 11.7 %collective-permute-start.35 = (bf16[192,1024]{1,0:T(8,128)(2,1)}, bf16[192,1024]{1,0:T(8,128)(2,1)S(1)}, u32[]{:S(2)}, u32[]{:S(2)}) collective-permute-start(bf16[192,1024]{1,0:T(8,128)(2,1)} %collective-permute-done.31), channel_id=1, source_target_pairs={{0,4},{1,5},{2,6},{3,7},{4,8},{5,9},{6,10},{7,11},{8,12},{9,13},{1... | collective-permute-start | bytes 1179656 | tf_op jit(solution)/shard_map/gather_slope/ppermute | solution.py:57
  (32 other events, 159.4 us)
Sparse Core Ops, SparseCore 0:
  15.3 33.5 all-gather.1

commit v6 on v2

--- a/solution.py
+++ b/solution.py
@@ -87,7 +87,7 @@
 
 
 def down_kernel(blocks_ref, tokens_ref, *refs):
-    coded_refs, exponent_refs, pieces = refs[:2], refs[2:4], refs[4:]
+    coded_refs, exponent_refs, pieces = refs[:side], refs[side : 2 * side], refs[2 * side :]
     i = pl.program_id(0)
     totals = []
     for coded_ref, exponent_ref in zip(coded_refs, exponent_refs):
@@ -98,10 +98,10 @@
         totals.append(jnp.dot(tokens_ref[...], weight, preferred_element_type=f32))
     for k, piece in enumerate(pieces):
 
-        @pl.when(i == k)
+        @pl.when(i == k // 2)
         def _():
-            for half, total in enumerate(totals):
-                piece[half] = total.astype(piece.dtype)
+            for half in range(2):
+                piece[half] = totals[k % 2 * 2 + half].astype(piece.dtype)
 
 
 def down_pieces(blocks, tokens, coded_weight, block_exponent, kind):
@@ -109,21 +109,17 @@
     width = coded_weight.shape[1] // (side * side)
     count = blocks.shape[0]
 
-    def column_block(height, half):
-        return pl.BlockSpec((height, width), lambda i, blocks: (0, blocks[2 * i + half]))
+    def column_block(height, turn):
+        return pl.BlockSpec((height, width), lambda i, blocks: (0, blocks[side * i + turn]))
 
     return pl.pallas_call(
         down_kernel,
         grid_spec=pltpu.PrefetchScalarGridSpec(
             num_scalar_prefetch=1,
-            grid=(count // 2,),
-            in_specs=[
-                pl.BlockSpec((rows, units), lambda i, blocks: (0, 0)),
-                column_block(units, 0),
-                column_block(units, 1),
-                column_block(units // block_units, 0),
-                column_block(units // block_units, 1),
-            ],
+            grid=(count // side,),
+            in_specs=[pl.BlockSpec((rows, units), lambda i, blocks: (0, 0))]
+            + [column_block(units, turn) for turn in range(side)]
+            + [column_block(units // block_units, turn) for turn in range(side)],
             out_specs=[
                 pl.BlockSpec((2, rows, width), lambda i, blocks: (0, 0, 0))
                 for _ in range(count // 2)
@@ -137,7 +133,7 @@
             transcendentals=0,
         ),
         name="down_projection",
-    )(blocks, tokens, coded_weight, coded_weight, block_exponent, block_exponent)
+    )(blocks, tokens, *[coded_weight] * side, *[block_exponent] * side)
 
 
 def round_kernel(after_ref, upper_ref, lower_ref, out_ref):
@@ -146,12 +142,12 @@
     out_ref[half:] = lower_ref[...].astype(bf16)
 
 
-def rounded_layers(wide, layers, start, after):
+def rounded_pair(wide, after):
     rows, columns = wide.shape
-    step = rows // 3
+    layers, step = 2, rows // 3
 
     def half_layer(half):
-        return pl.BlockSpec((step // 2, columns), lambda i: (2 * (start + i) + half, 0))
+        return pl.BlockSpec((step // 2, columns), lambda i: (2 * i + half, 0))
 
     return pl.pallas_call(
         round_kernel,
@@ -280,8 +276,8 @@
         mixed, first_sum = reduce_blocks(near, direct, own, q)
 
     flat_weight = draft_input_weight.reshape(3 * feature_slice, out_slice)
-    pair_weight = rounded_layers(flat_weight, 2, 0, first_sum)
-    third_weight = rounded_layers(flat_weight, 1, 2, first_sum)
+    pair_weight = rounded_pair(flat_weight, first_sum)
+    third_weight = draft_input_weight[2].astype(bf16)
     upper_layer = (
         stream_input.astype(f32) + mixed.reshape(steps, rows, feature_slice)
     ).astype(bf16)

time: 178 us -> 180 us (1.011)
  other arithmetic: 15.7 us -> 19.7 us
  Pallas kernels: 27 us -> 23.4 us
    pallas_call x2 -> x1, Pallas kernels: 5.89 us -> 3.25 us  [rounded_pair(): pl.pallas_call(round_kernel, grid=(layers,), in_specs=[pl.BlockSpec(memor...]
    unnamed x52 -> x54, local copies, waits for them, and re-layouts: 4.48 us -> 3.33 us
  transfers between devices with their start and end apart: 38 -> 38, of which waited for: 17 -> 17; matrix products, arithmetic and copies ran while one was open for 18% -> 21% of each run, Pallas kernels for 12% -> 10%
where the time goes in v6:
time: 180 us; the launch traced here: 179 us
  starting transfers between devices  64.8 us (36%)
  waiting for transfers between devices  26.3 us (15%)
  Pallas kernels  23.4 us (13%)
  other arithmetic  19.7 us (11%)
  matrix products  19.1 us (11%)
  between operations  15.2 us (8%)
  local copies, waits for them, and re-layouts  10.4 us (6%)
    ppermute x37, starting transfers between devices, send(): return lax.ppermute(array, mesh_axes, pairs)  64.7 us
    ppermute x37, waiting for transfers between devices, send(): return lax.ppermute(array, mesh_axes, pairs)  26.2 us
    pallas_call x3, Pallas kernels, down_pieces(): pl.pallas_call(down_kernel, grid_spec=pltpu.PrefetchScalarGridSpec(num_sc...  18.2 us
    dot_general x3, matrix products, product(): lax.dot_general(jnp.concatenate(inputs), jnp.concatenate(slopes), (((0,),...  9.59 us
    dot_general x8, matrix products, pair_product(): return jnp.dot(rows_of, weight, preferred_element_type=f32)  5.72 us
    add x5, other arithmetic, plus(): return functools.reduce(jnp.add, [term.astype(f32) for term in terms])  4.57 us
  transfers between devices with their start and end apart: 38, of which 17 were waited for; matrix products, arithmetic and copies ran while one was open for 21% of the time, Pallas kernels for 10%

profile of v6, /device:TPU:0, one launch (start us, length us, event | category | flops | bytes accessed | tf_op | source)
XLA Modules:
  0.0 178.9 jit_solution(18438926626313166466)
XLA Ops:
  7.8 5.1 %down_projection.3 = (bf16[2,256,512]{2,1,0:T(8,128)(2,1)}, bf16[2,256,512]{2,1,0:T(8,128)(2,1)}) custom-call(s32[4]{0:T(128)} %broadcast_select_fusion.17.blocks_ref, bf16[256,896]{1,0:T(8,128)(2,1)} %bitcast.121, bf16[896,8192]{1,0:T(8,128)(2,1)} %refs_3_.5, bf16[896,8192]{1,0:T(8,128)(2,1)} %refs_3_.5, bf16[896,8192]{1,0:T(8,128)(2,1)} %refs_3_.5, ...), custom_call_target="tpu_custom_call" | custom-call | flops 939524096 | bytes 5505024 | tf_op jit(solution)/shard_map/down/down_projection/pallas_call | solution.py:115
  14.9 4.2 %collective-permute-start.3 = (bf16[2,256,512]{2,1,0:T(8,128)(2,1)S(1)}, bf16[2,256,512]{2,1,0:T(8,128)(2,1)S(1)}, u32[]{:S(2)}, u32[]{:S(2)}) collective-permute-start(bf16[2,256,512]{2,1,0:T(8,128)(2,1)S(1)} %copy-done.20), channel_id=1, source_target_pairs={{0,12},{1,13},{2,14},{3,15},{4,0},{5,1},{6,2},{7,3},{8,4},{9,5},{1... | collective-permute-start | bytes 1572872 | tf_op jit(solution)/shard_map/reduce_down/ppermute | solution.py:57
  20.3 7.8 %down_projection.4 = (bf16[2,256,512]{2,1,0:T(8,128)(2,1)}, bf16[2,256,512]{2,1,0:T(8,128)(2,1)}, bf16[2,256,512]{2,1,0:T(8,128)(2,1)}, bf16[2,256,512]{2,1,0:T(8,128)(2,1)}) custom-call(s32[8]{0:T(128)} %pad_add_fusion.1.blocks_ref, bf16[256,896]{1,0:T(8,128)(2,1)} %bitcast.122, bf16[896,8192]{1,0:T(8,128)(2,1)} %refs_3_.5, bf16[896,8192]{1,0:T(8,128)(2,1)} %refs_3_.5, ...), custom_call_target="tpu_custom_call" | custom-call | flops 1879048192 | bytes 11010048 | tf_op jit(solution)/shard_map/down/down_projection/pallas_call | solution.py:115
  29.3 3.4 %collective-permute-start.4 = (bf16[2,256,512]{2,1,0:T(8,128)(2,1)S(1)}, bf16[2,256,512]{2,1,0:T(8,128)(2,1)S(1)}, u32[]{:S(2)}, u32[]{:S(2)}) collective-permute-start(bf16[2,256,512]{2,1,0:T(8,128)(2,1)S(1)} %add.415), channel_id=1, source_target_pairs={{0,12},{1,13},{2,14},{3,15},{4,0},{5,1},{6,2},{7,3},{8,4},{9,5},{1... | collective-permute-start | bytes 1572872 | tf_op jit(solution)/shard_map/reduce_down/ppermute | solution.py:57
  32.7 2.0 %collective-permute-start.2 = (bf16[2,256,512]{2,1,0:T(8,128)(2,1)}, bf16[2,256,512]{2,1,0:T(8,128)(2,1)S(1)}, u32[]{:S(2)}, u32[]{:S(2)}) collective-permute-start(bf16[2,256,512]{2,1,0:T(8,128)(2,1)} %get-tuple-element.47), channel_id=1, source_target_pairs={{0,12},{1,13},{2,14},{3,15},{4,0},{5,1},{6,2},{7,3},{8,4},{9,5},{1... | collective-permute-start | bytes 1572872 | tf_op jit(solution)/shard_map/reduce_down/ppermute | solution.py:57
  36.0 5.3 %down_projection.5 = (f32[2,256,512]{2,1,0:T(8,128)}, f32[2,256,512]{2,1,0:T(8,128)}) custom-call(s32[4]{0:T(128)} %get-tuple-element.43.blocks_ref, bf16[256,896]{1,0:T(8,128)(2,1)} %bitcast.123, bf16[896,8192]{1,0:T(8,128)(2,1)} %refs_3_.5, bf16[896,8192]{1,0:T(8,128)(2,1)} %refs_3_.5, bf16[896,8192]{1,0:T(8,128)(2,1)} %refs_3_.5, ...), custom_call_target="tpu_custom_call" | custom-call | flops 939524096 | bytes 5505024 | tf_op jit(solution)/shard_map/down/down_projection/pallas_call | solution.py:115
  52.1 2.0 %collective-permute-start.8 = (bf16[256,512]{1,0:T(8,128)(2,1)}, bf16[256,512]{1,0:T(8,128)(2,1)}, u32[]{:S(2)}, u32[]{:S(2)}) collective-permute-start(bf16[256,512]{1,0:T(8,128)(2,1)} %get-tuple-element.85), channel_id=1, source_target_pairs={{0,2},{1,3},{2,0},{3,1},{4,6},{5,7},{6,4},{7,5},{8,10},{9,11},{10,... | collective-permute-start | bytes 786440 | tf_op jit(solution)/shard_map/reduce_down/ppermute | solution.py:57
  54.1 1.7 fusion.23
  56.8 3.2 %round_weight.1 = bf16[1024,1024]{1,0:T(8,128)(2,1)} custom-call(f32[8,128]{1,0:T(8,128)} %slice_bitcast_fusion.2.after_ref, f32[1536,1024]{1,0:T(8,128)} %bitcast.102, f32[1536,1024]{1,0:T(8,128)} %bitcast.103), custom_call_target="tpu_custom_call" | custom-call | flops 1048576 | bytes 6291456 | tf_op jit(solution)/shard_map/round_weight/pallas_call | solution.py:152
  63.0 3.1 %collective-permute-start.10 = (bf16[96,512]{1,0:T(8,128)(2,1)S(1)}, bf16[96,512]{1,0:T(8,128)(2,1)S(1)}, u32[]{:S(2)}, u32[]{:S(2)}) collective-permute-start(bf16[96,512]{1,0:T(8,128)(2,1)S(1)} %convolution_convert_fusion.2), channel_id=1, source_target_pairs={{0,64},{1,65},{2,66},{3,67},{4,68},{5,69},{6,70},{7,71},{8,72},{9,... | collective-permute-start | bytes 294920 | tf_op jit(solution)/shard_map/back/ppermute | solution.py:57
  66.7 2.7 %collective-permute-start.9 = (bf16[96,512]{1,0:T(8,128)(2,1)S(1)}, bf16[96,512]{1,0:T(8,128)(2,1)S(1)}, u32[]{:S(2)}, u32[]{:S(2)}) collective-permute-start(bf16[96,512]{1,0:T(8,128)(2,1)S(1)} %convolution_convert_fusion.2), channel_id=1, source_target_pairs={{0,96},{1,97},{2,98},{3,99},{4,100},{5,101},{6,102},{7,103},{8,104... | collective-permute-start | bytes 294920 | tf_op jit(solution)/shard_map/back/ppermute | solution.py:57
  70.3 2.1 %collective-permute-start.13 = (bf16[96,512]{1,0:T(8,128)(2,1)}, bf16[96,512]{1,0:T(8,128)(2,1)}, u32[]{:S(2)}, u32[]{:S(2)}) collective-permute-start(bf16[96,512]{1,0:T(8,128)(2,1)} %get-tuple-element.105), channel_id=1, source_target_pairs={{0,0},{1,1},{2,16},{3,20},{4,32},{5,33},{6,48},{7,52},{8,64},{9,65... | collective-permute-start | bytes 294920 | tf_op jit(solution)/shard_map/targets/ppermute | solution.py:57
  83.5 2.9 %collective-permute-start.15 = (bf16[2,96,1024]{2,1,0:T(8,128)(2,1)S(1)}, bf16[2,96,1024]{2,1,0:T(8,128)(2,1)S(1)}, u32[]{:S(2)}, u32[]{:S(2)}) collective-permute-start(bf16[2,96,1024]{2,1,0:T(8,128)(2,1)S(1)} %bitcast.134), channel_id=1, source_target_pairs={{0,4},{1,5},{2,6},{3,7},{4,8},{5,9},{6,10},{7,11},{8,12},{9,13},{1... | collective-permute-start | bytes 1179656 | tf_op jit(solution)/shard_map/reduce_draft/ppermute | solution.py:57
  86.6 4.3 %collective-permute-start.18 = (bf16[2,96,1024]{2,1,0:T(8,128)(2,1)S(1)}, bf16[2,96,1024]{2,1,0:T(8,128)(2,1)S(1)}, u32[]{:S(2)}, u32[]{:S(2)}) collective-permute-start(bf16[2,96,1024]{2,1,0:T(8,128)(2,1)S(1)} %bitcast.131), channel_id=1, source_target_pairs={{0,12},{1,13},{2,14},{3,15},{4,0},{5,1},{6,2},{7,3},{8,4},{9,5},{1... | collective-permute-start | bytes 1179656 | tf_op jit(solution)/shard_map/reduce_draft/ppermute | solution.py:57
  92.6 2.1 %collective-permute-start.17 = (bf16[2,96,1024]{2,1,0:T(8,128)(2,1)S(1)}, bf16[2,96,1024]{2,1,0:T(8,128)(2,1)S(1)}, u32[]{:S(2)}, u32[]{:S(2)}) collective-permute-start(bf16[2,96,1024]{2,1,0:T(8,128)(2,1)S(1)} %bitcast.133), channel_id=1, source_target_pairs={{0,12},{1,13},{2,14},{3,15},{4,0},{5,1},{6,2},{7,3},{8,4},{9,5},{1... | collective-permute-start | bytes 1179656 | tf_op jit(solution)/shard_map/reduce_draft/ppermute | solution.py:57
  97.8 2.7 %collective-permute-start.19 = (bf16[2,96,1024]{2,1,0:T(8,128)(2,1)S(1)}, bf16[2,96,1024]{2,1,0:T(8,128)(2,1)S(1)}, u32[]{:S(2)}, u32[]{:S(2)}) collective-permute-start(bf16[2,96,1024]{2,1,0:T(8,128)(2,1)S(1)} %add.472), channel_id=1, source_target_pairs={{0,12},{1,13},{2,14},{3,15},{4,0},{5,1},{6,2},{7,3},{8,4},{9,5},{1... | collective-permute-start | bytes 1179656 | tf_op jit(solution)/shard_map/reduce_draft/ppermute | solution.py:57
  101.7 6.4 %collective-permute-done.16 = bf16[2,96,1024]{2,1,0:T(8,128)(2,1)S(1)} collective-permute-done((bf16[2,96,1024]{2,1,0:T(8,128)(2,1)S(1)}, bf16[2,96,1024]{2,1,0:T(8,128)(2,1)S(1)}, u32[]{:S(2)}, u32[]{:S(2)}) %collective-permute-start.16) | collective-permute-done | bytes 393248 | tf_op jit(solution)/shard_map/reduce_draft/ppermute | solution.py:57
  109.2 2.6 %collective-permute-start.22 = (bf16[96,1024]{1,0:T(8,128)(2,1)S(1)}, bf16[96,1024]{1,0:T(8,128)(2,1)S(1)}, u32[]{:S(2)}, u32[]{:S(2)}) collective-permute-start(bf16[96,1024]{1,0:T(8,128)(2,1)S(1)} %get-tuple-element.93), channel_id=1, source_target_pairs={{0,3},{1,0},{2,1},{3,2},{4,7},{5,4},{6,5},{7,6},{8,11},{9,8},{10,9... | collective-permute-start | bytes 589832 | tf_op jit(solution)/shard_map/reduce_draft/ppermute | solution.py:57
  113.5 2.0 %collective-permute-done.21 = bf16[96,1024]{1,0:T(8,128)(2,1)S(1)} collective-permute-done((bf16[96,1024]{1,0:T(8,128)(2,1)S(1)}, bf16[96,1024]{1,0:T(8,128)(2,1)S(1)}, u32[]{:S(2)}, u32[]{:S(2)}) %collective-permute-start.21) | collective-permute-done | bytes 196640 | tf_op jit(solution)/shard_map/reduce_draft/ppermute | solution.py:57
  117.2 1.8 %collective-permute-done.23 = bf16[96,1024]{1,0:T(8,128)(2,1)S(1)} collective-permute-done((bf16[96,1024]{1,0:T(8,128)(2,1)S(1)}, bf16[96,1024]{1,0:T(8,128)(2,1)S(1)}, u32[]{:S(2)}, u32[]{:S(2)}) %collective-permute-start.23) | collective-permute-done | bytes 196640 | tf_op jit(solution)/shard_map/reduce_draft/ppermute | solution.py:57
  121.7 2.8 %collective-permute-start.27 = (f32[3,96]{1,0:T(4,128)S(1)}, f32[3,96]{1,0:T(4,128)S(1)}, u32[]{:S(2)}, u32[]{:S(2)}) collective-permute-start(f32[3,96]{1,0:T(4,128)S(1)} %fusion.129), channel_id=1, source_target_pairs={{0,96},{1,97},{2,98},{3,99},{4,100},{5,101},{6,102},{7,103},{8,104... | collective-permute-start | bytes 3464 | tf_op jit(solution)/shard_map/norm/ppermute | solution.py:57
  127.0 7.2 %collective-permute-start.28 = (bf16[96,1024]{1,0:T(8,128)(2,1)S(1)}, bf16[96,1024]{1,0:T(8,128)(2,1)S(1)}, u32[]{:S(2)}, u32[]{:S(2)}) collective-permute-start(bf16[96,1024]{1,0:T(8,128)(2,1)S(1)} %fusion.58), channel_id=1, source_target_pairs={{0,3},{1,0},{2,1},{3,2},{4,7},{5,4},{6,5},{7,6},{8,11},{9,8},{10,9... | collective-permute-start | bytes 589832 | tf_op jit(solution)/shard_map/gather_slope/ppermute | solution.py:57
  135.6 2.4 %slice.72 = bf16[8,192,1024]{2,1,0:T(8,128)(2,1)S(1)} slice(bf16[8,240,1024]{2,1,0:T(8,128)(2,1)} %bitcast.120), slice={[0:8], [0:192], [0:1024]} | slice | bytes 6291456 | tf_op jit(solution)/shard_map/forward/slice | solution.py:309
  139.5 2.1 %collective-permute-done.29 = bf16[96,1024]{1,0:T(8,128)(2,1)} collective-permute-done((bf16[96,1024]{1,0:T(8,128)(2,1)S(1)}, bf16[96,1024]{1,0:T(8,128)(2,1)}, u32[]{:S(2)}, u32[]{:S(2)}) %collective-permute-start.29) | collective-permute-done | bytes 196640 | tf_op jit(solution)/shard_map/gather_slope/ppermute | solution.py:57
  141.6 1.8 %collective-permute-done.30 = bf16[96,1024]{1,0:T(8,128)(2,1)} collective-permute-done((bf16[96,1024]{1,0:T(8,128)(2,1)S(1)}, bf16[96,1024]{1,0:T(8,128)(2,1)}, u32[]{:S(2)}, u32[]{:S(2)}) %collective-permute-start.30) | collective-permute-done | bytes 196640 | tf_op jit(solution)/shard_map/gather_slope/ppermute | solution.py:57
  146.4 2.0 %together.1 = (bf16[192,1024]{1,0:T(8,128)(2,1)}, bf16[192,1024]{1,0:T(8,128)(2,1)}) custom-call(bf16[192,1024]{1,0:T(8,128)(2,1)} %pad_maximum_fusion.6.first_ref, bf16[192,1024]{1,0:T(8,128)(2,1)} %pad_maximum_fusion.7.second_ref), custom_call_target="tpu_custom_call" | custom-call | tf_op jit(solution)/shard_map/gather_slope/together/pallas_call | solution.py:174
  148.4 3.2 %collective-permute-start.34 = (bf16[192,1024]{1,0:T(8,128)(2,1)}, bf16[192,1024]{1,0:T(8,128)(2,1)S(1)}, u32[]{:S(2)}, u32[]{:S(2)}) collective-permute-start(bf16[192,1024]{1,0:T(8,128)(2,1)} %pad_maximum_fusion.7.second_ref), channel_id=1, source_target_pairs={{0,12},{1,13},{2,14},{3,15},{4,0},{5,1},{6,2},{7,3},{8,4},{9,5},{1... | collective-permute-start | bytes 1179656 | tf_op jit(solution)/shard_map/gather_slope/ppermute | solution.py:57
  151.6 3.2 %collective-permute-start.33 = (bf16[192,1024]{1,0:T(8,128)(2,1)}, bf16[192,1024]{1,0:T(8,128)(2,1)S(1)}, u32[]{:S(2)}, u32[]{:S(2)}) collective-permute-start(bf16[192,1024]{1,0:T(8,128)(2,1)} %get-tuple-element.67), channel_id=1, source_target_pairs={{0,12},{1,13},{2,14},{3,15},{4,0},{5,1},{6,2},{7,3},{8,4},{9,5},{1... | collective-permute-start | bytes 1179656 | tf_op jit(solution)/shard_map/gather_slope/ppermute | solution.py:57
  157.2 3.6 %collective-permute-start.36 = (bf16[192,1024]{1,0:T(8,128)(2,1)S(1)}, bf16[192,1024]{1,0:T(8,128)(2,1)S(1)}, u32[]{:S(2)}, u32[]{:S(2)}) collective-permute-start(bf16[192,1024]{1,0:T(8,128)(2,1)S(1)} %collective-permute-done.34), channel_id=1, source_target_pairs={{0,12},{1,13},{2,14},{3,15},{4,0},{5,1},{6,2},{7,3},{8,4},{9,5},{1... | collective-permute-start | bytes 1179656 | tf_op jit(solution)/shard_map/gather_slope/ppermute | solution.py:57
  161.4 3.7 %fusion = f32[1536,1024]{1,0:T(8,128)S(1)} fusion(bf16[192,1536]{1,0:T(8,128)(2,1)S(1)} %get-tuple-element.81, bf16[192,1536]{1,0:T(8,128)(2,1)S(1)} %get-tuple-element.79, bf16[192,1536]{1,0:T(8,128)(2,1)S(1)} %get-tuple-element.78, bf16[192,1536]{1,0:T(8,128)(2,1)S(1)} %get-tuple-element.77, bf16[192,1024]{1,0:T(8,128)(2,1)S(1)} %collective-permute-done.34, ...), kind=kOutput, calls=%fused_computation.21 | convolution fusion | flops 2431647744 | bytes 10223616 | tf_op jit(solution)/shard_map/step/dot_general | solution.py:412
  165.2 1.9 %convolution_add_fusion = f32[1536,1024]{1,0:T(8,128)S(1)} fusion(f32[1536,1024]{1,0:T(8,128)S(1)} %fusion, bf16[192,1536]{1,0:T(8,128)(2,1)S(1)} %get-tuple-element.76, bf16[192,1536]{1,0:T(8,128)(2,1)S(1)} %get-tuple-element.75, bf16[96,1024]{1,0:T(8,128)(2,1)S(1)} %copy-done.7, bf16[96,1024]{1,0:T(8,128)(2,1)S(1)} %copy-done.5, ...), kind=kOutput, calls=%fused_computation.17 | convolution fusion | flops 1215037440 | bytes 14548992 | tf_op jit(solution)/shard_map/step/dot_general | solution.py:412
  168.1 4.0 %subtract_convert_fusion = bf16[1536,1024]{1,0:T(8,128)(2,1)} fusion(f32[1536,1024]{1,0:T(8,128)S(1)} %bitcast.106, f32[1536,1024]{1,0:T(8,128)S(1)} %convolution_add_fusion, bf16[192,1536]{1,0:T(8,128)(2,1)S(1)} %get-tuple-element.80, bf16[192,1536]{1,0:T(8,128)(2,1)S(1)} %get-tuple-element.74, bf16[192,1024]{1,0:T(8,128)(2,1)S(1)} %collective-permute-done.36, ...), kind=kOutput, calls=%fused_computation.16 | convolution fusion | flops 1218183168 | bytes 17694720 | tf_op jit(solution)/shard_map/step/dot_general | solution.py:412
  (185 shorter events, 58.3 us)
Async XLA Ops:
  7.2 68.1 %all-gather.2.cloned.1.call-start = ((), (), s32[]{:S(2)}) async-start(), calls=%async_computation | async-start | bytes 4423680 | tf_op jit(solution)/shard_map/all_gather | solution.py:266
  14.9 13.2 %collective-permute-start.3 = (bf16[2,256,512]{2,1,0:T(8,128)(2,1)S(1)}, bf16[2,256,512]{2,1,0:T(8,128)(2,1)S(1)}, u32[]{:S(2)}, u32[]{:S(2)}) collective-permute-start(bf16[2,256,512]{2,1,0:T(8,128)(2,1)S(1)} %copy-done.20), channel_id=1, source_target_pairs={{0,12},{1,13},{2,14},{3,15},{4,0},{5,1},{6,2},{7,3},{8,4},{9,5},{1... | collective-permute-start | bytes 1572872 | tf_op jit(solution)/shard_map/reduce_down/ppermute | solution.py:57
  19.1 15.6 %collective-permute-start = (bf16[2,256,512]{2,1,0:T(8,128)(2,1)}, bf16[2,256,512]{2,1,0:T(8,128)(2,1)S(1)}, u32[]{:S(2)}, u32[]{:S(2)}) collective-permute-start(bf16[2,256,512]{2,1,0:T(8,128)(2,1)} %get-tuple-element.46), channel_id=1, source_target_pairs={{0,4},{1,5},{2,6},{3,7},{4,8},{5,9},{6,10},{7,11},{8,12},{9,13},{1... | collective-permute-start | bytes 1572872 | tf_op jit(solution)/shard_map/reduce_down/ppermute | solution.py:57
  28.1 13.2 %collective-permute-start.5 = (bf16[2,256,512]{2,1,0:T(8,128)(2,1)}, bf16[2,256,512]{2,1,0:T(8,128)(2,1)S(1)}, u32[]{:S(2)}, u32[]{:S(2)}) collective-permute-start(bf16[2,256,512]{2,1,0:T(8,128)(2,1)} %get-tuple-element.51), channel_id=1, source_target_pairs={{0,4},{1,5},{2,6},{3,7},{4,8},{5,9},{6,10},{7,11},{8,12},{9,13},{1... | collective-permute-start | bytes 1572872 | tf_op jit(solution)/shard_map/reduce_down/ppermute | solution.py:57
  29.3 12.0 %collective-permute-start.4 = (bf16[2,256,512]{2,1,0:T(8,128)(2,1)S(1)}, bf16[2,256,512]{2,1,0:T(8,128)(2,1)S(1)}, u32[]{:S(2)}, u32[]{:S(2)}) collective-permute-start(bf16[2,256,512]{2,1,0:T(8,128)(2,1)S(1)} %add.415), channel_id=1, source_target_pairs={{0,12},{1,13},{2,14},{3,15},{4,0},{5,1},{6,2},{7,3},{8,4},{9,5},{1... | collective-permute-start | bytes 1572872 | tf_op jit(solution)/shard_map/reduce_down/ppermute | solution.py:57
  32.7 12.4 %collective-permute-start.2 = (bf16[2,256,512]{2,1,0:T(8,128)(2,1)}, bf16[2,256,512]{2,1,0:T(8,128)(2,1)S(1)}, u32[]{:S(2)}, u32[]{:S(2)}) collective-permute-start(bf16[2,256,512]{2,1,0:T(8,128)(2,1)} %get-tuple-element.47), channel_id=1, source_target_pairs={{0,12},{1,13},{2,14},{3,15},{4,0},{5,1},{6,2},{7,3},{8,4},{9,5},{1... | collective-permute-start | bytes 1572872 | tf_op jit(solution)/shard_map/reduce_down/ppermute | solution.py:57
  35.9 10.6 %collective-permute-start.1 = (bf16[2,256,512]{2,1,0:T(8,128)(2,1)S(1)}, bf16[2,256,512]{2,1,0:T(8,128)(2,1)}, u32[]{:S(2)}, u32[]{:S(2)}) collective-permute-start(bf16[2,256,512]{2,1,0:T(8,128)(2,1)S(1)} %add.412), channel_id=1, source_target_pairs={{0,4},{1,5},{2,6},{3,7},{4,8},{5,9},{6,10},{7,11},{8,12},{9,13},{1... | collective-permute-start | bytes 1572872 | tf_op jit(solution)/shard_map/reduce_down/ppermute | solution.py:57
  48.9 11.1 %collective-permute-start.6 = (bf16[256,512]{1,0:T(8,128)(2,1)}, bf16[256,512]{1,0:T(8,128)(2,1)S(1)}, u32[]{:S(2)}, u32[]{:S(2)}) collective-permute-start(bf16[256,512]{1,0:T(8,128)(2,1)} %get-tuple-element.84), channel_id=1, source_target_pairs={{0,1},{1,2},{2,3},{3,0},{4,5},{5,6},{6,7},{7,4},{8,9},{9,10},{10,1... | collective-permute-start | bytes 786440 | tf_op jit(solution)/shard_map/reduce_down/ppermute | solution.py:57
  50.5 9.5 %collective-permute-start.7 = (bf16[256,512]{1,0:T(8,128)(2,1)}, bf16[256,512]{1,0:T(8,128)(2,1)}, u32[]{:S(2)}, u32[]{:S(2)}) collective-permute-start(bf16[256,512]{1,0:T(8,128)(2,1)} %get-tuple-element.86), channel_id=1, source_target_pairs={{0,3},{1,0},{2,1},{3,2},{4,7},{5,4},{6,5},{7,6},{8,11},{9,8},{10,9... | collective-permute-start | bytes 786440 | tf_op jit(solution)/shard_map/reduce_down/ppermute | solution.py:57
  52.1 8.7 %collective-permute-start.8 = (bf16[256,512]{1,0:T(8,128)(2,1)}, bf16[256,512]{1,0:T(8,128)(2,1)}, u32[]{:S(2)}, u32[]{:S(2)}) collective-permute-start(bf16[256,512]{1,0:T(8,128)(2,1)} %get-tuple-element.85), channel_id=1, source_target_pairs={{0,2},{1,3},{2,0},{3,1},{4,6},{5,7},{6,4},{7,5},{8,10},{9,11},{10,... | collective-permute-start | bytes 786440 | tf_op jit(solution)/shard_map/reduce_down/ppermute | solution.py:57
  63.0 10.8 %collective-permute-start.10 = (bf16[96,512]{1,0:T(8,128)(2,1)S(1)}, bf16[96,512]{1,0:T(8,128)(2,1)S(1)}, u32[]{:S(2)}, u32[]{:S(2)}) collective-permute-start(bf16[96,512]{1,0:T(8,128)(2,1)S(1)} %convolution_convert_fusion.2), channel_id=1, source_target_pairs={{0,64},{1,65},{2,66},{3,67},{4,68},{5,69},{6,70},{7,71},{8,72},{9,... | collective-permute-start | bytes 294920 | tf_op jit(solution)/shard_map/back/ppermute | solution.py:57
  66.2 7.7 %collective-permute-start.11 = (bf16[96,512]{1,0:T(8,128)(2,1)S(1)}, bf16[96,512]{1,0:T(8,128)(2,1)S(1)}, u32[]{:S(2)}, u32[]{:S(2)}) collective-permute-start(bf16[96,512]{1,0:T(8,128)(2,1)S(1)} %convolution_convert_fusion.2), channel_id=1, source_target_pairs={{0,32},{1,33},{2,34},{3,35},{4,36},{5,37},{6,38},{7,39},{8,40},{9,... | collective-permute-start | bytes 294920 | tf_op jit(solution)/shard_map/back/ppermute | solution.py:57
  66.7 7.1 %collective-permute-start.9 = (bf16[96,512]{1,0:T(8,128)(2,1)S(1)}, bf16[96,512]{1,0:T(8,128)(2,1)S(1)}, u32[]{:S(2)}, u32[]{:S(2)}) collective-permute-start(bf16[96,512]{1,0:T(8,128)(2,1)S(1)} %convolution_convert_fusion.2), channel_id=1, source_target_pairs={{0,96},{1,97},{2,98},{3,99},{4,100},{5,101},{6,102},{7,103},{8,104... | collective-permute-start | bytes 294920 | tf_op jit(solution)/shard_map/back/ppermute | solution.py:57
  70.3 20.6 %collective-permute-start.13 = (bf16[96,512]{1,0:T(8,128)(2,1)}, bf16[96,512]{1,0:T(8,128)(2,1)}, u32[]{:S(2)}, u32[]{:S(2)}) collective-permute-start(bf16[96,512]{1,0:T(8,128)(2,1)} %get-tuple-element.105), channel_id=1, source_target_pairs={{0,0},{1,1},{2,16},{3,20},{4,32},{5,33},{6,48},{7,52},{8,64},{9,65... | collective-permute-start | bytes 294920 | tf_op jit(solution)/shard_map/targets/ppermute | solution.py:57
  72.5 18.5 %collective-permute-start.14 = (bf16[96,512]{1,0:T(8,128)(2,1)}, bf16[96,512]{1,0:T(8,128)(2,1)}, u32[]{:S(2)}, u32[]{:S(2)}) collective-permute-start(bf16[96,512]{1,0:T(8,128)(2,1)} %get-tuple-element.104), channel_id=1, source_target_pairs={{0,1},{1,0},{2,20},{3,16},{4,33},{5,32},{6,52},{7,48},{8,65},{9,64... | collective-permute-start | bytes 294920 | tf_op jit(solution)/shard_map/targets/ppermute | solution.py:57
  83.5 12.9 %collective-permute-start.15 = (bf16[2,96,1024]{2,1,0:T(8,128)(2,1)S(1)}, bf16[2,96,1024]{2,1,0:T(8,128)(2,1)S(1)}, u32[]{:S(2)}, u32[]{:S(2)}) collective-permute-start(bf16[2,96,1024]{2,1,0:T(8,128)(2,1)S(1)} %bitcast.134), channel_id=1, source_target_pairs={{0,4},{1,5},{2,6},{3,7},{4,8},{5,9},{6,10},{7,11},{8,12},{9,13},{1... | collective-permute-start | bytes 1179656 | tf_op jit(solution)/shard_map/reduce_draft/ppermute | solution.py:57
  86.6 11.1 %collective-permute-start.18 = (bf16[2,96,1024]{2,1,0:T(8,128)(2,1)S(1)}, bf16[2,96,1024]{2,1,0:T(8,128)(2,1)S(1)}, u32[]{:S(2)}, u32[]{:S(2)}) collective-permute-start(bf16[2,96,1024]{2,1,0:T(8,128)(2,1)S(1)} %bitcast.131), channel_id=1, source_target_pairs={{0,12},{1,13},{2,14},{3,15},{4,0},{5,1},{6,2},{7,3},{8,4},{9,5},{1... | collective-permute-start | bytes 1179656 | tf_op jit(solution)/shard_map/reduce_draft/ppermute | solution.py:57
  92.6 9.1 %collective-permute-start.17 = (bf16[2,96,1024]{2,1,0:T(8,128)(2,1)S(1)}, bf16[2,96,1024]{2,1,0:T(8,128)(2,1)S(1)}, u32[]{:S(2)}, u32[]{:S(2)}) collective-permute-start(bf16[2,96,1024]{2,1,0:T(8,128)(2,1)S(1)} %bitcast.133), channel_id=1, source_target_pairs={{0,12},{1,13},{2,14},{3,15},{4,0},{5,1},{6,2},{7,3},{8,4},{9,5},{1... | collective-permute-start | bytes 1179656 | tf_op jit(solution)/shard_map/reduce_draft/ppermute | solution.py:57
  94.8 13.4 %collective-permute-start.20 = (bf16[2,96,1024]{2,1,0:T(8,128)(2,1)S(1)}, bf16[2,96,1024]{2,1,0:T(8,128)(2,1)S(1)}, u32[]{:S(2)}, u32[]{:S(2)}) collective-permute-start(bf16[2,96,1024]{2,1,0:T(8,128)(2,1)S(1)} %bitcast.132), channel_id=1, source_target_pairs={{0,4},{1,5},{2,6},{3,7},{4,8},{5,9},{6,10},{7,11},{8,12},{9,13},{1... | collective-permute-start | bytes 1179656 | tf_op jit(solution)/shard_map/reduce_draft/ppermute | solution.py:57
  96.6 11.4 %collective-permute-start.16 = (bf16[2,96,1024]{2,1,0:T(8,128)(2,1)S(1)}, bf16[2,96,1024]{2,1,0:T(8,128)(2,1)S(1)}, u32[]{:S(2)}, u32[]{:S(2)}) collective-permute-start(bf16[2,96,1024]{2,1,0:T(8,128)(2,1)S(1)} %add.467), channel_id=1, source_target_pairs={{0,4},{1,5},{2,6},{3,7},{4,8},{5,9},{6,10},{7,11},{8,12},{9,13},{1... | collective-permute-start | bytes 1179656 | tf_op jit(solution)/shard_map/reduce_draft/ppermute | solution.py:57
  97.8 10.4 %collective-permute-start.19 = (bf16[2,96,1024]{2,1,0:T(8,128)(2,1)S(1)}, bf16[2,96,1024]{2,1,0:T(8,128)(2,1)S(1)}, u32[]{:S(2)}, u32[]{:S(2)}) collective-permute-start(bf16[2,96,1024]{2,1,0:T(8,128)(2,1)S(1)} %add.472), channel_id=1, source_target_pairs={{0,12},{1,13},{2,14},{3,15},{4,0},{5,1},{6,2},{7,3},{8,4},{9,5},{1... | collective-permute-start | bytes 1179656 | tf_op jit(solution)/shard_map/reduce_draft/ppermute | solution.py:57
  109.2 8.0 %collective-permute-start.22 = (bf16[96,1024]{1,0:T(8,128)(2,1)S(1)}, bf16[96,1024]{1,0:T(8,128)(2,1)S(1)}, u32[]{:S(2)}, u32[]{:S(2)}) collective-permute-start(bf16[96,1024]{1,0:T(8,128)(2,1)S(1)} %get-tuple-element.93), channel_id=1, source_target_pairs={{0,3},{1,0},{2,1},{3,2},{4,7},{5,4},{6,5},{7,6},{8,11},{9,8},{10,9... | collective-permute-start | bytes 589832 | tf_op jit(solution)/shard_map/reduce_draft/ppermute | solution.py:57
  111.9 7.2 %collective-permute-start.23 = (bf16[96,1024]{1,0:T(8,128)(2,1)S(1)}, bf16[96,1024]{1,0:T(8,128)(2,1)S(1)}, u32[]{:S(2)}, u32[]{:S(2)}) collective-permute-start(bf16[96,1024]{1,0:T(8,128)(2,1)S(1)} %get-tuple-element.92), channel_id=1, source_target_pairs={{0,2},{1,3},{2,0},{3,1},{4,6},{5,7},{6,4},{7,5},{8,10},{9,11},{10,... | collective-permute-start | bytes 589832 | tf_op jit(solution)/shard_map/reduce_draft/ppermute | solution.py:57
  127.0 12.5 %collective-permute-start.28 = (bf16[96,1024]{1,0:T(8,128)(2,1)S(1)}, bf16[96,1024]{1,0:T(8,128)(2,1)S(1)}, u32[]{:S(2)}, u32[]{:S(2)}) collective-permute-start(bf16[96,1024]{1,0:T(8,128)(2,1)S(1)} %fusion.58), channel_id=1, source_target_pairs={{0,3},{1,0},{2,1},{3,2},{4,7},{5,4},{6,5},{7,6},{8,11},{9,8},{10,9... | collective-permute-start | bytes 589832 | tf_op jit(solution)/shard_map/gather_slope/ppermute | solution.py:57
  134.2 7.4 %collective-permute-start.29 = (bf16[96,1024]{1,0:T(8,128)(2,1)S(1)}, bf16[96,1024]{1,0:T(8,128)(2,1)}, u32[]{:S(2)}, u32[]{:S(2)}) collective-permute-start(bf16[96,1024]{1,0:T(8,128)(2,1)S(1)} %fusion.58), channel_id=1, source_target_pairs={{0,2},{1,3},{2,0},{3,1},{4,6},{5,7},{6,4},{7,5},{8,10},{9,11},{10,... | collective-permute-start | bytes 589832 | tf_op jit(solution)/shard_map/gather_slope/ppermute | solution.py:57
  134.3 9.1 %collective-permute-start.30 = (bf16[96,1024]{1,0:T(8,128)(2,1)S(1)}, bf16[96,1024]{1,0:T(8,128)(2,1)}, u32[]{:S(2)}, u32[]{:S(2)}) collective-permute-start(bf16[96,1024]{1,0:T(8,128)(2,1)S(1)} %fusion.58), channel_id=1, source_target_pairs={{0,1},{1,2},{2,3},{3,0},{4,5},{5,6},{6,7},{7,4},{8,9},{9,10},{10,1... | collective-permute-start | bytes 589832 | tf_op jit(solution)/shard_map/gather_slope/ppermute | solution.py:57
  145.5 11.2 %collective-permute-start.31 = (bf16[192,1024]{1,0:T(8,128)(2,1)}, bf16[192,1024]{1,0:T(8,128)(2,1)}, u32[]{:S(2)}, u32[]{:S(2)}) collective-permute-start(bf16[192,1024]{1,0:T(8,128)(2,1)} %pad_maximum_fusion.6.first_ref), channel_id=1, source_target_pairs={{0,4},{1,5},{2,6},{3,7},{4,8},{5,9},{6,10},{7,11},{8,12},{9,13},{1... | collective-permute-start | bytes 1179656 | tf_op jit(solution)/shard_map/gather_slope/ppermute | solution.py:57
  148.4 8.8 %collective-permute-start.34 = (bf16[192,1024]{1,0:T(8,128)(2,1)}, bf16[192,1024]{1,0:T(8,128)(2,1)S(1)}, u32[]{:S(2)}, u32[]{:S(2)}) collective-permute-start(bf16[192,1024]{1,0:T(8,128)(2,1)} %pad_maximum_fusion.7.second_ref), channel_id=1, source_target_pairs={{0,12},{1,13},{2,14},{3,15},{4,0},{5,1},{6,2},{7,3},{8,4},{9,5},{1... | collective-permute-start | bytes 1179656 | tf_op jit(solution)/shard_map/gather_slope/ppermute | solution.py:57
  151.6 9.2 %collective-permute-start.32 = (bf16[192,1024]{1,0:T(8,128)(2,1)}, bf16[192,1024]{1,0:T(8,128)(2,1)S(1)}, u32[]{:S(2)}, u32[]{:S(2)}) collective-permute-start(bf16[192,1024]{1,0:T(8,128)(2,1)} %get-tuple-element.66), channel_id=1, source_target_pairs={{0,4},{1,5},{2,6},{3,7},{4,8},{5,9},{6,10},{7,11},{8,12},{9,13},{1... | collective-permute-start | bytes 1179656 | tf_op jit(solution)/shard_map/gather_slope/ppermute | solution.py:57
  151.6 9.8 %collective-permute-start.33 = (bf16[192,1024]{1,0:T(8,128)(2,1)}, bf16[192,1024]{1,0:T(8,128)(2,1)S(1)}, u32[]{:S(2)}, u32[]{:S(2)}) collective-permute-start(bf16[192,1024]{1,0:T(8,128)(2,1)} %get-tuple-element.67), channel_id=1, source_target_pairs={{0,12},{1,13},{2,14},{3,15},{4,0},{5,1},{6,2},{7,3},{8,4},{9,5},{1... | collective-permute-start | bytes 1179656 | tf_op jit(solution)/shard_map/gather_slope/ppermute | solution.py:57
  156.8 10.4 %collective-permute-start.35 = (bf16[192,1024]{1,0:T(8,128)(2,1)}, bf16[192,1024]{1,0:T(8,128)(2,1)S(1)}, u32[]{:S(2)}, u32[]{:S(2)}) collective-permute-start(bf16[192,1024]{1,0:T(8,128)(2,1)} %collective-permute-done.31), channel_id=1, source_target_pairs={{0,4},{1,5},{2,6},{3,7},{4,8},{5,9},{6,10},{7,11},{8,12},{9,13},{1... | collective-permute-start | bytes 1179656 | tf_op jit(solution)/shard_map/gather_slope/ppermute | solution.py:57
  157.2 9.9 %collective-permute-start.36 = (bf16[192,1024]{1,0:T(8,128)(2,1)S(1)}, bf16[192,1024]{1,0:T(8,128)(2,1)S(1)}, u32[]{:S(2)}, u32[]{:S(2)}) collective-permute-start(bf16[192,1024]{1,0:T(8,128)(2,1)S(1)} %collective-permute-done.34), channel_id=1, source_target_pairs={{0,12},{1,13},{2,14},{3,15},{4,0},{5,1},{6,2},{7,3},{8,4},{9,5},{1... | collective-permute-start | bytes 1179656 | tf_op jit(solution)/shard_map/gather_slope/ppermute | solution.py:57
  (33 other events, 153.8 us)
Sparse Core Ops, SparseCore 0:
  15.0 33.4 all-gather.1

commit v7 on v2

--- a/solution.py
+++ b/solution.py
@@ -35,16 +35,16 @@
 
 def along_first(shift):
     return moved(
+        lambda x, c, z, y: device_at(x, c, z + shift * (c == 1), y + shift * (c == 0))
+    )
+
+
+def along_second(shift):
+    return moved(
         lambda x, c, z, y: device_at(x, c, z + shift * (c == 0), y + shift * (c == 1))
     )
 
 
-def along_second(shift):
-    return moved(
-        lambda x, c, z, y: device_at(x, c, z + shift * (c == 1), y + shift * (c == 0))
-    )
-
-
 def along_x(shift):
     return moved(lambda x, c, z, y: device_at(x + shift, c, z, y))
 
@@ -67,7 +67,7 @@
 
 def row_block(c, tensor):
     z, y = tensor // side, tensor % side
-    return z * side + y if c == 0 else y * side + z
+    return y * side + z if c == 0 else z * side + y
 
 
 def turned(pieces, places):
@@ -83,7 +83,7 @@
     replica, tensor = lax.axis_index("replica"), lax.axis_index("tensor")
     x, c = replica // cores, replica % cores
     z, y = tensor // side, tensor % side
-    return x, c, jnp.where(c == 0, z, y), jnp.where(c == 0, y, z)
+    return x, c, jnp.where(c == 0, y, z), jnp.where(c == 0, z, y)
 
 
 def down_kernel(blocks_ref, tokens_ref, *refs):
@@ -234,7 +234,7 @@
 
         def columns(shift):
             first = (p + shift) % side
-            return jnp.where(c == 0, first * side + second, second * side + first)
+            return jnp.where(c == 0, second * side + first, first * side + second)
 
         near = down_pieces(columns(2), tokens, coded_weight, block_exponent, bf16)
         near, accepted = lax.optimization_barrier((near, accepted))

time: 178 us -> 179 us (level)
  transfers between devices with their start and end apart: 38 -> 38, of which waited for: 17 -> 16; matrix products, arithmetic and copies ran while one was open for 18% -> 18% of each run, Pallas kernels for 12% -> 12%
where the time goes in v7:
time: 179 us; the launch traced here: 178 us
  starting transfers between devices  65.5 us (37%)
  Pallas kernels  26.9 us (15%)
  waiting for transfers between devices  26 us (15%)
  matrix products  19.1 us (11%)
  other arithmetic  15.8 us (9%)
  between operations  14.8 us (8%)
  local copies, waits for them, and re-layouts  9.36 us (5%)
    ppermute x37, starting transfers between devices, send(): return lax.ppermute(array, mesh_axes, pairs)  65.5 us
    ppermute x37, waiting for transfers between devices, send(): return lax.ppermute(array, mesh_axes, pairs)  26 us
    pallas_call x3, Pallas kernels, down_pieces(): pl.pallas_call(down_kernel, grid_spec=pltpu.PrefetchScalarGridSpec(num_sc...  19 us
    dot_general x3, matrix products, product(): lax.dot_general(jnp.concatenate(inputs), jnp.concatenate(slopes), (((0,),...  9.59 us
    pallas_call x2, Pallas kernels, rounded_layers(): pl.pallas_call(round_kernel, grid=(layers,), in_specs=[pl.BlockSpec(memor...  5.89 us
    dot_general x8, matrix products, pair_product(): return jnp.dot(rows_of, weight, preferred_element_type=f32)  5.72 us
    unnamed x52, local copies, waits for them, and re-layouts  4.15 us
  transfers between devices with their start and end apart: 38, of which 16 were waited for; matrix products, arithmetic and copies ran while one was open for 18% of the time, Pallas kernels for 12%

profile of v7, /device:TPU:0, one launch (start us, length us, event | category | flops | bytes accessed | tf_op | source)
XLA Modules:
  0.0 177.6 jit_solution(6595448797928511816)
XLA Ops:
  7.8 5.3 %down_projection.3 = (bf16[2,256,512]{2,1,0:T(8,128)(2,1)}, bf16[2,256,512]{2,1,0:T(8,128)(2,1)}) custom-call(s32[4]{0:T(128)} %broadcast_select_fusion.17.blocks_ref, bf16[256,896]{1,0:T(8,128)(2,1)} %bitcast.121, bf16[896,8192]{1,0:T(8,128)(2,1)} %refs_1_.5, bf16[896,8192]{1,0:T(8,128)(2,1)} %refs_1_.5, s32[28,8192]{1,0:T(8,128)} %refs_3_.5, ...), custom_call_target="tpu_custom_call" | custom-call | flops 939524096 | bytes 5505024 | tf_op jit(solution)/shard_map/down/down_projection/pallas_call | solution.py:115
  15.2 3.2 %collective-permute-start.3 = (bf16[2,256,512]{2,1,0:T(8,128)(2,1)S(1)}, bf16[2,256,512]{2,1,0:T(8,128)(2,1)S(1)}, u32[]{:S(2)}, u32[]{:S(2)}) collective-permute-start(bf16[2,256,512]{2,1,0:T(8,128)(2,1)S(1)} %copy-done.19), channel_id=1, source_target_pairs={{0,3},{1,0},{2,1},{3,2},{4,7},{5,4},{6,5},{7,6},{8,11},{9,8},{10,9... | collective-permute-start | bytes 1572872 | tf_op jit(solution)/shard_map/reduce_down/ppermute | solution.py:57
  19.5 8.0 %down_projection.4 = (bf16[2,256,512]{2,1,0:T(8,128)(2,1)}, bf16[2,256,512]{2,1,0:T(8,128)(2,1)}, bf16[2,256,512]{2,1,0:T(8,128)(2,1)}, bf16[2,256,512]{2,1,0:T(8,128)(2,1)}) custom-call(s32[8]{0:T(128)} %pad_add_fusion.1.blocks_ref, bf16[256,896]{1,0:T(8,128)(2,1)} %bitcast.122, bf16[896,8192]{1,0:T(8,128)(2,1)} %refs_1_.5, bf16[896,8192]{1,0:T(8,128)(2,1)} %refs_1_.5, ...), custom_call_target="tpu_custom_call" | custom-call | flops 1879048192 | bytes 11010048 | tf_op jit(solution)/shard_map/down/down_projection/pallas_call | solution.py:115
  29.3 2.8 %collective-permute-start.4 = (bf16[2,256,512]{2,1,0:T(8,128)(2,1)S(1)}, bf16[2,256,512]{2,1,0:T(8,128)(2,1)S(1)}, u32[]{:S(2)}, u32[]{:S(2)}) collective-permute-start(bf16[2,256,512]{2,1,0:T(8,128)(2,1)S(1)} %add.415), channel_id=1, source_target_pairs={{0,3},{1,0},{2,1},{3,2},{4,7},{5,4},{6,5},{7,6},{8,11},{9,8},{10,9... | collective-permute-start | bytes 1572872 | tf_op jit(solution)/shard_map/reduce_down/ppermute | solution.py:57
  35.5 5.6 %down_projection.5 = (f32[2,256,512]{2,1,0:T(8,128)}, f32[2,256,512]{2,1,0:T(8,128)}) custom-call(s32[4]{0:T(128)} %get-tuple-element.43.blocks_ref, bf16[256,896]{1,0:T(8,128)(2,1)} %bitcast.123, bf16[896,8192]{1,0:T(8,128)(2,1)} %refs_1_.5, bf16[896,8192]{1,0:T(8,128)(2,1)} %refs_1_.5, s32[28,8192]{1,0:T(8,128)} %refs_3_.5, s32[28,8192]{1,0:T(8,128)} %refs_3_.5), custom_call_target="tpu_custom_call" | custom-call | flops 939524096 | bytes 5505024 | tf_op jit(solution)/shard_map/down/down_projection/pallas_call | solution.py:115
  42.7 1.9 %collective-permute-done.2 = bf16[2,256,512]{2,1,0:T(8,128)(2,1)S(1)} collective-permute-done((bf16[2,256,512]{2,1,0:T(8,128)(2,1)}, bf16[2,256,512]{2,1,0:T(8,128)(2,1)S(1)}, u32[]{:S(2)}, u32[]{:S(2)}) %collective-permute-start.2) | collective-permute-done | bytes 524320 | tf_op jit(solution)/shard_map/reduce_down/ppermute | solution.py:57
  48.0 1.9 %collective-permute-start.6 = (bf16[256,512]{1,0:T(8,128)(2,1)}, bf16[256,512]{1,0:T(8,128)(2,1)S(1)}, u32[]{:S(2)}, u32[]{:S(2)}) collective-permute-start(bf16[256,512]{1,0:T(8,128)(2,1)} %get-tuple-element.84), channel_id=1, source_target_pairs={{0,4},{1,5},{2,6},{3,7},{4,8},{5,9},{6,10},{7,11},{8,12},{9,13},{1... | collective-permute-start | bytes 786440 | tf_op jit(solution)/shard_map/reduce_down/ppermute | solution.py:57
  49.9 2.2 %collective-permute-start.7 = (bf16[256,512]{1,0:T(8,128)(2,1)S(1)}, bf16[256,512]{1,0:T(8,128)(2,1)S(1)}, u32[]{:S(2)}, u32[]{:S(2)}) collective-permute-start(bf16[256,512]{1,0:T(8,128)(2,1)S(1)} %get-tuple-element.86), channel_id=1, source_target_pairs={{0,12},{1,13},{2,14},{3,15},{4,0},{5,1},{6,2},{7,3},{8,4},{9,5},{1... | collective-permute-start | bytes 786440 | tf_op jit(solution)/shard_map/reduce_down/ppermute | solution.py:57
  52.1 1.9 %collective-permute-start.8 = (bf16[256,512]{1,0:T(8,128)(2,1)S(1)}, bf16[256,512]{1,0:T(8,128)(2,1)S(1)}, u32[]{:S(2)}, u32[]{:S(2)}) collective-permute-start(bf16[256,512]{1,0:T(8,128)(2,1)S(1)} %get-tuple-element.85), channel_id=1, source_target_pairs={{0,8},{1,9},{2,10},{3,11},{4,12},{5,13},{6,14},{7,15},{8,0},{9,1},... | collective-permute-start | bytes 786440 | tf_op jit(solution)/shard_map/reduce_down/ppermute | solution.py:57
  54.5 2.6 %round_weight.3 = bf16[512,1024]{1,0:T(8,128)(2,1)} custom-call(f32[8,128]{1,0:T(8,128)} %slice_bitcast_fusion.2.after_ref, f32[1536,1024]{1,0:T(8,128)} %bitcast.100, f32[1536,1024]{1,0:T(8,128)} %bitcast.101), custom_call_target="tpu_custom_call" | custom-call | flops 524288 | bytes 3145728 | tf_op jit(solution)/shard_map/round_weight/pallas_call | solution.py:156
  57.2 3.2 %round_weight.2 = bf16[1024,1024]{1,0:T(8,128)(2,1)} custom-call(f32[8,128]{1,0:T(8,128)} %slice_bitcast_fusion.2.after_ref, f32[1536,1024]{1,0:T(8,128)} %bitcast.102, f32[1536,1024]{1,0:T(8,128)} %bitcast.103), custom_call_target="tpu_custom_call" | custom-call | flops 1048576 | bytes 6291456 | tf_op jit(solution)/shard_map/round_weight/pallas_call | solution.py:156
  62.3 3.0 %collective-permute-start.10 = (bf16[96,512]{1,0:T(8,128)(2,1)S(1)}, bf16[96,512]{1,0:T(8,128)(2,1)S(1)}, u32[]{:S(2)}, u32[]{:S(2)}) collective-permute-start(bf16[96,512]{1,0:T(8,128)(2,1)S(1)} %convolution_convert_fusion.2), channel_id=1, source_target_pairs={{0,64},{1,65},{2,66},{3,67},{4,68},{5,69},{6,70},{7,71},{8,72},{9,... | collective-permute-start | bytes 294920 | tf_op jit(solution)/shard_map/back/ppermute | solution.py:57
  66.0 2.6 %collective-permute-start.9 = (bf16[96,512]{1,0:T(8,128)(2,1)S(1)}, bf16[96,512]{1,0:T(8,128)(2,1)S(1)}, u32[]{:S(2)}, u32[]{:S(2)}) collective-permute-start(bf16[96,512]{1,0:T(8,128)(2,1)S(1)} %convolution_convert_fusion.2), channel_id=1, source_target_pairs={{0,96},{1,97},{2,98},{3,99},{4,100},{5,101},{6,102},{7,103},{8,104... | collective-permute-start | bytes 294920 | tf_op jit(solution)/shard_map/back/ppermute | solution.py:57
  72.7 2.0 %collective-permute-start.12 = (bf16[4,96,512]{2,1,0:T(8,128)(2,1)S(1)}, bf16[4,96,512]{2,1,0:T(8,128)(2,1)S(1)}, u32[]{:S(2)}, u32[]{:S(2)}) collective-permute-start(bf16[4,96,512]{2,1,0:T(8,128)(2,1)S(1)} %pad_maximum_fusion.5), channel_id=1, source_target_pairs={{0,16},{1,17},{2,18},{3,19},{4,20},{5,21},{6,22},{7,23},{8,24},{9,... | collective-permute-start | bytes 1179656 | tf_op jit(solution)/shard_map/back/ppermute | solution.py:57
  84.6 2.1 %collective-permute-start.18 = (bf16[2,96,1024]{2,1,0:T(8,128)(2,1)S(1)}, bf16[2,96,1024]{2,1,0:T(8,128)(2,1)S(1)}, u32[]{:S(2)}, u32[]{:S(2)}) collective-permute-start(bf16[2,96,1024]{2,1,0:T(8,128)(2,1)S(1)} %bitcast.131), channel_id=1, source_target_pairs={{0,3},{1,0},{2,1},{3,2},{4,7},{5,4},{6,5},{7,6},{8,11},{9,8},{10,9... | collective-permute-start | bytes 1179656 | tf_op jit(solution)/shard_map/reduce_draft/ppermute | solution.py:57
  88.4 5.2 %collective-permute-start.17 = (bf16[2,96,1024]{2,1,0:T(8,128)(2,1)S(1)}, bf16[2,96,1024]{2,1,0:T(8,128)(2,1)S(1)}, u32[]{:S(2)}, u32[]{:S(2)}) collective-permute-start(bf16[2,96,1024]{2,1,0:T(8,128)(2,1)S(1)} %bitcast.133), channel_id=1, source_target_pairs={{0,3},{1,0},{2,1},{3,2},{4,7},{5,4},{6,5},{7,6},{8,11},{9,8},{10,9... | collective-permute-start | bytes 1179656 | tf_op jit(solution)/shard_map/reduce_draft/ppermute | solution.py:57
  96.0 3.3 %collective-permute-start.19 = (bf16[2,96,1024]{2,1,0:T(8,128)(2,1)S(1)}, bf16[2,96,1024]{2,1,0:T(8,128)(2,1)S(1)}, u32[]{:S(2)}, u32[]{:S(2)}) collective-permute-start(bf16[2,96,1024]{2,1,0:T(8,128)(2,1)S(1)} %add.472), channel_id=1, source_target_pairs={{0,3},{1,0},{2,1},{3,2},{4,7},{5,4},{6,5},{7,6},{8,11},{9,8},{10,9... | collective-permute-start | bytes 1179656 | tf_op jit(solution)/shard_map/reduce_draft/ppermute | solution.py:57
  99.7 7.3 %collective-permute-done.16 = bf16[2,96,1024]{2,1,0:T(8,128)(2,1)S(1)} collective-permute-done((bf16[2,96,1024]{2,1,0:T(8,128)(2,1)S(1)}, bf16[2,96,1024]{2,1,0:T(8,128)(2,1)S(1)}, u32[]{:S(2)}, u32[]{:S(2)}) %collective-permute-start.16) | collective-permute-done | bytes 393248 | tf_op jit(solution)/shard_map/reduce_draft/ppermute | solution.py:57
  107.6 3.2 %collective-permute-start.22 = (bf16[96,1024]{1,0:T(8,128)(2,1)S(1)}, bf16[96,1024]{1,0:T(8,128)(2,1)S(1)}, u32[]{:S(2)}, u32[]{:S(2)}) collective-permute-start(bf16[96,1024]{1,0:T(8,128)(2,1)S(1)} %get-tuple-element.93), channel_id=1, source_target_pairs={{0,12},{1,13},{2,14},{3,15},{4,0},{5,1},{6,2},{7,3},{8,4},{9,5},{1... | collective-permute-start | bytes 589832 | tf_op jit(solution)/shard_map/reduce_draft/ppermute | solution.py:57
  112.6 1.9 %collective-permute-done.21 = bf16[96,1024]{1,0:T(8,128)(2,1)S(1)} collective-permute-done((bf16[96,1024]{1,0:T(8,128)(2,1)S(1)}, bf16[96,1024]{1,0:T(8,128)(2,1)S(1)}, u32[]{:S(2)}, u32[]{:S(2)}) %collective-permute-start.21) | collective-permute-done | bytes 196640 | tf_op jit(solution)/shard_map/reduce_draft/ppermute | solution.py:57
  119.8 3.1 %collective-permute-start.27 = (f32[3,96]{1,0:T(4,128)S(1)}, f32[3,96]{1,0:T(4,128)S(1)}, u32[]{:S(2)}, u32[]{:S(2)}) collective-permute-start(f32[3,96]{1,0:T(4,128)S(1)} %fusion.128), channel_id=1, source_target_pairs={{0,96},{1,97},{2,98},{3,99},{4,100},{5,101},{6,102},{7,103},{8,104... | collective-permute-start | bytes 3464 | tf_op jit(solution)/shard_map/norm/ppermute | solution.py:57
  125.6 7.1 %collective-permute-start.28 = (bf16[96,1024]{1,0:T(8,128)(2,1)S(1)}, bf16[96,1024]{1,0:T(8,128)(2,1)S(1)}, u32[]{:S(2)}, u32[]{:S(2)}) collective-permute-start(bf16[96,1024]{1,0:T(8,128)(2,1)S(1)} %fusion.57), channel_id=1, source_target_pairs={{0,12},{1,13},{2,14},{3,15},{4,0},{5,1},{6,2},{7,3},{8,4},{9,5},{1... | collective-permute-start | bytes 589832 | tf_op jit(solution)/shard_map/gather_slope/ppermute | solution.py:57
  134.6 2.4 %slice.67 = bf16[8,192,1024]{2,1,0:T(8,128)(2,1)S(1)} slice(bf16[8,240,1024]{2,1,0:T(8,128)(2,1)} %bitcast.120), slice={[0:8], [0:192], [0:1024]} | slice | bytes 6291456 | tf_op jit(solution)/shard_map/forward/slice | solution.py:313
  138.0 2.1 %collective-permute-done.29 = bf16[96,1024]{1,0:T(8,128)(2,1)} collective-permute-done((bf16[96,1024]{1,0:T(8,128)(2,1)S(1)}, bf16[96,1024]{1,0:T(8,128)(2,1)}, u32[]{:S(2)}, u32[]{:S(2)}) %collective-permute-start.29) | collective-permute-done | bytes 196640 | tf_op jit(solution)/shard_map/gather_slope/ppermute | solution.py:57
  140.1 2.0 %collective-permute-done.30 = bf16[96,1024]{1,0:T(8,128)(2,1)} collective-permute-done((bf16[96,1024]{1,0:T(8,128)(2,1)S(1)}, bf16[96,1024]{1,0:T(8,128)(2,1)}, u32[]{:S(2)}, u32[]{:S(2)}) %collective-permute-start.30) | collective-permute-done | bytes 196640 | tf_op jit(solution)/shard_map/gather_slope/ppermute | solution.py:57
  145.1 2.0 %together.1 = (bf16[192,1024]{1,0:T(8,128)(2,1)}, bf16[192,1024]{1,0:T(8,128)(2,1)}) custom-call(bf16[192,1024]{1,0:T(8,128)(2,1)} %pad_maximum_fusion.6.first_ref, bf16[192,1024]{1,0:T(8,128)(2,1)} %pad_maximum_fusion.7.second_ref), custom_call_target="tpu_custom_call" | custom-call | tf_op jit(solution)/shard_map/gather_slope/together/pallas_call | solution.py:178
  147.1 3.2 %collective-permute-start.34 = (bf16[192,1024]{1,0:T(8,128)(2,1)}, bf16[192,1024]{1,0:T(8,128)(2,1)S(1)}, u32[]{:S(2)}, u32[]{:S(2)}) collective-permute-start(bf16[192,1024]{1,0:T(8,128)(2,1)} %pad_maximum_fusion.7.second_ref), channel_id=1, source_target_pairs={{0,3},{1,0},{2,1},{3,2},{4,7},{5,4},{6,5},{7,6},{8,11},{9,8},{10,9... | collective-permute-start | bytes 1179656 | tf_op jit(solution)/shard_map/gather_slope/ppermute | solution.py:57
  150.3 3.2 %collective-permute-start.33 = (bf16[192,1024]{1,0:T(8,128)(2,1)}, bf16[192,1024]{1,0:T(8,128)(2,1)S(1)}, u32[]{:S(2)}, u32[]{:S(2)}) collective-permute-start(bf16[192,1024]{1,0:T(8,128)(2,1)} %get-tuple-element.67), channel_id=1, source_target_pairs={{0,3},{1,0},{2,1},{3,2},{4,7},{5,4},{6,5},{7,6},{8,11},{9,8},{10,9... | collective-permute-start | bytes 1179656 | tf_op jit(solution)/shard_map/gather_slope/ppermute | solution.py:57
  155.9 3.6 %collective-permute-start.36 = (bf16[192,1024]{1,0:T(8,128)(2,1)S(1)}, bf16[192,1024]{1,0:T(8,128)(2,1)S(1)}, u32[]{:S(2)}, u32[]{:S(2)}) collective-permute-start(bf16[192,1024]{1,0:T(8,128)(2,1)S(1)} %collective-permute-done.34), channel_id=1, source_target_pairs={{0,3},{1,0},{2,1},{3,2},{4,7},{5,4},{6,5},{7,6},{8,11},{9,8},{10,9... | collective-permute-start | bytes 1179656 | tf_op jit(solution)/shard_map/gather_slope/ppermute | solution.py:57
  160.1 3.7 %fusion = f32[1536,1024]{1,0:T(8,128)S(1)} fusion(bf16[192,1536]{1,0:T(8,128)(2,1)S(1)} %get-tuple-element.81, bf16[192,1536]{1,0:T(8,128)(2,1)S(1)} %get-tuple-element.79, bf16[192,1536]{1,0:T(8,128)(2,1)S(1)} %get-tuple-element.78, bf16[192,1536]{1,0:T(8,128)(2,1)S(1)} %get-tuple-element.77, bf16[192,1024]{1,0:T(8,128)(2,1)S(1)} %collective-permute-done.34, ...), kind=kOutput, calls=%fused_computation.21 | convolution fusion | flops 2431647744 | bytes 10223616 | tf_op jit(solution)/shard_map/step/dot_general | solution.py:416
  163.9 1.9 %convolution_add_fusion = f32[1536,1024]{1,0:T(8,128)S(1)} fusion(f32[1536,1024]{1,0:T(8,128)S(1)} %fusion, bf16[192,1536]{1,0:T(8,128)(2,1)S(1)} %get-tuple-element.76, bf16[192,1536]{1,0:T(8,128)(2,1)S(1)} %get-tuple-element.75, bf16[96,1024]{1,0:T(8,128)(2,1)S(1)} %copy-done.8, bf16[96,1024]{1,0:T(8,128)(2,1)S(1)} %copy-done.6, ...), kind=kOutput, calls=%fused_computation.17 | convolution fusion | flops 1215037440 | bytes 14548992 | tf_op jit(solution)/shard_map/step/dot_general | solution.py:416
  166.8 4.0 %subtract_convert_fusion = bf16[1536,1024]{1,0:T(8,128)(2,1)} fusion(f32[1536,1024]{1,0:T(8,128)S(1)} %bitcast.106, f32[1536,1024]{1,0:T(8,128)S(1)} %convolution_add_fusion, bf16[192,1536]{1,0:T(8,128)(2,1)S(1)} %get-tuple-element.80, bf16[192,1536]{1,0:T(8,128)(2,1)S(1)} %get-tuple-element.74, bf16[192,1024]{1,0:T(8,128)(2,1)S(1)} %collective-permute-done.36, ...), kind=kOutput, calls=%fused_computation.16 | convolution fusion | flops 1218183168 | bytes 17694720 | tf_op jit(solution)/shard_map/step/dot_general | solution.py:416
  (183 shorter events, 54.9 us)
Async XLA Ops:
  7.2 67.5 %all-gather.2.cloned.1.call-start = ((), (), s32[]{:S(2)}) async-start(), calls=%async_computation | async-start | bytes 4423680 | tf_op jit(solution)/shard_map/all_gather | solution.py:270
  15.2 12.9 %collective-permute-start.3 = (bf16[2,256,512]{2,1,0:T(8,128)(2,1)S(1)}, bf16[2,256,512]{2,1,0:T(8,128)(2,1)S(1)}, u32[]{:S(2)}, u32[]{:S(2)}) collective-permute-start(bf16[2,256,512]{2,1,0:T(8,128)(2,1)S(1)} %copy-done.19), channel_id=1, source_target_pairs={{0,3},{1,0},{2,1},{3,2},{4,7},{5,4},{6,5},{7,6},{8,11},{9,8},{10,9... | collective-permute-start | bytes 1572872 | tf_op jit(solution)/shard_map/reduce_down/ppermute | solution.py:57
  18.3 15.7 %collective-permute-start = (bf16[2,256,512]{2,1,0:T(8,128)(2,1)}, bf16[2,256,512]{2,1,0:T(8,128)(2,1)S(1)}, u32[]{:S(2)}, u32[]{:S(2)}) collective-permute-start(bf16[2,256,512]{2,1,0:T(8,128)(2,1)} %get-tuple-element.46), channel_id=1, source_target_pairs={{0,1},{1,2},{2,3},{3,0},{4,5},{5,6},{6,7},{7,4},{8,9},{9,10},{10,1... | collective-permute-start | bytes 1572872 | tf_op jit(solution)/shard_map/reduce_down/ppermute | solution.py:57
  27.5 13.5 %collective-permute-start.5 = (bf16[2,256,512]{2,1,0:T(8,128)(2,1)}, bf16[2,256,512]{2,1,0:T(8,128)(2,1)S(1)}, u32[]{:S(2)}, u32[]{:S(2)}) collective-permute-start(bf16[2,256,512]{2,1,0:T(8,128)(2,1)} %get-tuple-element.51), channel_id=1, source_target_pairs={{0,1},{1,2},{2,3},{3,0},{4,5},{5,6},{6,7},{7,4},{8,9},{9,10},{10,1... | collective-permute-start | bytes 1572872 | tf_op jit(solution)/shard_map/reduce_down/ppermute | solution.py:57
  29.3 11.7 %collective-permute-start.4 = (bf16[2,256,512]{2,1,0:T(8,128)(2,1)S(1)}, bf16[2,256,512]{2,1,0:T(8,128)(2,1)S(1)}, u32[]{:S(2)}, u32[]{:S(2)}) collective-permute-start(bf16[2,256,512]{2,1,0:T(8,128)(2,1)S(1)} %add.415), channel_id=1, source_target_pairs={{0,3},{1,0},{2,1},{3,2},{4,7},{5,4},{6,5},{7,6},{8,11},{9,8},{10,9... | collective-permute-start | bytes 1572872 | tf_op jit(solution)/shard_map/reduce_down/ppermute | solution.py:57
  32.2 12.4 %collective-permute-start.2 = (bf16[2,256,512]{2,1,0:T(8,128)(2,1)}, bf16[2,256,512]{2,1,0:T(8,128)(2,1)S(1)}, u32[]{:S(2)}, u32[]{:S(2)}) collective-permute-start(bf16[2,256,512]{2,1,0:T(8,128)(2,1)} %get-tuple-element.47), channel_id=1, source_target_pairs={{0,3},{1,0},{2,1},{3,2},{4,7},{5,4},{6,5},{7,6},{8,11},{9,8},{10,9... | collective-permute-start | bytes 1572872 | tf_op jit(solution)/shard_map/reduce_down/ppermute | solution.py:57
  35.2 10.6 %collective-permute-start.1 = (bf16[2,256,512]{2,1,0:T(8,128)(2,1)S(1)}, bf16[2,256,512]{2,1,0:T(8,128)(2,1)}, u32[]{:S(2)}, u32[]{:S(2)}) collective-permute-start(bf16[2,256,512]{2,1,0:T(8,128)(2,1)S(1)} %add.412), channel_id=1, source_target_pairs={{0,1},{1,2},{2,3},{3,0},{4,5},{5,6},{6,7},{7,4},{8,9},{9,10},{10,1... | collective-permute-start | bytes 1572872 | tf_op jit(solution)/shard_map/reduce_down/ppermute | solution.py:57
  48.0 12.5 %collective-permute-start.6 = (bf16[256,512]{1,0:T(8,128)(2,1)}, bf16[256,512]{1,0:T(8,128)(2,1)S(1)}, u32[]{:S(2)}, u32[]{:S(2)}) collective-permute-start(bf16[256,512]{1,0:T(8,128)(2,1)} %get-tuple-element.84), channel_id=1, source_target_pairs={{0,4},{1,5},{2,6},{3,7},{4,8},{5,9},{6,10},{7,11},{8,12},{9,13},{1... | collective-permute-start | bytes 786440 | tf_op jit(solution)/shard_map/reduce_down/ppermute | solution.py:57
  49.9 10.6 %collective-permute-start.7 = (bf16[256,512]{1,0:T(8,128)(2,1)S(1)}, bf16[256,512]{1,0:T(8,128)(2,1)S(1)}, u32[]{:S(2)}, u32[]{:S(2)}) collective-permute-start(bf16[256,512]{1,0:T(8,128)(2,1)S(1)} %get-tuple-element.86), channel_id=1, source_target_pairs={{0,12},{1,13},{2,14},{3,15},{4,0},{5,1},{6,2},{7,3},{8,4},{9,5},{1... | collective-permute-start | bytes 786440 | tf_op jit(solution)/shard_map/reduce_down/ppermute | solution.py:57
  52.1 8.8 %collective-permute-start.8 = (bf16[256,512]{1,0:T(8,128)(2,1)S(1)}, bf16[256,512]{1,0:T(8,128)(2,1)S(1)}, u32[]{:S(2)}, u32[]{:S(2)}) collective-permute-start(bf16[256,512]{1,0:T(8,128)(2,1)S(1)} %get-tuple-element.85), channel_id=1, source_target_pairs={{0,8},{1,9},{2,10},{3,11},{4,12},{5,13},{6,14},{7,15},{8,0},{9,1},... | collective-permute-start | bytes 786440 | tf_op jit(solution)/shard_map/reduce_down/ppermute | solution.py:57
  62.3 10.3 %collective-permute-start.10 = (bf16[96,512]{1,0:T(8,128)(2,1)S(1)}, bf16[96,512]{1,0:T(8,128)(2,1)S(1)}, u32[]{:S(2)}, u32[]{:S(2)}) collective-permute-start(bf16[96,512]{1,0:T(8,128)(2,1)S(1)} %convolution_convert_fusion.2), channel_id=1, source_target_pairs={{0,64},{1,65},{2,66},{3,67},{4,68},{5,69},{6,70},{7,71},{8,72},{9,... | collective-permute-start | bytes 294920 | tf_op jit(solution)/shard_map/back/ppermute | solution.py:57
  65.4 7.2 %collective-permute-start.11 = (bf16[96,512]{1,0:T(8,128)(2,1)S(1)}, bf16[96,512]{1,0:T(8,128)(2,1)S(1)}, u32[]{:S(2)}, u32[]{:S(2)}) collective-permute-start(bf16[96,512]{1,0:T(8,128)(2,1)S(1)} %convolution_convert_fusion.2), channel_id=1, source_target_pairs={{0,32},{1,33},{2,34},{3,35},{4,36},{5,37},{6,38},{7,39},{8,40},{9,... | collective-permute-start | bytes 294920 | tf_op jit(solution)/shard_map/back/ppermute | solution.py:57
  69.5 17.2 %collective-permute-start.13 = (bf16[96,512]{1,0:T(8,128)(2,1)}, bf16[96,512]{1,0:T(8,128)(2,1)S(1)}, u32[]{:S(2)}, u32[]{:S(2)}) collective-permute-start(bf16[96,512]{1,0:T(8,128)(2,1)} %get-tuple-element.105), channel_id=1, source_target_pairs={{0,0},{1,4},{2,16},{3,17},{4,32},{5,36},{6,48},{7,49},{8,64},{9,68... | collective-permute-start | bytes 294920 | tf_op jit(solution)/shard_map/targets/ppermute | solution.py:57
  71.1 15.7 %collective-permute-start.14 = (bf16[96,512]{1,0:T(8,128)(2,1)}, bf16[96,512]{1,0:T(8,128)(2,1)S(1)}, u32[]{:S(2)}, u32[]{:S(2)}) collective-permute-start(bf16[96,512]{1,0:T(8,128)(2,1)} %get-tuple-element.104), channel_id=1, source_target_pairs={{0,4},{1,0},{2,17},{3,16},{4,36},{5,32},{6,49},{7,48},{8,68},{9,64... | collective-permute-start | bytes 294920 | tf_op jit(solution)/shard_map/targets/ppermute | solution.py:57
  72.7 8.0 %collective-permute-start.12 = (bf16[4,96,512]{2,1,0:T(8,128)(2,1)S(1)}, bf16[4,96,512]{2,1,0:T(8,128)(2,1)S(1)}, u32[]{:S(2)}, u32[]{:S(2)}) collective-permute-start(bf16[4,96,512]{2,1,0:T(8,128)(2,1)S(1)} %pad_maximum_fusion.5), channel_id=1, source_target_pairs={{0,16},{1,17},{2,18},{3,19},{4,20},{5,21},{6,22},{7,23},{8,24},{9,... | collective-permute-start | bytes 1179656 | tf_op jit(solution)/shard_map/back/ppermute | solution.py:57
  83.3 12.0 %collective-permute-start.15 = (bf16[2,96,1024]{2,1,0:T(8,128)(2,1)S(1)}, bf16[2,96,1024]{2,1,0:T(8,128)(2,1)S(1)}, u32[]{:S(2)}, u32[]{:S(2)}) collective-permute-start(bf16[2,96,1024]{2,1,0:T(8,128)(2,1)S(1)} %bitcast.134), channel_id=1, source_target_pairs={{0,1},{1,2},{2,3},{3,0},{4,5},{5,6},{6,7},{7,4},{8,9},{9,10},{10,1... | collective-permute-start | bytes 1179656 | tf_op jit(solution)/shard_map/reduce_draft/ppermute | solution.py:57
  84.6 11.2 %collective-permute-start.18 = (bf16[2,96,1024]{2,1,0:T(8,128)(2,1)S(1)}, bf16[2,96,1024]{2,1,0:T(8,128)(2,1)S(1)}, u32[]{:S(2)}, u32[]{:S(2)}) collective-permute-start(bf16[2,96,1024]{2,1,0:T(8,128)(2,1)S(1)} %bitcast.131), channel_id=1, source_target_pairs={{0,3},{1,0},{2,1},{3,2},{4,7},{5,4},{6,5},{7,6},{8,11},{9,8},{10,9... | collective-permute-start | bytes 1179656 | tf_op jit(solution)/shard_map/reduce_draft/ppermute | solution.py:57
  88.4 11.3 %collective-permute-start.17 = (bf16[2,96,1024]{2,1,0:T(8,128)(2,1)S(1)}, bf16[2,96,1024]{2,1,0:T(8,128)(2,1)S(1)}, u32[]{:S(2)}, u32[]{:S(2)}) collective-permute-start(bf16[2,96,1024]{2,1,0:T(8,128)(2,1)S(1)} %bitcast.133), channel_id=1, source_target_pairs={{0,3},{1,0},{2,1},{3,2},{4,7},{5,4},{6,5},{7,6},{8,11},{9,8},{10,9... | collective-permute-start | bytes 1179656 | tf_op jit(solution)/shard_map/reduce_draft/ppermute | solution.py:57
  93.8 13.4 %collective-permute-start.20 = (bf16[2,96,1024]{2,1,0:T(8,128)(2,1)S(1)}, bf16[2,96,1024]{2,1,0:T(8,128)(2,1)S(1)}, u32[]{:S(2)}, u32[]{:S(2)}) collective-permute-start(bf16[2,96,1024]{2,1,0:T(8,128)(2,1)S(1)} %bitcast.132), channel_id=1, source_target_pairs={{0,1},{1,2},{2,3},{3,0},{4,5},{5,6},{6,7},{7,4},{8,9},{9,10},{10,1... | collective-permute-start | bytes 1179656 | tf_op jit(solution)/shard_map/reduce_draft/ppermute | solution.py:57
  95.4 11.6 %collective-permute-start.16 = (bf16[2,96,1024]{2,1,0:T(8,128)(2,1)S(1)}, bf16[2,96,1024]{2,1,0:T(8,128)(2,1)S(1)}, u32[]{:S(2)}, u32[]{:S(2)}) collective-permute-start(bf16[2,96,1024]{2,1,0:T(8,128)(2,1)S(1)} %add.467), channel_id=1, source_target_pairs={{0,1},{1,2},{2,3},{3,0},{4,5},{5,6},{6,7},{7,4},{8,9},{9,10},{10,1... | collective-permute-start | bytes 1179656 | tf_op jit(solution)/shard_map/reduce_draft/ppermute | solution.py:57
  96.0 11.2 %collective-permute-start.19 = (bf16[2,96,1024]{2,1,0:T(8,128)(2,1)S(1)}, bf16[2,96,1024]{2,1,0:T(8,128)(2,1)S(1)}, u32[]{:S(2)}, u32[]{:S(2)}) collective-permute-start(bf16[2,96,1024]{2,1,0:T(8,128)(2,1)S(1)} %add.472), channel_id=1, source_target_pairs={{0,3},{1,0},{2,1},{3,2},{4,7},{5,4},{6,5},{7,6},{8,11},{9,8},{10,9... | collective-permute-start | bytes 1179656 | tf_op jit(solution)/shard_map/reduce_draft/ppermute | solution.py:57
  107.6 8.6 %collective-permute-start.22 = (bf16[96,1024]{1,0:T(8,128)(2,1)S(1)}, bf16[96,1024]{1,0:T(8,128)(2,1)S(1)}, u32[]{:S(2)}, u32[]{:S(2)}) collective-permute-start(bf16[96,1024]{1,0:T(8,128)(2,1)S(1)} %get-tuple-element.93), channel_id=1, source_target_pairs={{0,12},{1,13},{2,14},{3,15},{4,0},{5,1},{6,2},{7,3},{8,4},{9,5},{1... | collective-permute-start | bytes 589832 | tf_op jit(solution)/shard_map/reduce_draft/ppermute | solution.py:57
  110.9 7.2 %collective-permute-start.23 = (bf16[96,1024]{1,0:T(8,128)(2,1)S(1)}, bf16[96,1024]{1,0:T(8,128)(2,1)S(1)}, u32[]{:S(2)}, u32[]{:S(2)}) collective-permute-start(bf16[96,1024]{1,0:T(8,128)(2,1)S(1)} %get-tuple-element.92), channel_id=1, source_target_pairs={{0,8},{1,9},{2,10},{3,11},{4,12},{5,13},{6,14},{7,15},{8,0},{9,1},... | collective-permute-start | bytes 589832 | tf_op jit(solution)/shard_map/reduce_draft/ppermute | solution.py:57
  125.6 12.4 %collective-permute-start.28 = (bf16[96,1024]{1,0:T(8,128)(2,1)S(1)}, bf16[96,1024]{1,0:T(8,128)(2,1)S(1)}, u32[]{:S(2)}, u32[]{:S(2)}) collective-permute-start(bf16[96,1024]{1,0:T(8,128)(2,1)S(1)} %fusion.57), channel_id=1, source_target_pairs={{0,12},{1,13},{2,14},{3,15},{4,0},{5,1},{6,2},{7,3},{8,4},{9,5},{1... | collective-permute-start | bytes 589832 | tf_op jit(solution)/shard_map/gather_slope/ppermute | solution.py:57
  132.7 7.4 %collective-permute-start.29 = (bf16[96,1024]{1,0:T(8,128)(2,1)S(1)}, bf16[96,1024]{1,0:T(8,128)(2,1)}, u32[]{:S(2)}, u32[]{:S(2)}) collective-permute-start(bf16[96,1024]{1,0:T(8,128)(2,1)S(1)} %fusion.57), channel_id=1, source_target_pairs={{0,8},{1,9},{2,10},{3,11},{4,12},{5,13},{6,14},{7,15},{8,0},{9,1},... | collective-permute-start | bytes 589832 | tf_op jit(solution)/shard_map/gather_slope/ppermute | solution.py:57
  133.3 8.8 %collective-permute-start.30 = (bf16[96,1024]{1,0:T(8,128)(2,1)S(1)}, bf16[96,1024]{1,0:T(8,128)(2,1)}, u32[]{:S(2)}, u32[]{:S(2)}) collective-permute-start(bf16[96,1024]{1,0:T(8,128)(2,1)S(1)} %fusion.57), channel_id=1, source_target_pairs={{0,4},{1,5},{2,6},{3,7},{4,8},{5,9},{6,10},{7,11},{8,12},{9,13},{1... | collective-permute-start | bytes 589832 | tf_op jit(solution)/shard_map/gather_slope/ppermute | solution.py:57
  144.2 11.2 %collective-permute-start.31 = (bf16[192,1024]{1,0:T(8,128)(2,1)}, bf16[192,1024]{1,0:T(8,128)(2,1)}, u32[]{:S(2)}, u32[]{:S(2)}) collective-permute-start(bf16[192,1024]{1,0:T(8,128)(2,1)} %pad_maximum_fusion.6.first_ref), channel_id=1, source_target_pairs={{0,1},{1,2},{2,3},{3,0},{4,5},{5,6},{6,7},{7,4},{8,9},{9,10},{10,1... | collective-permute-start | bytes 1179656 | tf_op jit(solution)/shard_map/gather_slope/ppermute | solution.py:57
  147.1 8.8 %collective-permute-start.34 = (bf16[192,1024]{1,0:T(8,128)(2,1)}, bf16[192,1024]{1,0:T(8,128)(2,1)S(1)}, u32[]{:S(2)}, u32[]{:S(2)}) collective-permute-start(bf16[192,1024]{1,0:T(8,128)(2,1)} %pad_maximum_fusion.7.second_ref), channel_id=1, source_target_pairs={{0,3},{1,0},{2,1},{3,2},{4,7},{5,4},{6,5},{7,6},{8,11},{9,8},{10,9... | collective-permute-start | bytes 1179656 | tf_op jit(solution)/shard_map/gather_slope/ppermute | solution.py:57
  150.3 9.2 %collective-permute-start.32 = (bf16[192,1024]{1,0:T(8,128)(2,1)}, bf16[192,1024]{1,0:T(8,128)(2,1)S(1)}, u32[]{:S(2)}, u32[]{:S(2)}) collective-permute-start(bf16[192,1024]{1,0:T(8,128)(2,1)} %get-tuple-element.66), channel_id=1, source_target_pairs={{0,1},{1,2},{2,3},{3,0},{4,5},{5,6},{6,7},{7,4},{8,9},{9,10},{10,1... | collective-permute-start | bytes 1179656 | tf_op jit(solution)/shard_map/gather_slope/ppermute | solution.py:57
  150.3 9.8 %collective-permute-start.33 = (bf16[192,1024]{1,0:T(8,128)(2,1)}, bf16[192,1024]{1,0:T(8,128)(2,1)S(1)}, u32[]{:S(2)}, u32[]{:S(2)}) collective-permute-start(bf16[192,1024]{1,0:T(8,128)(2,1)} %get-tuple-element.67), channel_id=1, source_target_pairs={{0,3},{1,0},{2,1},{3,2},{4,7},{5,4},{6,5},{7,6},{8,11},{9,8},{10,9... | collective-permute-start | bytes 1179656 | tf_op jit(solution)/shard_map/gather_slope/ppermute | solution.py:57
  155.4 10.4 %collective-permute-start.35 = (bf16[192,1024]{1,0:T(8,128)(2,1)}, bf16[192,1024]{1,0:T(8,128)(2,1)S(1)}, u32[]{:S(2)}, u32[]{:S(2)}) collective-permute-start(bf16[192,1024]{1,0:T(8,128)(2,1)} %collective-permute-done.31), channel_id=1, source_target_pairs={{0,1},{1,2},{2,3},{3,0},{4,5},{5,6},{6,7},{7,4},{8,9},{9,10},{10,1... | collective-permute-start | bytes 1179656 | tf_op jit(solution)/shard_map/gather_slope/ppermute | solution.py:57
  155.9 9.9 %collective-permute-start.36 = (bf16[192,1024]{1,0:T(8,128)(2,1)S(1)}, bf16[192,1024]{1,0:T(8,128)(2,1)S(1)}, u32[]{:S(2)}, u32[]{:S(2)}) collective-permute-start(bf16[192,1024]{1,0:T(8,128)(2,1)S(1)} %collective-permute-done.34), channel_id=1, source_target_pairs={{0,3},{1,0},{2,1},{3,2},{4,7},{5,4},{6,5},{7,6},{8,11},{9,8},{10,9... | collective-permute-start | bytes 1179656 | tf_op jit(solution)/shard_map/gather_slope/ppermute | solution.py:57
  (32 other events, 153.6 us)
Sparse Core Ops, SparseCore 0:
  15.3 33.5 all-gather.1
